TPU v7x, 1024 devices: a whole 8x8x8 slice. The times are simulated.
1024 devices in a mesh: dp: 8 (over x_lo, core), expert: 8 (over z), etensor: 16 (over y, x_hi).
Axes of the slice: x: 8 (x_hi: 2, x_lo: 4; x = x_hi * 4 + x_lo), y: 8, z: 8, core: 2. Of those that a mesh axis runs over, the one named last changes fastest.
Arguments:
- tokens: bfloat16 [4096, 3072], P(('dp', 'expert', 'etensor')), may hold values from -6 to 6
- routes: int32 [4096, 2], P(('dp', 'expert', 'etensor')), may hold values from 0 to 7, as said below
- up_weight: bfloat16 [8, 3072, 16384], P('expert', 'dp', 'etensor'), may hold values from -0.046875 to 0.046875
- hidden_grad: bfloat16 [8, 1024, 16384], P('expert', 'dp', 'etensor'), may hold values from -6 to 6
- gate_pre: bfloat16 [8, 1024, 16384], P('expert', 'dp', 'etensor'), may hold values from -8 to 8
Outputs:
- grad_tokens: bfloat16 [4096, 3072], P(('dp', 'expert', 'etensor'))
- grad_up_weight: bfloat16 [8, 3072, 16384], P('expert', 'dp', 'etensor')
Inputs may be any that keep to these rules, and one draw needn't show every extreme that they name: `routes`: among the 8 picks of one device every expert is named exactly 1 times, and a token names 2 different experts.
All inputs are finite; a program needn't handle non-finite values.
Results may differ from a plain program's by a relative error of at most 0.0059.
Values may be sent and summed in bfloat16 or wider, within the bound.
No kernel may reach another device: no remote copies, remote signals or barrier semaphores. Data moves between devices by JAX's collectives and lax.ppermute only.
A program may use at most 32 MiB of HBM per device.

v0:
```python
import jax
import jax.numpy as jnp
from jax import lax
from jax.sharding import PartitionSpec as P


def derive(grad_rows, gate_rows):
    gate_wide = gate_rows.astype(jnp.float32)
    sigma = jax.nn.sigmoid(gate_wide)
    return (grad_rows.astype(jnp.float32) * gate_wide * sigma).astype(jnp.bfloat16)


def on_device(tokens, routes, up_weight, hidden_grad, gate_pre):
    data_count = lax.axis_size("dp")
    expert_count = lax.axis_size("expert")
    tensor_count = lax.axis_size("etensor")
    token_count, width = tokens.shape
    top_count = routes.shape[1]
    per_device = token_count * top_count
    slot_count = per_device // expert_count
    shard_width = up_weight.shape[1]
    chosen = routes.reshape(per_device)
    expert_ids = jnp.arange(expert_count, dtype=jnp.int32)
    onehot = (chosen[:, None] == expert_ids[None, :]).astype(jnp.int32)
    ordinal = jnp.sum(jnp.cumsum(onehot, axis=0) * onehot, axis=1) - 1
    slot_ids = chosen * slot_count + ordinal
    selector = (
        jnp.arange(expert_count * slot_count, dtype=jnp.int32)[:, None] == slot_ids[None, :]
    ).astype(jnp.float32)
    owner = (
        jnp.arange(per_device, dtype=jnp.int32)[None, :] // top_count
        == jnp.arange(token_count, dtype=jnp.int32)[:, None]
    ).astype(jnp.float32)
    combine = jnp.dot(owner, selector.T).astype(jnp.bfloat16)
    split_tokens = tokens.reshape(token_count, data_count, shard_width)
    outgoing = jnp.einsum(
        "tr,tqc->qrc", combine, split_tokens, preferred_element_type=jnp.float32
    ).astype(jnp.bfloat16)
    outgoing = outgoing.reshape(data_count, expert_count, slot_count, shard_width)
    arrived = lax.all_to_all(
        lax.all_to_all(outgoing, "dp", split_axis=0, concat_axis=0, tiled=True),
        "expert",
        split_axis=1,
        concat_axis=1,
        tiled=True,
    )
    gathered = lax.all_gather(arrived[:, :, None], "etensor", axis=2, tiled=True)
    layer_rows = gathered.reshape(-1, shard_width)
    weight_up = up_weight[0]
    grad_up = derive(
        lax.all_gather(hidden_grad[0], "dp", axis=0, tiled=True),
        lax.all_gather(gate_pre[0], "dp", axis=0, tiled=True),
    )
    contract_rows = (((0,), (0,)), ((), ()))
    sum_up = lax.dot_general(layer_rows, grad_up, contract_rows, preferred_element_type=jnp.float32)
    contract_hidden = (((1,), (1,)), ((), ()))
    block = lax.dot_general(grad_up, weight_up, contract_hidden, preferred_element_type=jnp.float32)
    partial_value = block
    totals = (sum_up, partial_value)
    sum_up, partial_value = totals
    partial_value = partial_value.reshape(
        data_count, expert_count, tensor_count, slot_count, shard_width
    )
    summed = lax.psum_scatter(partial_value, "etensor", scatter_dimension=2, tiled=True)
    row_grad = summed.reshape(data_count, expert_count, slot_count, shard_width).astype(
        jnp.bfloat16
    )
    returned = lax.all_to_all(
        lax.all_to_all(row_grad, "dp", split_axis=0, concat_axis=0, tiled=True),
        "expert",
        split_axis=1,
        concat_axis=1,
        tiled=True,
    )
    backward_rows = returned.reshape(data_count, expert_count * slot_count, shard_width)
    grad_tokens = jnp.einsum(
        "tr,qrc->tqc", combine, backward_rows, preferred_element_type=jnp.float32
    )
    grad_tokens = grad_tokens.astype(jnp.bfloat16).reshape(token_count, width)
    return (grad_tokens, sum_up.astype(jnp.bfloat16)[None])


def solution(mesh):
    in_specs = (
        P(("dp", "expert", "etensor"), None),
        P(("dp", "expert", "etensor"), None),
        P("expert", "dp", "etensor"),
        P("expert", "dp", "etensor"),
        P("expert", "dp", "etensor"),
    )
    out_specs = (P(("dp", "expert", "etensor"), None), P("expert", "dp", "etensor"))
    return jax.shard_map(
        on_device, mesh=mesh, in_specs=in_specs, out_specs=out_specs, check_vma=False
    )
```

profile of v0, /device:TPU:26, one launch (start us, length us, event | category | flops | bytes accessed | tf_op | source)
XLA Modules:
  0.0 447.4 jit_solution(6759793134621316822)
XLA Ops:
  7.2 0.7 all-gather.6.cloned.1.call-update
  8.0 0.7 all-gather.8.cloned.1.call-update
  8.7 53.5 %all-gather.6.cloned.1.call-done = bf16[1,1024,1024]{2,1,0:T(8,128)(2,1)} async-done(((bf16[1,128,1024]{2,1,0:T(8,128)(2,1)}), bf16[1,1024,1024]{2,1,0:T(8,128)(2,1)}) %all-gather.6.cloned.1.call-update) | async-done | bytes 2097168 | tf_op jit(solution)/shard_map/all_gather | solution.py:51
  62.2 47.3 %all-gather.8.cloned.1.call-done = bf16[1,1024,1024]{2,1,0:T(8,128)(2,1)} async-done(((bf16[1,128,1024]{2,1,0:T(8,128)(2,1)}), bf16[1,1024,1024]{2,1,0:T(8,128)(2,1)}) %all-gather.8.cloned.1.call-update) | async-done | bytes 2097168 | tf_op jit(solution)/shard_map/all_gather | solution.py:52
  109.5 3.4 fusion.4
  112.9 1.3 convolution_bitcast_fusion
  114.2 1.6 copy.24
  115.9 0.1 copy.23
  116.0 0.1 reshape.90
  116.2 0.2 select_reduce_fusion
  116.4 0.1 fusion.14
  116.5 0.2 fusion.13
  116.7 11.3 %all_to_all.20 = bf16[8,8,1,384]{3,1,2,0:T(8,128)(2,1)S(1)} all-to-all(bf16[8,8,1,384]{3,1,2,0:T(8,128)(2,1)S(1)} %fusion.13), channel_id=1, replica_groups=mesh['dp'=8,'expert'=8,'etensor'=16] {'dp'}, dimensions={0} | all-to-all | bytes 98304 | tf_op jit(solution)/shard_map/all_to_all | solution.py:41
  128.0 16.1 %all_to_all.21 = bf16[8,8,1,384]{3,0,2,1:T(8,128)(2,1)S(1)} all-to-all(bf16[8,8,1,384]{3,0,2,1:T(8,128)(2,1)S(1)} %copy.31), channel_id=1, replica_groups=mesh['dp'=8,'expert'=8,'etensor'=16] {'expert'}, dimensions={1} | all-to-all | bytes 98304 | tf_op jit(solution)/shard_map/all_to_all | solution.py:40
  144.1 200.6 %reduce-scatter.2.cloned.1.call-done = f32[8,8,1,1,384]{4,1,3,0,2:T(8,128)} async-done(((f32[8,8,16,1,384]{4,1,3,0,2:T(8,128)}), f32[8,8,1,1,384]{4,1,3,0,2:T(8,128)}) %reduce-scatter.2.cloned.1.call-update) | async-done | bytes 98320 | tf_op jit(solution)/shard_map/reduce_scatter | solution.py:64
  344.7 1.5 fusion.16
  346.3 4.8 %all-to-all-start = ((bf16[8,8,1,384]{3,1,2,0:T(8,128)(2,1)}), bf16[8,8,1,384]{3,1,2,0:T(8,128)(2,1)S(1)}, u32[]{:S(2)}, u32[]{:S(2)}) async-start(bf16[8,8,1,384]{3,1,2,0:T(8,128)(2,1)} %fusion.16), calls=%async_computation.1 | async-start | bytes 98304 | tf_op jit(solution)/shard_map/all_to_all | solution.py:69
  351.1 69.6 %all-gather.2 = bf16[8,8,16,384]{3,1,0,2:T(8,128)(2,1)S(1)} all-gather(bf16[8,8,1,384]{3,1,0,2:T(8,128)(2,1)S(1)} %copy.32), channel_id=4, replica_groups=mesh['dp'=8,'expert'=8,'etensor'=16] {'etensor'}, dimensions={2}, use_global_device_ids=true | all-gather | bytes 835584 | tf_op jit(solution)/shard_map/all_gather | solution.py:47
  420.6 1.3 copy.33
  422.0 0.6 copy.27
  422.6 9.3 %all-to-all-start.1 = ((bf16[8,8,1,384]{3,0,2,1:T(8,128)(2,1)}), bf16[8,8,1,384]{3,0,2,1:T(8,128)(2,1)S(1)}, u32[]{:S(2)}, u32[]{:S(2)}) async-start(bf16[8,8,1,384]{3,0,2,1:T(8,128)(2,1)} %copy.27), calls=%async_computation.2 | async-start | bytes 98304 | tf_op jit(solution)/shard_map/all_to_all | solution.py:68
  431.9 3.0 fusion.10
  434.9 5.2 %all-to-all-done.1 = bf16[8,8,1,384]{3,0,2,1:T(8,128)(2,1)S(1)} async-done(((bf16[8,8,1,384]{3,0,2,1:T(8,128)(2,1)}), bf16[8,8,1,384]{3,0,2,1:T(8,128)(2,1)S(1)}, u32[]{:S(2)}, u32[]{:S(2)}) %all-to-all-start.1) | async-done | bytes 49184 | tf_op jit(solution)/shard_map/all_to_all | solution.py:68
  440.1 0.7 convolution_convert_fusion.1
  (16 shorter events, 0.3 us)
Async XLA Ops:
  7.2 105.8 %copy-start = (bf16[1,384,1024]{2,1,0:T(8,128)(2,1)S(1)}, bf16[1,384,1024]{2,1,0:T(8,128)(2,1)}, u32[]{:S(2)}) copy-start(bf16[1,384,1024]{2,1,0:T(8,128)(2,1)} %param.7) | copy-start | bytes 2359300
  7.2 55.0 %all-gather.6.cloned.1.call-start = ((), (), s32[]{:S(2)}) async-start(), calls=%async_computation.6 | async-start | bytes 2359296 | tf_op jit(solution)/shard_map/all_gather | solution.py:51
  7.9 101.6 %all-gather.8.cloned.1.call-start = ((), (), s32[]{:S(2)}) async-start(), calls=%async_computation.7 | async-start | bytes 2359296 | tf_op jit(solution)/shard_map/all_gather | solution.py:52
  8.7 336.1 %reduce-scatter.2.cloned.1.call-start = ((), (), s32[]{:S(2)}) async-start(), calls=%async_computation.5 | async-start | bytes 1671168 | tf_op jit(solution)/shard_map/reduce_scatter | solution.py:64
  114.2 1.7 copy-start.2
  114.2 2.3 copy-start.1
  346.3 75.7 %all-to-all-start = ((bf16[8,8,1,384]{3,1,2,0:T(8,128)(2,1)}), bf16[8,8,1,384]{3,1,2,0:T(8,128)(2,1)S(1)}, u32[]{:S(2)}, u32[]{:S(2)}) async-start(bf16[8,8,1,384]{3,1,2,0:T(8,128)(2,1)} %fusion.16), calls=%async_computation.1 | async-start | bytes 98304 | tf_op jit(solution)/shard_map/all_to_all | solution.py:69
  422.6 17.5 %all-to-all-start.1 = ((bf16[8,8,1,384]{3,0,2,1:T(8,128)(2,1)}), bf16[8,8,1,384]{3,0,2,1:T(8,128)(2,1)S(1)}, u32[]{:S(2)}, u32[]{:S(2)}) async-start(bf16[8,8,1,384]{3,0,2,1:T(8,128)(2,1)} %copy.27), calls=%async_computation.2 | async-start | bytes 98304 | tf_op jit(solution)/shard_map/all_to_all | solution.py:68
Sparse Core Ops, SparseCore 0:
  10.7 51.4 all-gather.5
  64.8 44.6 all-gather.7
  116.0 228.6 reduce-scatter.1
where the time goes:
time: 448 us; the launch traced here: 447 us
  waiting for transfers between devices  308 us (69%)
  blocking collectives  97 us (22%)
  starting transfers between devices  14.2 us (3%)
  between operations  13.8 us (3%)
  matrix products  5.34 us (1%)
  other arithmetic  5.25 us (1%)
    reduce_scatter x1, waiting for transfers between devices, on_device(): lax.psum_scatter(partial_value, 'etensor', scatter_dimension=2, tiled=True)  201 us
    all_gather x1, blocking collectives, on_device(): lax.all_gather(arrived[:, :, None], 'etensor', axis=2, tiled=True)  69.6 us
    all_gather x1, waiting for transfers between devices, on_device(): lax.all_gather(hidden_grad[0], 'dp', axis=0, tiled=True)  53.5 us
    all_gather x1, waiting for transfers between devices, on_device(): lax.all_gather(gate_pre[0], 'dp', axis=0, tiled=True)  47.3 us
    all_to_all x1, blocking collectives, on_device(): lax.all_to_all(lax.all_to_all(outgoing, 'dp', split_axis=0, concat_axis=0...  16.1 us
    all_to_all x1, blocking collectives, on_device(): lax.all_to_all(outgoing, 'dp', split_axis=0, concat_axis=0, tiled=True)  11.3 us
    all_to_all x1, starting transfers between devices, on_device(): lax.all_to_all(lax.all_to_all(row_grad, 'dp', split_axis=0, concat_axis=0...  9.28 us
  transfers between devices with their start and end apart: 5, of which 4 were waited for; matrix products, arithmetic and copies ran while one was open for 1% of the time, Pallas kernels for 0%

commit v1 on v0

v1 whole, which is shorter than its diff:
```python
import jax
import jax.numpy as jnp
from jax import lax
from jax.sharding import Mesh, PartitionSpec as P

CORE_SWAP = ((0, 1), (1, 0))


def derive(grad_rows, gate_rows):
    gate_wide = gate_rows.astype(jnp.float32)
    sigma = jax.nn.sigmoid(gate_wide)
    return (grad_rows.astype(jnp.float32) * gate_wide * sigma).astype(jnp.bfloat16)


def exchange(blocks, axes):
    return lax.all_to_all(blocks, axes, split_axis=0, concat_axis=0, tiled=True)


def on_device(tokens, routes, up_weight, hidden_grad, gate_pre):
    chips, cores, experts = lax.axis_size("xl"), lax.axis_size("core"), lax.axis_size("ex")
    ys, halves = lax.axis_size("y"), lax.axis_size("h")
    owners = chips * cores
    token_count, width = tokens.shape
    _, shard, hidden = up_weight.shape
    rows = hidden_grad.shape[1]
    inner = halves * experts
    first = lax.axis_index("core") == 0

    grad_up = derive(hidden_grad[0], gate_pre[0])
    grad_up = grad_up.reshape(experts, ys, halves, hidden).transpose(1, 2, 0, 3)
    grad_up = grad_up.reshape(rows, hidden)
    chip_rows = exchange(jnp.broadcast_to(grad_up[None], (chips, rows, hidden)), "xl")
    weight = up_weight[0]
    other_weight = lax.ppermute(weight, "core", CORE_SWAP)
    weights = jnp.concatenate(
        [jnp.where(first, weight, other_weight), jnp.where(first, other_weight, weight)], axis=0
    )

    picks = jnp.any(
        routes[:, :, None] == jnp.arange(experts, dtype=jnp.int32)[None, None, :], axis=1
    ).astype(jnp.bfloat16)
    outgoing = jnp.einsum(
        "te,tqc->qec",
        picks,
        tokens.reshape(token_count, owners, shard),
        preferred_element_type=jnp.float32,
    ).astype(jnp.bfloat16)
    outgoing = jnp.broadcast_to(outgoing[:, None], (owners, halves, experts, shard))
    arrived = exchange(
        outgoing.reshape(owners * halves, experts, shard), ("xl", "core", "h")
    )
    arrived = exchange(arrived.transpose(1, 0, 2), "ex")
    arrived = arrived.reshape(experts, owners, halves, shard).transpose(1, 2, 0, 3)
    arrived = arrived.reshape(owners * inner, shard)

    partial = lax.dot_general(
        chip_rows, weights, (((2,), (1,)), ((), ())), preferred_element_type=jnp.float32
    ).astype(jnp.bfloat16)
    partial = partial.reshape(chips, ys, inner, cores * shard).transpose(1, 0, 2, 3)
    summed = jnp.sum(exchange(partial, "y").astype(jnp.float32), axis=0).astype(jnp.bfloat16)
    summed = exchange(summed.reshape(chips * halves, experts, cores * shard), ("xl", "h"))
    summed = summed.reshape(chips, halves, experts, cores * shard).astype(jnp.float32)
    row_grad = jnp.sum(summed, axis=1).astype(jnp.bfloat16)
    returned = exchange(row_grad.transpose(1, 0, 2), "ex")
    grad_tokens = jnp.einsum(
        "te,eqc->tqc", picks, returned, preferred_element_type=jnp.float32
    ).astype(jnp.bfloat16)

    layer_rows = exchange(jnp.broadcast_to(arrived[None], (ys,) + arrived.shape), "y")
    layer_rows = layer_rows.reshape(ys, chips, cores, inner, shard).transpose(1, 2, 0, 3, 4)
    own_rows = jnp.where(first, layer_rows[:, 0], layer_rows[:, 1]).reshape(chips, rows, shard)
    other_rows = jnp.where(first, layer_rows[:, 1], layer_rows[:, 0]).reshape(chips, rows, shard)
    other_chip_rows = lax.ppermute(chip_rows, "core", CORE_SWAP)
    contract = (((0, 1), (0, 1)), ((), ()))
    weight_grad = lax.dot_general(
        own_rows, chip_rows, contract, preferred_element_type=jnp.float32
    ) + lax.dot_general(
        other_rows, other_chip_rows, contract, preferred_element_type=jnp.float32
    )
    return grad_tokens.reshape(token_count, width), weight_grad.astype(jnp.bfloat16)[None]


def solution(mesh):
    shape = (mesh.shape["dp"] // 2, 2, mesh.shape["expert"], mesh.shape["etensor"] // 2, 2)
    fine = Mesh(mesh.devices.reshape(shape), ("xl", "core", "ex", "y", "h"))
    tokens_spec = P(("xl", "core", "ex", "y", "h"), None)
    expert_spec = P("ex", ("xl", "core"), ("y", "h"))
    return jax.shard_map(
        on_device,
        mesh=fine,
        in_specs=(tokens_spec, tokens_spec, expert_spec, expert_spec, expert_spec),
        out_specs=(tokens_spec, expert_spec),
        check_vma=False,
    )
```

time: 448 us -> 155 us (0.35)
  the two profiles are of different devices: /device:TPU:26 before, /device:TPU:1 now
where the time goes in v1:
time: 155 us; the launch traced here: 153 us
  waiting for transfers between devices  78 us (50%)
  starting transfers between devices  36.6 us (24%)
  blocking collectives  24.4 us (16%)
  matrix products  5.28 us (3%)
  local copies, waits for them, and re-layouts  4.71 us (3%)
  other arithmetic  2.91 us (2%)
    all_to_all x6, waiting for transfers between devices, exchange(): return lax.all_to_all(blocks, axes, split_axis=0, concat_axis=0, tiled=True)  76.2 us
    all_to_all x6, starting transfers between devices, exchange(): return lax.all_to_all(blocks, axes, split_axis=0, concat_axis=0, tiled=True)  29.4 us
    all_to_all x1, blocking collectives, exchange(): return lax.all_to_all(blocks, axes, split_axis=0, concat_axis=0, tiled=True)  24.4 us
    ppermute x1, starting transfers between devices, on_device(): other_weight = lax.ppermute(weight, 'core', CORE_SWAP)  3.65 us
    ppermute x1, starting transfers between devices, on_device(): other_chip_rows = lax.ppermute(chip_rows, 'core', CORE_SWAP)  3.54 us
  transfers between devices with their start and end apart: 8, of which 7 were waited for; matrix products, arithmetic and copies ran while one was open for 6% of the time, Pallas kernels for 0%

profile of v1, /device:TPU:1, one launch (start us, length us, event | category | flops | bytes accessed | tf_op | source)
XLA Modules:
  0.0 152.8 jit_solution(10091472528225795868)
XLA Ops:
  0.6 0.8 fusion.13
  1.6 24.4 %all_to_all.35 = bf16[16,8,384]{2,1,0:T(8,128)(2,1)S(1)} all-to-all(bf16[16,8,384]{2,1,0:T(8,128)(2,1)S(1)} %bitcast.63), channel_id=1, replica_groups=mesh['xl'=4,'core'=2,'ex'=8,'y'=8,'h'=2] {'xl','core','h'}, dimensions={0} | all-to-all | bytes 196608 | tf_op jit(solution)/shard_map/all_to_all | solution.py:16
  26.7 8.3 %all-to-all-start.5 = ((bf16[8,16,384]{2,1,0:T(8,128)(2,1)}), bf16[8,16,384]{2,1,0:T(8,128)(2,1)S(1)}, u32[]{:S(2)}, u32[]{:S(2)}) async-start(bf16[8,16,384]{2,1,0:T(8,128)(2,1)} %copy.44), calls=%async_computation.5 | async-start | bytes 196608 | tf_op jit(solution)/shard_map/all_to_all | solution.py:16
  35.1 1.2 fusion.8
  36.5 6.2 %all-to-all-done.5 = bf16[8,16,384]{2,1,0:T(8,128)(2,1)S(1)} async-done(((bf16[8,16,384]{2,1,0:T(8,128)(2,1)}), bf16[8,16,384]{2,1,0:T(8,128)(2,1)S(1)}, u32[]{:S(2)}, u32[]{:S(2)}) %all-to-all-start.5) | async-done | bytes 98336 | tf_op jit(solution)/shard_map/all_to_all | solution.py:16
  42.7 1.1 broadcast_in_dim.26
  43.8 3.5 %all-to-all-start = ((bf16[4,128,1024]{2,1,0:T(8,128)(2,1)}), bf16[4,128,1024]{2,1,0:T(8,128)(2,1)S(1)}, u32[]{:S(2)}, u32[]{:S(2)}) async-start(bf16[4,128,1024]{2,1,0:T(8,128)(2,1)} %broadcast_in_dim.26), calls=%async_computation | async-start | bytes 2097152 | tf_op jit(solution)/shard_map/all_to_all | solution.py:16
  47.4 25.1 %all-to-all-done = bf16[4,128,1024]{2,1,0:T(8,128)(2,1)S(1)} async-done(((bf16[4,128,1024]{2,1,0:T(8,128)(2,1)}), bf16[4,128,1024]{2,1,0:T(8,128)(2,1)S(1)}, u32[]{:S(2)}, u32[]{:S(2)}) %all-to-all-start) | async-done | bytes 1048608 | tf_op jit(solution)/shard_map/all_to_all | solution.py:16
  72.5 1.0 broadcast_in_dim.29
  73.5 7.3 %all-to-all-start.6 = ((bf16[8,128,384]{2,1,0:T(8,128)(2,1)}), bf16[8,128,384]{2,1,0:T(8,128)(2,1)S(1)}, u32[]{:S(2)}, u32[]{:S(2)}) async-start(bf16[8,128,384]{2,1,0:T(8,128)(2,1)} %broadcast_in_dim.29), calls=%async_computation.6 | async-start | bytes 1572864 | tf_op jit(solution)/shard_map/all_to_all | solution.py:16
  80.8 3.7 %collective-permute-start = (bf16[384,1024]{1,0:T(8,128)(2,1)S(1)}, bf16[384,1024]{1,0:T(8,128)(2,1)S(1)}, u32[]{:S(2)}, u32[]{:S(2)}) collective-permute-start(bf16[384,1024]{1,0:T(8,128)(2,1)S(1)} %bitcast.61), channel_id=1, source_target_pairs={{0,128},{128,0},{1,129},{129,1},{2,130},{130,2},{3,131},{131,3},{4... | collective-permute-start | bytes 2359304 | tf_op jit(solution)/shard_map/ppermute | solution.py:34
  84.4 1.9 %collective-permute-done = bf16[384,1024]{1,0:T(8,128)(2,1)S(1)} collective-permute-done((bf16[384,1024]{1,0:T(8,128)(2,1)S(1)}, bf16[384,1024]{1,0:T(8,128)(2,1)S(1)}, u32[]{:S(2)}, u32[]{:S(2)}) %collective-permute-start) | collective-permute-done | bytes 786464 | tf_op jit(solution)/shard_map/ppermute | solution.py:34
  86.4 1.0 fusion.4
  87.5 1.0 copy.55
  88.4 14.8 %all-to-all-done.6 = bf16[8,128,384]{2,1,0:T(8,128)(2,1)S(1)} async-done(((bf16[8,128,384]{2,1,0:T(8,128)(2,1)}), bf16[8,128,384]{2,1,0:T(8,128)(2,1)S(1)}, u32[]{:S(2)}, u32[]{:S(2)}) %all-to-all-start.6) | async-done | bytes 786464 | tf_op jit(solution)/shard_map/all_to_all | solution.py:16
  103.2 3.5 %all-to-all-start.1 = ((bf16[8,4,16,768]{3,2,1,0:T(8,128)(2,1)}), bf16[8,4,16,768]{3,2,1,0:T(8,128)(2,1)S(1)}, u32[]{:S(2)}, u32[]{:S(2)}) async-start(bf16[8,4,16,768]{3,2,1,0:T(8,128)(2,1)} %bitcast.53), calls=%async_computation.1 | async-start | bytes 1572864 | tf_op jit(solution)/shard_map/all_to_all | solution.py:16
  106.8 3.5 %collective-permute-start.1 = (bf16[4,128,1024]{2,1,0:T(8,128)(2,1)S(1)}, bf16[4,128,1024]{2,1,0:T(8,128)(2,1)}, u32[]{:S(2)}, u32[]{:S(2)}) collective-permute-start(bf16[4,128,1024]{2,1,0:T(8,128)(2,1)S(1)} %all-to-all-done), channel_id=1, source_target_pairs={{0,128},{128,0},{1,129},{129,1},{2,130},{130,2},{3,131},{131,3},{4... | collective-permute-start | bytes 3145736 | tf_op jit(solution)/shard_map/ppermute | solution.py:73
  110.5 19.7 %all-to-all-done.1 = bf16[8,4,16,768]{3,2,1,0:T(8,128)(2,1)S(1)} async-done(((bf16[8,4,16,768]{3,2,1,0:T(8,128)(2,1)}), bf16[8,4,16,768]{3,2,1,0:T(8,128)(2,1)S(1)}, u32[]{:S(2)}, u32[]{:S(2)}) %all-to-all-start.1) | async-done | bytes 786464 | tf_op jit(solution)/shard_map/all_to_all | solution.py:16
  130.2 0.8 reduce_sum.24
  131.0 3.4 %all-to-all-start.2 = ((bf16[8,8,768]{2,1,0:T(8,128)(2,1)}), bf16[8,8,768]{2,1,0:T(8,128)(2,1)S(1)}, u32[]{:S(2)}, u32[]{:S(2)}) async-start(bf16[8,8,768]{2,1,0:T(8,128)(2,1)} %bitcast.7), calls=%async_computation.2 | async-start | bytes 196608 | tf_op jit(solution)/shard_map/all_to_all | solution.py:16
  135.0 6.0 %all-to-all-done.2 = bf16[8,8,768]{2,1,0:T(8,128)(2,1)S(1)} async-done(((bf16[8,8,768]{2,1,0:T(8,128)(2,1)}), bf16[8,8,768]{2,1,0:T(8,128)(2,1)S(1)}, u32[]{:S(2)}, u32[]{:S(2)}) %all-to-all-start.2) | async-done | bytes 98336 | tf_op jit(solution)/shard_map/all_to_all | solution.py:16
  141.6 3.3 %all-to-all-start.3 = ((bf16[8,4,768]{2,1,0:T(4,128)(2,1)}), bf16[8,4,768]{2,1,0:T(4,128)(2,1)S(1)}, u32[]{:S(2)}, u32[]{:S(2)}) async-start(bf16[8,4,768]{2,1,0:T(4,128)(2,1)} %copy.41), calls=%async_computation.3 | async-start | bytes 98304 | tf_op jit(solution)/shard_map/all_to_all | solution.py:16
  145.0 2.7 %fusion.5 = bf16[1,384,1024]{2,1,0:T(8,128)(2,1)} fusion(bf16[4,128,384]{2,1,0:T(8,128)(2,1)S(1)} %bitcast.56, bf16[4,128,1024]{2,1,0:T(8,128)(2,1)} %collective-permute-done.1, f32[384,1024,1]{1,0,2:T(8,128)S(1)} %fusion.17), kind=kOutput, calls=%fused_computation.7 | convolution fusion | flops 403439616 | bytes 3801088 | tf_op jit(solution)/shard_map/dot_general | solution.py:77
  147.7 4.3 %all-to-all-done.3 = bf16[8,4,768]{2,1,0:T(4,128)(2,1)S(1)} async-done(((bf16[8,4,768]{2,1,0:T(4,128)(2,1)}), bf16[8,4,768]{2,1,0:T(4,128)(2,1)S(1)}, u32[]{:S(2)}, u32[]{:S(2)}) %all-to-all-start.3) | async-done | bytes 49184 | tf_op jit(solution)/shard_map/all_to_all | solution.py:16
  (20 shorter events, 3.4 us)
Async XLA Ops:
  0.6 0.8 copy-start
  26.7 16.0 %all-to-all-start.5 = ((bf16[8,16,384]{2,1,0:T(8,128)(2,1)}), bf16[8,16,384]{2,1,0:T(8,128)(2,1)S(1)}, u32[]{:S(2)}, u32[]{:S(2)}) async-start(bf16[8,16,384]{2,1,0:T(8,128)(2,1)} %copy.44), calls=%async_computation.5 | async-start | bytes 196608 | tf_op jit(solution)/shard_map/all_to_all | solution.py:16
  43.8 28.7 %all-to-all-start = ((bf16[4,128,1024]{2,1,0:T(8,128)(2,1)}), bf16[4,128,1024]{2,1,0:T(8,128)(2,1)S(1)}, u32[]{:S(2)}, u32[]{:S(2)}) async-start(bf16[4,128,1024]{2,1,0:T(8,128)(2,1)} %broadcast_in_dim.26), calls=%async_computation | async-start | bytes 2097152 | tf_op jit(solution)/shard_map/all_to_all | solution.py:16
  47.4 33.4 %copy-start.1 = (bf16[1,384,1024]{2,1,0:T(8,128)(2,1)S(1)}, bf16[1,384,1024]{2,1,0:T(8,128)(2,1)}, u32[]{:S(2)}) copy-start(bf16[1,384,1024]{2,1,0:T(8,128)(2,1)} %param.7) | copy-start | bytes 2359300
  73.5 29.7 %all-to-all-start.6 = ((bf16[8,128,384]{2,1,0:T(8,128)(2,1)}), bf16[8,128,384]{2,1,0:T(8,128)(2,1)S(1)}, u32[]{:S(2)}, u32[]{:S(2)}) async-start(bf16[8,128,384]{2,1,0:T(8,128)(2,1)} %broadcast_in_dim.29), calls=%async_computation.6 | async-start | bytes 1572864 | tf_op jit(solution)/shard_map/all_to_all | solution.py:16
  80.8 5.6 %collective-permute-start = (bf16[384,1024]{1,0:T(8,128)(2,1)S(1)}, bf16[384,1024]{1,0:T(8,128)(2,1)S(1)}, u32[]{:S(2)}, u32[]{:S(2)}) collective-permute-start(bf16[384,1024]{1,0:T(8,128)(2,1)S(1)} %bitcast.61), channel_id=1, source_target_pairs={{0,128},{128,0},{1,129},{129,1},{2,130},{130,2},{3,131},{131,3},{4... | collective-permute-start | bytes 2359304 | tf_op jit(solution)/shard_map/ppermute | solution.py:34
  103.2 27.0 %all-to-all-start.1 = ((bf16[8,4,16,768]{3,2,1,0:T(8,128)(2,1)}), bf16[8,4,16,768]{3,2,1,0:T(8,128)(2,1)S(1)}, u32[]{:S(2)}, u32[]{:S(2)}) async-start(bf16[8,4,16,768]{3,2,1,0:T(8,128)(2,1)} %bitcast.53), calls=%async_computation.1 | async-start | bytes 1572864 | tf_op jit(solution)/shard_map/all_to_all | solution.py:16
  106.8 38.2 %collective-permute-start.1 = (bf16[4,128,1024]{2,1,0:T(8,128)(2,1)S(1)}, bf16[4,128,1024]{2,1,0:T(8,128)(2,1)}, u32[]{:S(2)}, u32[]{:S(2)}) collective-permute-start(bf16[4,128,1024]{2,1,0:T(8,128)(2,1)S(1)} %all-to-all-done), channel_id=1, source_target_pairs={{0,128},{128,0},{1,129},{129,1},{2,130},{130,2},{3,131},{131,3},{4... | collective-permute-start | bytes 3145736 | tf_op jit(solution)/shard_map/ppermute | solution.py:73
  131.0 9.9 %all-to-all-start.2 = ((bf16[8,8,768]{2,1,0:T(8,128)(2,1)}), bf16[8,8,768]{2,1,0:T(8,128)(2,1)S(1)}, u32[]{:S(2)}, u32[]{:S(2)}) async-start(bf16[8,8,768]{2,1,0:T(8,128)(2,1)} %bitcast.7), calls=%async_computation.2 | async-start | bytes 196608 | tf_op jit(solution)/shard_map/all_to_all | solution.py:16
  141.6 10.4 %all-to-all-start.3 = ((bf16[8,4,768]{2,1,0:T(4,128)(2,1)}), bf16[8,4,768]{2,1,0:T(4,128)(2,1)S(1)}, u32[]{:S(2)}, u32[]{:S(2)}) async-start(bf16[8,4,768]{2,1,0:T(4,128)(2,1)} %copy.41), calls=%async_computation.3 | async-start | bytes 98304 | tf_op jit(solution)/shard_map/all_to_all | solution.py:16

commit v2 on v1

v2 whole, which is shorter than its diff:
```python
import jax
import jax.numpy as jnp
from jax import lax
from jax.experimental import pallas as pl
from jax.experimental.pallas import tpu as pltpu
from jax.sharding import Mesh, PartitionSpec as P

CORE_SWAP = ((0, 1), (1, 0))
VMEM_BYTES = 40 * 1024 * 1024


def derive(grad_rows, gate_rows):
    gate_wide = gate_rows.astype(jnp.float32)
    sigma = jax.nn.sigmoid(gate_wide)
    return (grad_rows.astype(jnp.float32) * gate_wide * sigma).astype(jnp.bfloat16)


def exchange(blocks, axes):
    return lax.all_to_all(blocks, axes, split_axis=0, concat_axis=0, tiled=True)


def flip(value, axis, bits):
    return lax.ppermute(value, axis, [(i, i ^ bits) for i in range(lax.axis_size(axis))])


def row_partials(chip_rows, weight, other_weight):
    chips = len(chip_rows)
    rows, hidden = chip_rows[0].shape
    shard = weight.shape[0]
    ys = lax.axis_size("y")
    inner = rows // ys

    def kernel(place, *refs):
        row_refs, (weight_ref, other_ref, out_ref, stack_ref, both) = refs[:chips], refs[chips:]
        chip, core = place[0], place[1]
        both[pl.ds(pl.multiple_of(core * shard, shard), shard)] = weight_ref[...]
        both[pl.ds(pl.multiple_of((1 - core) * shard, shard), shard)] = other_ref[...]
        for k in range(chips):
            owner = jnp.bitwise_xor(chip, k)
            block = row_refs[k][...]
            stack_ref[owner] = block
            part = lax.dot_general(
                block, both[...], (((1,), (1,)), ((), ())), preferred_element_type=jnp.float32
            ).astype(jnp.bfloat16)
            for y in range(ys):
                out_ref[y, owner] = part[y * inner : (y + 1) * inner]

    place = jnp.stack([lax.axis_index("xl"), lax.axis_index("core")]).astype(jnp.int32)
    return pl.pallas_call(
        kernel,
        out_shape=(
            jax.ShapeDtypeStruct((ys, chips, inner, 2 * shard), jnp.bfloat16),
            jax.ShapeDtypeStruct((chips, rows, hidden), jnp.bfloat16),
        ),
        in_specs=[pl.BlockSpec(memory_space=pltpu.SMEM)]
        + [pl.BlockSpec(memory_space=pltpu.VMEM)] * (chips + 2),
        out_specs=(pl.BlockSpec(memory_space=pltpu.VMEM),) * 2,
        scratch_shapes=[pltpu.VMEM((2 * shard, hidden), jnp.bfloat16)],
        compiler_params=pltpu.CompilerParams(vmem_limit_bytes=VMEM_BYTES),
        cost_estimate=pl.CostEstimate(
            flops=4 * chips * rows * hidden * shard, bytes_accessed=6 << 20, transcendentals=0
        ),
        name="row_partials",
    )(place, *chip_rows, weight, other_weight)


def weight_gradient(pieces, chip_rows, other_rows):
    chips, rows, hidden = chip_rows.shape
    ys = lax.axis_size("y")
    inner = rows // ys
    shard = pieces[0].shape[1]

    def kernel(place, *refs):
        piece_refs, (own_ref, other_ref, out_ref, layer) = refs[: len(pieces)], refs[len(pieces) :]
        core, here, beside = place[0], place[1], place[2]
        owners = (here, here ^ 4, here ^ 2, here ^ 6, here ^ 1, here ^ 5, beside, beside ^ 4)
        step = 0
        for ref in piece_refs:
            for half in range(ref.shape[0] // rows):
                for chip in range(chips):
                    for c in range(2):
                        start = half * rows + (chip * 2 + c) * inner
                        layer[jnp.bitwise_xor(core, c), chip, owners[step]] = ref[
                            start : start + inner
                        ]
                step += 1
        contract = (((0,), (0,)), ((), ()))
        for n in range(0, hidden, 256):
            total = jnp.zeros((shard, 256), jnp.float32)
            for side, ref in enumerate((own_ref, other_ref)):
                total += lax.dot_general(
                    layer[side].reshape(chips * rows, shard),
                    ref[:, :, n : n + 256].reshape(chips * rows, 256),
                    contract,
                    preferred_element_type=jnp.float32,
                )
            out_ref[:, n : n + 256] = total.astype(jnp.bfloat16)

    y = lax.axis_index("y")
    beside = (y + 1 + (ys - 2) * (1 - (y & 1))) & (ys - 1)
    place = jnp.stack([lax.axis_index("core"), y, beside]).astype(jnp.int32)
    return pl.pallas_call(
        kernel,
        out_shape=jax.ShapeDtypeStruct((shard, hidden), jnp.bfloat16),
        in_specs=[pl.BlockSpec(memory_space=pltpu.SMEM)]
        + [pl.BlockSpec(memory_space=pltpu.VMEM)] * (len(pieces) + 2),
        out_specs=pl.BlockSpec(memory_space=pltpu.VMEM),
        scratch_shapes=[pltpu.VMEM((2, chips, ys, inner, shard), jnp.bfloat16)],
        compiler_params=pltpu.CompilerParams(vmem_limit_bytes=VMEM_BYTES),
        cost_estimate=pl.CostEstimate(
            flops=4 * chips * rows * hidden * shard, bytes_accessed=6 << 20, transcendentals=0
        ),
        name="weight_gradient",
    )(place, *pieces, chip_rows, other_rows)


def on_device(tokens, routes, up_weight, hidden_grad, gate_pre):
    chips, cores, experts = lax.axis_size("xl"), lax.axis_size("core"), lax.axis_size("ex")
    ys, halves = lax.axis_size("y"), lax.axis_size("h")
    owners = chips * cores
    token_count, width = tokens.shape
    _, shard, hidden = up_weight.shape
    rows = hidden_grad.shape[1]
    inner = halves * experts

    grad_up = derive(hidden_grad[0], gate_pre[0])
    grad_up = grad_up.reshape(experts, ys, halves, hidden).transpose(1, 2, 0, 3)
    grad_up = grad_up.reshape(rows, hidden)
    far, farther, near = (flip(grad_up, "xl", k) for k in (2, 3, 1))
    weight = up_weight[0]
    other_weight = lax.ppermute(weight, "core", CORE_SWAP)

    picks = jnp.any(
        routes[:, :, None] == jnp.arange(experts, dtype=jnp.int32)[None, None, :], axis=1
    ).astype(jnp.bfloat16)
    outgoing = jnp.einsum(
        "te,tqc->qec",
        picks,
        tokens.reshape(token_count, owners, shard),
        preferred_element_type=jnp.float32,
    ).astype(jnp.bfloat16)
    outgoing = jnp.broadcast_to(outgoing[:, None], (owners, halves, experts, shard))
    arrived = exchange(
        outgoing.reshape(owners * halves, experts, shard), ("xl", "core", "h")
    )
    arrived = exchange(arrived.transpose(1, 0, 2), "ex")
    arrived = arrived.reshape(experts, owners, halves, shard).transpose(1, 2, 0, 3)
    arrived = arrived.reshape(rows, shard)

    partial, chip_rows = row_partials((grad_up, near, far, farther), weight, other_weight)
    summed = exchange(
        partial.reshape(ys * chips * halves, experts, cores * shard), ("y", "xl", "h")
    )
    summed = summed.reshape(ys, chips, halves, experts, cores * shard).astype(jnp.float32)
    row_grad = jnp.sum(summed, axis=(0, 2)).astype(jnp.bfloat16)
    returned = exchange(row_grad.transpose(1, 0, 2), "ex")
    grad_tokens = jnp.einsum(
        "te,eqc->tqc", picks, returned, preferred_element_type=jnp.float32
    ).astype(jnp.bfloat16)

    across = flip(arrived, "y", 4)
    pair = jnp.concatenate([arrived, across], axis=0)
    beside = [(y, (y + (ys - 1 if y % 2 == 0 else 1)) % ys) for y in range(ys)]
    pieces = (
        arrived,
        across,
        flip(pair, "y", 2),
        flip(pair, "y", 1),
        lax.ppermute(pair, "y", beside),
    )
    other_chip_rows = lax.ppermute(chip_rows, "core", CORE_SWAP)
    weight_grad = weight_gradient(pieces, chip_rows, other_chip_rows)
    return grad_tokens.reshape(token_count, width), weight_grad[None]


def solution(mesh):
    shape = (mesh.shape["dp"] // 2, 2, mesh.shape["expert"], mesh.shape["etensor"] // 2, 2)
    fine = Mesh(mesh.devices.reshape(shape), ("xl", "core", "ex", "y", "h"))
    tokens_spec = P(("xl", "core", "ex", "y", "h"), None)
    expert_spec = P("ex", ("xl", "core"), ("y", "h"))
    return jax.shard_map(
        on_device,
        mesh=fine,
        in_specs=(tokens_spec, tokens_spec, expert_spec, expert_spec, expert_spec),
        out_specs=(tokens_spec, expert_spec),
        check_vma=False,
    )
```

time: 155 us -> 123 us (0.79)
  waiting for transfers between devices: 78 us -> 28 us
  starting transfers between devices: 36.6 us -> 79.3 us
  blocking collectives: 24.4 us -> 0 us
  Pallas kernels: 0 us -> 6.25 us
  matrix products: 5.28 us -> 0.93 us
    all_to_all x6 -> x4, waiting for transfers between devices: 76.2 us -> 4.52 us  [exchange(): return lax.all_to_all(blocks, axes, split_axis=0, concat_axis=0, tiled=True)]
    all_to_all x1 -> x0, blocking collectives: 24.4 us -> none  [exchange(): return lax.all_to_all(blocks, axes, split_axis=0, concat_axis=0, tiled=True)]
    ppermute x0 -> x7, starting transfers between devices: none -> 24.4 us  [the longest x6 22 us: flip(): lax.ppermute(value, axis, [(i, i ^ bits) for i in range(lax.axis_size(axi...]
    ppermute x0 -> x7, waiting for transfers between devices: none -> 23.5 us  [the longest x6 23.5 us: flip(): lax.ppermute(value, axis, [(i, i ^ bits) for i in range(lax.axis_size(axi...]
    ppermute x1, starting transfers between devices: 3.65 us -> 16.2 us  [on_device(): other_weight = lax.ppermute(weight, 'core', CORE_SWAP)]
    pallas_call x0 -> x2, Pallas kernels: none -> 6.25 us  [the longest x1 3.71 us: row_partials(): pl.pallas_call(kernel, out_shape=(jax.ShapeDtypeStruct((ys, chips, inner,...]
    all_to_all x6 -> x4, starting transfers between devices: 29.4 us -> 35 us  [exchange(): return lax.all_to_all(blocks, axes, split_axis=0, concat_axis=0, tiled=True)]
    dot_general x3 -> x0, matrix products: 4.35 us -> none  [the longest x1 2.71 us: on_device(): lax.dot_general(other_rows, other_chip_rows, contract, preferred_element_...]
  transfers between devices with their start and end apart: 8 -> 13, of which waited for: 7 -> 3; matrix products, arithmetic and copies ran while one was open for 6% -> 4% of each run, Pallas kernels for 0% -> 5%
where the time goes in v2:
time: 123 us; the launch traced here: 122 us
  starting transfers between devices  79.3 us (64%)
  waiting for transfers between devices  28 us (23%)
  Pallas kernels  6.25 us (5%)
  local copies, waits for them, and re-layouts  3.91 us (3%)
  other arithmetic  2.61 us (2%)
    all_to_all x4, starting transfers between devices, exchange(): return lax.all_to_all(blocks, axes, split_axis=0, concat_axis=0, tiled=True)  35 us
    ppermute x6, waiting for transfers between devices, flip(): lax.ppermute(value, axis, [(i, i ^ bits) for i in range(lax.axis_size(axi...  23.5 us
    ppermute x6, starting transfers between devices, flip(): lax.ppermute(value, axis, [(i, i ^ bits) for i in range(lax.axis_size(axi...  22 us
    ppermute x1, starting transfers between devices, on_device(): other_weight = lax.ppermute(weight, 'core', CORE_SWAP)  16.2 us
    all_to_all x4, waiting for transfers between devices, exchange(): return lax.all_to_all(blocks, axes, split_axis=0, concat_axis=0, tiled=True)  4.52 us
    pallas_call x1, Pallas kernels, row_partials(): pl.pallas_call(kernel, out_shape=(jax.ShapeDtypeStruct((ys, chips, inner,...  3.71 us
    ppermute x1, starting transfers between devices, on_device(): other_chip_rows = lax.ppermute(chip_rows, 'core', CORE_SWAP)  3.65 us
    pallas_call x1, Pallas kernels, weight_gradient(): pl.pallas_call(kernel, out_shape=jax.ShapeDtypeStruct((shard, hidden), jn...  2.54 us
  transfers between devices with their start and end apart: 13, of which 3 were waited for; matrix products, arithmetic and copies ran while one was open for 4% of the time, Pallas kernels for 5%

profile of v2, /device:TPU:1, one launch (start us, length us, event | category | flops | bytes accessed | tf_op | source)
XLA Modules:
  0.0 121.8 jit_solution(15506012957741025764)
XLA Ops:
  0.7 16.2 %collective-permute-start.3 = (bf16[384,1024]{1,0:T(8,128)(2,1)}, bf16[384,1024]{1,0:T(8,128)(2,1)S(1)}, u32[]{:S(2)}, u32[]{:S(2)}) collective-permute-start(bf16[384,1024]{1,0:T(8,128)(2,1)} %bitcast.39), channel_id=1, source_target_pairs={{0,128},{128,0},{1,129},{129,1},{2,130},{130,2},{3,131},{131,3},{4... | collective-permute-start | bytes 2359304 | tf_op jit(solution)/shard_map/ppermute | solution.py:131
  17.8 3.4 %all-to-all-start.2 = ((bf16[16,8,384]{2,1,0:T(8,128)(2,1)}), bf16[16,8,384]{2,1,0:T(8,128)(2,1)S(1)}, u32[]{:S(2)}, u32[]{:S(2)}) async-start(bf16[16,8,384]{2,1,0:T(8,128)(2,1)} %bitcast.15), calls=%async_computation.2 | async-start | bytes 196608 | tf_op jit(solution)/shard_map/all_to_all | solution.py:19
  21.2 1.1 fusion.2
  22.6 3.2 %collective-permute-start = (bf16[128,1024]{1,0:T(8,128)(2,1)S(1)}, bf16[128,1024]{1,0:T(8,128)(2,1)S(1)}, u32[]{:S(2)}, u32[]{:S(2)}) collective-permute-start(bf16[128,1024]{1,0:T(8,128)(2,1)S(1)} %bitcast.35), channel_id=1, source_target_pairs={{0,256},{256,0},{512,768},{768,512},{1,257},{257,1},{513,769},{769... | collective-permute-start | bytes 786440 | tf_op jit(solution)/shard_map/ppermute | solution.py:23
  25.8 4.0 %collective-permute-start.1 = (bf16[128,1024]{1,0:T(8,128)(2,1)S(1)}, bf16[128,1024]{1,0:T(8,128)(2,1)S(1)}, u32[]{:S(2)}, u32[]{:S(2)}) collective-permute-start(bf16[128,1024]{1,0:T(8,128)(2,1)S(1)} %bitcast.36), channel_id=1, source_target_pairs={{0,512},{256,768},{512,0},{768,256},{1,513},{257,769},{513,1},{769... | collective-permute-start | bytes 786440 | tf_op jit(solution)/shard_map/ppermute | solution.py:23
  29.9 2.1 %collective-permute-start.2 = (bf16[128,1024]{1,0:T(8,128)(2,1)S(1)}, bf16[128,1024]{1,0:T(8,128)(2,1)S(1)}, u32[]{:S(2)}, u32[]{:S(2)}) collective-permute-start(bf16[128,1024]{1,0:T(8,128)(2,1)S(1)} %bitcast.37), channel_id=1, source_target_pairs={{0,768},{256,512},{512,256},{768,0},{1,769},{257,513},{513,257},{7... | collective-permute-start | bytes 786440 | tf_op jit(solution)/shard_map/ppermute | solution.py:23
  32.0 0.7 copy.27
  32.6 7.2 %all-to-all-start.3 = ((bf16[8,16,384]{2,1,0:T(8,128)(2,1)}), bf16[8,16,384]{2,1,0:T(8,128)(2,1)S(1)}, u32[]{:S(2)}, u32[]{:S(2)}) async-start(bf16[8,16,384]{2,1,0:T(8,128)(2,1)} %copy.27), calls=%async_computation.3 | async-start | bytes 196608 | tf_op jit(solution)/shard_map/all_to_all | solution.py:19
  39.9 7.2 %collective-permute-done.1.refs_2_ = bf16[128,1024]{1,0:T(8,128)(2,1)S(1)} collective-permute-done((bf16[128,1024]{1,0:T(8,128)(2,1)S(1)}, bf16[128,1024]{1,0:T(8,128)(2,1)S(1)}, u32[]{:S(2)}, u32[]{:S(2)}) %collective-permute-start.1) | collective-permute-done | bytes 262176 | tf_op jit(solution)/shard_map/ppermute | solution.py:23
  47.2 0.7 copy-done.2
  47.9 0.9 copy-done.3
  48.8 3.7 %row_partials.1 = (bf16[8,4,16,768]{3,2,1,0:T(8,128)(2,1)}, bf16[4,128,1024]{2,1,0:T(8,128)(2,1)S(1)}) custom-call(s32[2]{0:T(128)S(1)} %pad_add_fusion.place, bf16[128,1024]{1,0:T(8,128)(2,1)S(1)} %bitcast.38, bf16[128,1024]{1,0:T(8,128)(2,1)S(1)} %collective-permute-done.refs_1_, bf16[128,1024]{1,0:T(8,128)(2,1)S(1)} %collective-permute-done.1.refs_2_, ...), custom_call_target="tpu_custom_call" | custom-call | flops 805306368 | bytes 6291456 | tf_op jit(solution)/shard_map/row_partials/pallas_call | solution.py:49
  52.6 11.4 %all-to-all-start = ((bf16[64,8,768]{2,1,0:T(8,128)(2,1)}), bf16[64,8,768]{2,1,0:T(8,128)(2,1)}, u32[]{:S(2)}, u32[]{:S(2)}) async-start(bf16[64,8,768]{2,1,0:T(8,128)(2,1)} %bitcast.7), calls=%async_computation | async-start | bytes 1572864 | tf_op jit(solution)/shard_map/all_to_all | solution.py:19
  64.0 3.6 %collective-permute-start.8 = (bf16[4,128,1024]{2,1,0:T(8,128)(2,1)S(1)}, bf16[4,128,1024]{2,1,0:T(8,128)(2,1)S(1)}, u32[]{:S(2)}, u32[]{:S(2)}) collective-permute-start(bf16[4,128,1024]{2,1,0:T(8,128)(2,1)S(1)} %get-tuple-element.5.refs_5_), channel_id=1, source_target_pairs={{0,128},{128,0},{1,129},{129,1},{2,130},{130,2},{3,131},{131,3},{4... | collective-permute-start | bytes 3145736 | tf_op jit(solution)/shard_map/ppermute | solution.py:171
  67.7 7.1 %collective-permute-start.4 = (bf16[128,384]{1,0:T(8,128)(2,1)S(1)}, bf16[128,384]{1,0:T(8,128)(2,1)S(1)}, u32[]{:S(2)}, u32[]{:S(2)}) collective-permute-start(bf16[128,384]{1,0:T(8,128)(2,1)S(1)} %bitcast.32), channel_id=1, source_target_pairs={{0,8},{2,10},{4,12},{6,14},{8,0},{10,2},{12,4},{14,6},{1,9},{3,11}... | collective-permute-start | bytes 294920 | tf_op jit(solution)/shard_map/ppermute | solution.py:23
  74.8 16.2 %collective-permute-done.4.refs_1_ = bf16[128,384]{1,0:T(8,128)(2,1)S(1)} collective-permute-done((bf16[128,384]{1,0:T(8,128)(2,1)S(1)}, bf16[128,384]{1,0:T(8,128)(2,1)S(1)}, u32[]{:S(2)}, u32[]{:S(2)}) %collective-permute-start.4) | collective-permute-done | bytes 98336 | tf_op jit(solution)/shard_map/ppermute | solution.py:23
  91.1 3.2 %collective-permute-start.5 = (bf16[256,384]{1,0:T(8,128)(2,1)S(1)}, bf16[256,384]{1,0:T(8,128)(2,1)S(1)}, u32[]{:S(2)}, u32[]{:S(2)}) collective-permute-start(bf16[256,384]{1,0:T(8,128)(2,1)S(1)} %pad_maximum_fusion), channel_id=1, source_target_pairs={{0,4},{2,6},{4,0},{6,2},{8,12},{10,14},{12,8},{14,10},{1,5},{3,7},... | collective-permute-start | bytes 589832 | tf_op jit(solution)/shard_map/ppermute | solution.py:23
  94.3 2.4 %collective-permute-start.6 = (bf16[256,384]{1,0:T(8,128)(2,1)S(1)}, bf16[256,384]{1,0:T(8,128)(2,1)S(1)}, u32[]{:S(2)}, u32[]{:S(2)}) collective-permute-start(bf16[256,384]{1,0:T(8,128)(2,1)S(1)} %pad_maximum_fusion), channel_id=1, source_target_pairs={{0,2},{2,0},{4,6},{6,4},{8,10},{10,8},{12,14},{14,12},{1,3},{3,1},... | collective-permute-start | bytes 589832 | tf_op jit(solution)/shard_map/ppermute | solution.py:23
  96.6 2.4 %collective-permute-start.7 = (bf16[256,384]{1,0:T(8,128)(2,1)S(1)}, bf16[256,384]{1,0:T(8,128)(2,1)S(1)}, u32[]{:S(2)}, u32[]{:S(2)}) collective-permute-start(bf16[256,384]{1,0:T(8,128)(2,1)S(1)} %pad_maximum_fusion), channel_id=1, source_target_pairs={{0,14},{2,4},{4,2},{6,8},{8,6},{10,12},{12,10},{14,0},{1,15},{3,5}... | collective-permute-start | bytes 589832 | tf_op jit(solution)/shard_map/ppermute | solution.py:169
  99.1 1.2 %reduce_sum.12 = bf16[4,8,768]{2,1,0:T(8,128)(2,1)S(1)} reduce(bf16[8,4,2,8,768]{4,3,2,1,0:T(8,128)(2,1)} %bitcast.8, bf16[]{:T(256)} %constant.24.clone.1), dimensions={0,2}, to_apply=%region_1.0 | reduce | flops 368640 | bytes 835586 | tf_op jit(solution)/shard_map/reduce_sum | solution.py:155
  101.0 13.0 %all-to-all-start.1 = ((bf16[8,4,768]{2,1,0:T(4,128)(2,1)}), bf16[8,4,768]{2,1,0:T(4,128)(2,1)S(1)}, u32[]{:S(2)}, u32[]{:S(2)}) async-start(bf16[8,4,768]{2,1,0:T(4,128)(2,1)} %copy.24), calls=%async_computation.1 | async-start | bytes 98304 | tf_op jit(solution)/shard_map/all_to_all | solution.py:19
  114.0 2.5 %weight_gradient.1 = bf16[384,1024]{1,0:T(8,128)(2,1)} custom-call(s32[3]{0:T(128)S(1)} %pad_add_fusion.1.place, bf16[128,384]{1,0:T(8,128)(2,1)S(1)} %bitcast.34, bf16[128,384]{1,0:T(8,128)(2,1)S(1)} %collective-permute-done.4.refs_1_, bf16[256,384]{1,0:T(8,128)(2,1)S(1)} %collective-permute-done.5.refs_2_, ...), custom_call_target="tpu_custom_call" | custom-call | flops 805306368 | bytes 6291456 | tf_op jit(solution)/shard_map/weight_gradient/pallas_call | solution.py:102
  116.6 4.5 %all-to-all-done.1 = bf16[8,4,768]{2,1,0:T(4,128)(2,1)S(1)} async-done(((bf16[8,4,768]{2,1,0:T(4,128)(2,1)}), bf16[8,4,768]{2,1,0:T(4,128)(2,1)S(1)}, u32[]{:S(2)}, u32[]{:S(2)}) %all-to-all-start.1) | async-done | bytes 49184 | tf_op jit(solution)/shard_map/all_to_all | solution.py:19
  121.1 0.7 convolution_convert_fusion.1
  (30 shorter events, 2.1 us)
Async XLA Ops:
  0.6 16.3 %copy-start = (bf16[4,3072]{1,0:T(4,128)(2,1)S(1)}, bf16[4,3072]{1,0:T(4,128)(2,1)}, u32[]{:S(2)}) copy-start(bf16[4,3072]{1,0:T(4,128)(2,1)} %param.5) | copy-start | bytes 73732
  0.6 16.2 %copy-start.5 = (s32[4,2]{0,1:T(2,128)S(1)}, s32[4,2]{0,1:T(2,128)}, u32[]{:S(2)}) copy-start(s32[4,2]{0,1:T(2,128)} %param.6) | copy-start | bytes 100
  0.7 20.6 %copy-start.4 = (bf16[1,128,1024]{2,1,0:T(8,128)(2,1)S(1)}, bf16[1,128,1024]{2,1,0:T(8,128)(2,1)}, u32[]{:S(2)}) copy-start(bf16[1,128,1024]{2,1,0:T(8,128)(2,1)} %param.9) | copy-start | bytes 786436
  0.7 47.2 %collective-permute-start.3 = (bf16[384,1024]{1,0:T(8,128)(2,1)}, bf16[384,1024]{1,0:T(8,128)(2,1)S(1)}, u32[]{:S(2)}, u32[]{:S(2)}) collective-permute-start(bf16[384,1024]{1,0:T(8,128)(2,1)} %bitcast.39), channel_id=1, source_target_pairs={{0,128},{128,0},{1,129},{129,1},{2,130},{130,2},{3,131},{131,3},{4... | collective-permute-start | bytes 2359304 | tf_op jit(solution)/shard_map/ppermute | solution.py:131
  17.8 14.2 %all-to-all-start.2 = ((bf16[16,8,384]{2,1,0:T(8,128)(2,1)}), bf16[16,8,384]{2,1,0:T(8,128)(2,1)S(1)}, u32[]{:S(2)}, u32[]{:S(2)}) async-start(bf16[16,8,384]{2,1,0:T(8,128)(2,1)} %bitcast.15), calls=%async_computation.2 | async-start | bytes 196608 | tf_op jit(solution)/shard_map/all_to_all | solution.py:19
  22.4 25.5 %copy-start.1 = (bf16[1,384,1024]{2,1,0:T(8,128)(2,1)S(1)}, bf16[1,384,1024]{2,1,0:T(8,128)(2,1)}, u32[]{:S(2)}) copy-start(bf16[1,384,1024]{2,1,0:T(8,128)(2,1)} %param.7) | copy-start | bytes 2359300
  22.6 17.3 %collective-permute-start = (bf16[128,1024]{1,0:T(8,128)(2,1)S(1)}, bf16[128,1024]{1,0:T(8,128)(2,1)S(1)}, u32[]{:S(2)}, u32[]{:S(2)}) collective-permute-start(bf16[128,1024]{1,0:T(8,128)(2,1)S(1)} %bitcast.35), channel_id=1, source_target_pairs={{0,256},{256,0},{512,768},{768,512},{1,257},{257,1},{513,769},{769... | collective-permute-start | bytes 786440 | tf_op jit(solution)/shard_map/ppermute | solution.py:23
  25.8 21.3 %collective-permute-start.1 = (bf16[128,1024]{1,0:T(8,128)(2,1)S(1)}, bf16[128,1024]{1,0:T(8,128)(2,1)S(1)}, u32[]{:S(2)}, u32[]{:S(2)}) collective-permute-start(bf16[128,1024]{1,0:T(8,128)(2,1)S(1)} %bitcast.36), channel_id=1, source_target_pairs={{0,512},{256,768},{512,0},{768,256},{1,513},{257,769},{513,1},{769... | collective-permute-start | bytes 786440 | tf_op jit(solution)/shard_map/ppermute | solution.py:23
  29.9 17.3 %collective-permute-start.2 = (bf16[128,1024]{1,0:T(8,128)(2,1)S(1)}, bf16[128,1024]{1,0:T(8,128)(2,1)S(1)}, u32[]{:S(2)}, u32[]{:S(2)}) collective-permute-start(bf16[128,1024]{1,0:T(8,128)(2,1)S(1)} %bitcast.37), channel_id=1, source_target_pairs={{0,768},{256,512},{512,256},{768,0},{1,769},{257,513},{513,257},{7... | collective-permute-start | bytes 786440 | tf_op jit(solution)/shard_map/ppermute | solution.py:23
  32.6 19.9 %all-to-all-start.3 = ((bf16[8,16,384]{2,1,0:T(8,128)(2,1)}), bf16[8,16,384]{2,1,0:T(8,128)(2,1)S(1)}, u32[]{:S(2)}, u32[]{:S(2)}) async-start(bf16[8,16,384]{2,1,0:T(8,128)(2,1)} %copy.27), calls=%async_computation.3 | async-start | bytes 196608 | tf_op jit(solution)/shard_map/all_to_all | solution.py:19
  47.2 0.7 copy-start.2
  47.9 1.0 copy-start.3
  52.6 46.5 %all-to-all-start = ((bf16[64,8,768]{2,1,0:T(8,128)(2,1)}), bf16[64,8,768]{2,1,0:T(8,128)(2,1)}, u32[]{:S(2)}, u32[]{:S(2)}) async-start(bf16[64,8,768]{2,1,0:T(8,128)(2,1)} %bitcast.7), calls=%async_computation | async-start | bytes 1572864 | tf_op jit(solution)/shard_map/all_to_all | solution.py:19
  64.0 50.0 %collective-permute-start.8 = (bf16[4,128,1024]{2,1,0:T(8,128)(2,1)S(1)}, bf16[4,128,1024]{2,1,0:T(8,128)(2,1)S(1)}, u32[]{:S(2)}, u32[]{:S(2)}) collective-permute-start(bf16[4,128,1024]{2,1,0:T(8,128)(2,1)S(1)} %get-tuple-element.5.refs_5_), channel_id=1, source_target_pairs={{0,128},{128,0},{1,129},{129,1},{2,130},{130,2},{3,131},{131,3},{4... | collective-permute-start | bytes 3145736 | tf_op jit(solution)/shard_map/ppermute | solution.py:171
  67.7 23.4 %collective-permute-start.4 = (bf16[128,384]{1,0:T(8,128)(2,1)S(1)}, bf16[128,384]{1,0:T(8,128)(2,1)S(1)}, u32[]{:S(2)}, u32[]{:S(2)}) collective-permute-start(bf16[128,384]{1,0:T(8,128)(2,1)S(1)} %bitcast.32), channel_id=1, source_target_pairs={{0,8},{2,10},{4,12},{6,14},{8,0},{10,2},{12,4},{14,6},{1,9},{3,11}... | collective-permute-start | bytes 294920 | tf_op jit(solution)/shard_map/ppermute | solution.py:23
  91.1 23.0 %collective-permute-start.5 = (bf16[256,384]{1,0:T(8,128)(2,1)S(1)}, bf16[256,384]{1,0:T(8,128)(2,1)S(1)}, u32[]{:S(2)}, u32[]{:S(2)}) collective-permute-start(bf16[256,384]{1,0:T(8,128)(2,1)S(1)} %pad_maximum_fusion), channel_id=1, source_target_pairs={{0,4},{2,6},{4,0},{6,2},{8,12},{10,14},{12,8},{14,10},{1,5},{3,7},... | collective-permute-start | bytes 589832 | tf_op jit(solution)/shard_map/ppermute | solution.py:23
  94.3 19.8 %collective-permute-start.6 = (bf16[256,384]{1,0:T(8,128)(2,1)S(1)}, bf16[256,384]{1,0:T(8,128)(2,1)S(1)}, u32[]{:S(2)}, u32[]{:S(2)}) collective-permute-start(bf16[256,384]{1,0:T(8,128)(2,1)S(1)} %pad_maximum_fusion), channel_id=1, source_target_pairs={{0,2},{2,0},{4,6},{6,4},{8,10},{10,8},{12,14},{14,12},{1,3},{3,1},... | collective-permute-start | bytes 589832 | tf_op jit(solution)/shard_map/ppermute | solution.py:23
  96.6 17.4 %collective-permute-start.7 = (bf16[256,384]{1,0:T(8,128)(2,1)S(1)}, bf16[256,384]{1,0:T(8,128)(2,1)S(1)}, u32[]{:S(2)}, u32[]{:S(2)}) collective-permute-start(bf16[256,384]{1,0:T(8,128)(2,1)S(1)} %pad_maximum_fusion), channel_id=1, source_target_pairs={{0,14},{2,4},{4,2},{6,8},{8,6},{10,12},{12,10},{14,0},{1,15},{3,5}... | collective-permute-start | bytes 589832 | tf_op jit(solution)/shard_map/ppermute | solution.py:169
  101.0 20.1 %all-to-all-start.1 = ((bf16[8,4,768]{2,1,0:T(4,128)(2,1)}), bf16[8,4,768]{2,1,0:T(4,128)(2,1)S(1)}, u32[]{:S(2)}, u32[]{:S(2)}) async-start(bf16[8,4,768]{2,1,0:T(4,128)(2,1)} %copy.24), calls=%async_computation.1 | async-start | bytes 98304 | tf_op jit(solution)/shard_map/all_to_all | solution.py:19

commit v3 on v2

v3 whole, which is shorter than its diff:
```python
import jax
import jax.numpy as jnp
from jax import lax
from jax.experimental import pallas as pl
from jax.experimental.pallas import tpu as pltpu
from jax.sharding import Mesh, PartitionSpec as P

CORE_SWAP = ((0, 1), (1, 0))
VMEM_BYTES = 40 * 1024 * 1024


def derive(grad_rows, gate_rows):
    gate_wide = gate_rows.astype(jnp.float32)
    sigma = jax.nn.sigmoid(gate_wide)
    return (grad_rows.astype(jnp.float32) * gate_wide * sigma).astype(jnp.bfloat16)


def exchange(blocks, axes):
    return lax.all_to_all(blocks, axes, split_axis=0, concat_axis=0, tiled=True)


def flip(value, axis, bits):
    return lax.ppermute(value, axis, [(i, i ^ bits) for i in range(lax.axis_size(axis))])


def place_of(*indices):
    return jnp.stack(indices).astype(jnp.int32)


SMEM = pl.BlockSpec(memory_space=pltpu.SMEM)
VMEM = pl.BlockSpec(memory_space=pltpu.VMEM)


def row_partials(chip_rows, weight, other_weight):
    chips = len(chip_rows)
    rows, hidden = chip_rows[0].shape
    shard = weight.shape[0]
    ys = lax.axis_size("y")
    inner = rows // ys

    def kernel(place, *refs):
        row_refs, (weight_ref, other_ref, out_ref, stack_ref) = refs[:chips], refs[chips:]
        chip, core = place[0], place[1]
        for k in range(chips):
            stack_ref[chip ^ k] = row_refs[k][...]
        blocks = stack_ref[...].reshape(chips * rows, hidden)
        for side, ref in ((core, weight_ref), (1 - core, other_ref)):
            part = lax.dot_general(
                blocks, ref[...], (((1,), (1,)), ((), ())), preferred_element_type=jnp.float32
            ).astype(jnp.bfloat16)
            columns = pl.ds(pl.multiple_of(side * shard, 128), shard)
            for chip_to in range(chips):
                for y in range(ys):
                    start = (chip_to * ys + y) * inner
                    out_ref[y, chip_to, :, columns] = part[start : start + inner]

    return pl.pallas_call(
        kernel,
        out_shape=(
            jax.ShapeDtypeStruct((ys, chips, inner, 2 * shard), jnp.bfloat16),
            jax.ShapeDtypeStruct((chips, rows, hidden), jnp.bfloat16),
        ),
        in_specs=[SMEM] + [VMEM] * (chips + 2),
        out_specs=(VMEM,) * 2,
        compiler_params=pltpu.CompilerParams(vmem_limit_bytes=VMEM_BYTES),
        cost_estimate=pl.CostEstimate(
            flops=4 * chips * rows * hidden * shard, bytes_accessed=6 << 20, transcendentals=0
        ),
        name="row_partials",
    )(
        place_of(lax.axis_index("xl"), lax.axis_index("core")),
        *chip_rows, weight, other_weight,
    )


def reduce_rows(partials):
    ys, chips, halves, experts, features = partials.shape

    def kernel(in_ref, out_ref):
        sums = []
        for chip in range(chips):
            total = jnp.zeros((experts, features), jnp.float32)
            for y in range(ys):
                for half in range(halves):
                    total += in_ref[y, chip, half].astype(jnp.float32)
            sums.append(total)
        out_ref[...] = jnp.stack(sums, axis=1).astype(jnp.bfloat16)

    return pl.pallas_call(
        kernel,
        out_shape=jax.ShapeDtypeStruct((experts, chips, features), jnp.bfloat16),
        in_specs=[VMEM],
        out_specs=VMEM,
        compiler_params=pltpu.CompilerParams(vmem_limit_bytes=VMEM_BYTES),
        cost_estimate=pl.CostEstimate(
            flops=ys * halves * chips * experts * features, bytes_accessed=1 << 20, transcendentals=0
        ),
        name="reduce_rows",
    )(partials)


def weight_gradient(token_rows, chip_rows, other_rows):
    chips, rows, hidden = chip_rows.shape
    ys, _, shard = token_rows.shape
    inner = rows // ys

    def kernel(place, token_ref, own_ref, other_ref, out_ref, layer):
        core = place[0]
        for y in range(ys):
            for chip in range(chips):
                for c in range(2):
                    start = (chip * 2 + c) * inner
                    layer[core ^ c, chip, y] = token_ref[y, start : start + inner]
        contract = (((0,), (0,)), ((), ()))
        for n in range(0, hidden, 256):
            total = jnp.zeros((shard, 256), jnp.float32)
            for side, ref in enumerate((own_ref, other_ref)):
                total += lax.dot_general(
                    layer[side].reshape(chips * rows, shard),
                    ref[:, :, n : n + 256].reshape(chips * rows, 256),
                    contract,
                    preferred_element_type=jnp.float32,
                )
            out_ref[:, n : n + 256] = total.astype(jnp.bfloat16)

    return pl.pallas_call(
        kernel,
        out_shape=jax.ShapeDtypeStruct((shard, hidden), jnp.bfloat16),
        in_specs=[SMEM] + [VMEM] * 3,
        out_specs=VMEM,
        scratch_shapes=[pltpu.VMEM((2, chips, ys, inner, shard), jnp.bfloat16)],
        compiler_params=pltpu.CompilerParams(vmem_limit_bytes=VMEM_BYTES),
        cost_estimate=pl.CostEstimate(
            flops=4 * chips * rows * hidden * shard, bytes_accessed=6 << 20, transcendentals=0
        ),
        name="weight_gradient",
    )(place_of(lax.axis_index("core")), token_rows, chip_rows, other_rows)


def on_device(tokens, routes, up_weight, hidden_grad, gate_pre):
    chips, cores, experts = lax.axis_size("xl"), lax.axis_size("core"), lax.axis_size("ex")
    ys, halves = lax.axis_size("y"), lax.axis_size("h")
    owners = chips * cores
    token_count, width = tokens.shape
    _, shard, hidden = up_weight.shape
    rows = hidden_grad.shape[1]
    inner = halves * experts

    grad_up = derive(hidden_grad[0], gate_pre[0])
    grad_up = grad_up.reshape(experts, ys, halves, hidden).transpose(1, 2, 0, 3)
    grad_up = grad_up.reshape(rows, hidden)
    far, farther, near = (flip(grad_up, "xl", k) for k in (2, 3, 1))

    picks = jnp.any(
        routes[:, :, None] == jnp.arange(experts, dtype=jnp.int32)[None, None, :], axis=1
    ).astype(jnp.bfloat16)
    outgoing = jnp.einsum(
        "te,tqc->qec",
        picks,
        tokens.reshape(token_count, owners, shard),
        preferred_element_type=jnp.float32,
    ).astype(jnp.bfloat16)
    outgoing = jnp.broadcast_to(outgoing[:, None], (owners, halves, experts, shard))
    arrived = exchange(
        outgoing.reshape(owners * halves, experts, shard), ("xl", "core", "h")
    )
    arrived, weight = lax.optimization_barrier((arrived, up_weight[0]))
    other_weight = lax.ppermute(weight, "core", CORE_SWAP)
    arrived = exchange(arrived.transpose(1, 0, 2), "ex")
    arrived = arrived.reshape(experts, owners, halves, shard).transpose(1, 2, 0, 3)
    arrived = arrived.reshape(rows, shard)

    arrived, near, far = lax.optimization_barrier((arrived, near, far))
    token_rows = exchange(jnp.broadcast_to(arrived[None], (ys,) + arrived.shape), "y")

    partial, chip_rows = row_partials(
        (grad_up, near, far, farther), weight, other_weight
    )
    partial, token_rows = lax.optimization_barrier((partial, token_rows))
    partial = exchange(
        partial.reshape(ys * chips * halves, experts, cores * shard), ("y", "xl", "h")
    )
    row_grad = reduce_rows(partial.reshape(ys, chips, halves, experts, cores * shard))
    returned = exchange(row_grad, "ex")
    grad_tokens = jnp.einsum(
        "te,eqc->tqc", picks, returned, preferred_element_type=jnp.float32
    ).astype(jnp.bfloat16)

    other_chip_rows = lax.ppermute(chip_rows, "core", CORE_SWAP)
    weight_grad = weight_gradient(token_rows, chip_rows, other_chip_rows)
    return grad_tokens.reshape(token_count, width), weight_grad[None]


def solution(mesh):
    shape = (mesh.shape["dp"] // 2, 2, mesh.shape["expert"], mesh.shape["etensor"] // 2, 2)
    fine = Mesh(mesh.devices.reshape(shape), ("xl", "core", "ex", "y", "h"))
    tokens_spec = P(("xl", "core", "ex", "y", "h"), None)
    expert_spec = P("ex", ("xl", "core"), ("y", "h"))
    return jax.shard_map(
        on_device,
        mesh=fine,
        in_specs=(tokens_spec, tokens_spec, expert_spec, expert_spec, expert_spec),
        out_specs=(tokens_spec, expert_spec),
        check_vma=False,
    )
```

time: 123 us -> 127 us (1.033)
  starting transfers between devices: 79.3 us -> 58.7 us
  blocking collectives: 0 us -> 14.6 us
  waiting for transfers between devices: 28 us -> 35.2 us
  local copies, waits for them, and re-layouts: 3.91 us -> 5.62 us
    all_to_all x4, waiting for transfers between devices: 4.52 us -> 25.5 us  [exchange(): return lax.all_to_all(blocks, axes, split_axis=0, concat_axis=0, tiled=True)]
    all_to_all x0 -> x1, blocking collectives: none -> 14.6 us  [exchange(): return lax.all_to_all(blocks, axes, split_axis=0, concat_axis=0, tiled=True)]
    ppermute x6 -> x3, waiting for transfers between devices: 23.5 us -> 9.66 us  [flip(): lax.ppermute(value, axis, [(i, i ^ bits) for i in range(lax.axis_size(axi...]
    ppermute x6 -> x3, starting transfers between devices: 22 us -> 9.27 us  [flip(): lax.ppermute(value, axis, [(i, i ^ bits) for i in range(lax.axis_size(axi...]
    ppermute x1, starting transfers between devices: 16.2 us -> 4.44 us  [on_device(): other_weight = lax.ppermute(weight, 'core', CORE_SWAP)]
    all_to_all x4, starting transfers between devices: 35 us -> 42 us  [exchange(): return lax.all_to_all(blocks, axes, split_axis=0, concat_axis=0, tiled=True)]
    ppermute x1 -> x0, starting transfers between devices: 2.41 us -> none  [on_device(): lax.ppermute(pair, 'y', beside)]
    unnamed x12 -> x14, local copies, waits for them, and re-layouts: 1.68 us -> 3.68 us
  transfers between devices with their start and end apart: 13 -> 9, of which waited for: 3 -> 3; matrix products, arithmetic and copies ran while one was open for 4% -> 1% of each run, Pallas kernels for 5% -> 5%
where the time goes in v3:
time: 127 us; the launch traced here: 125 us
  starting transfers between devices  58.7 us (46%)
  waiting for transfers between devices  35.2 us (28%)
  blocking collectives  14.6 us (11%)
  Pallas kernels  6.73 us (5%)
  local copies, waits for them, and re-layouts  5.62 us (4%)
  other arithmetic  1.99 us (2%)
    all_to_all x4, starting transfers between devices, exchange(): return lax.all_to_all(blocks, axes, split_axis=0, concat_axis=0, tiled=True)  42 us
    all_to_all x4, waiting for transfers between devices, exchange(): return lax.all_to_all(blocks, axes, split_axis=0, concat_axis=0, tiled=True)  25.5 us
    all_to_all x1, blocking collectives, exchange(): return lax.all_to_all(blocks, axes, split_axis=0, concat_axis=0, tiled=True)  14.6 us
    ppermute x3, waiting for transfers between devices, flip(): lax.ppermute(value, axis, [(i, i ^ bits) for i in range(lax.axis_size(axi...  9.66 us
    ppermute x3, starting transfers between devices, flip(): lax.ppermute(value, axis, [(i, i ^ bits) for i in range(lax.axis_size(axi...  9.27 us
    ppermute x1, starting transfers between devices, on_device(): other_weight = lax.ppermute(weight, 'core', CORE_SWAP)  4.44 us
    unnamed x14, local copies, waits for them, and re-layouts  3.68 us
    pallas_call x1, Pallas kernels, weight_gradient(): pl.pallas_call(kernel, out_shape=jax.ShapeDtypeStruct((shard, hidden), jn...  3.22 us
  transfers between devices with their start and end apart: 9, of which 3 were waited for; matrix products, arithmetic and copies ran while one was open for 1% of the time, Pallas kernels for 5%

profile of v3, /device:TPU:1, one launch (start us, length us, event | category | flops | bytes accessed | tf_op | source)
XLA Modules:
  0.0 124.6 jit_solution(18360774429873967791)
XLA Ops:
  0.7 0.8 fusion.7
  2.3 17.5 %all-to-all-start = ((bf16[16,8,384]{2,1,0:T(8,128)(2,1)}), bf16[16,8,384]{2,1,0:T(8,128)(2,1)S(1)}, u32[]{:S(2)}, u32[]{:S(2)}) async-start(bf16[16,8,384]{2,1,0:T(8,128)(2,1)} %bitcast.7), calls=%async_computation | async-start | bytes 196608 | tf_op jit(solution)/shard_map/all_to_all | solution.py:19
  19.8 1.1 fusion.2
  21.2 3.3 %collective-permute-start = (bf16[128,1024]{1,0:T(8,128)(2,1)S(1)}, bf16[128,1024]{1,0:T(8,128)(2,1)S(1)}, u32[]{:S(2)}, u32[]{:S(2)}) collective-permute-start(bf16[128,1024]{1,0:T(8,128)(2,1)S(1)} %bitcast.25), channel_id=1, source_target_pairs={{0,256},{256,0},{512,768},{768,512},{1,257},{257,1},{513,769},{769... | collective-permute-start | bytes 786440 | tf_op jit(solution)/shard_map/ppermute | solution.py:23
  24.5 4.0 %collective-permute-start.1 = (bf16[128,1024]{1,0:T(8,128)(2,1)S(1)}, bf16[128,1024]{1,0:T(8,128)(2,1)S(1)}, u32[]{:S(2)}, u32[]{:S(2)}) collective-permute-start(bf16[128,1024]{1,0:T(8,128)(2,1)S(1)} %bitcast.26), channel_id=1, source_target_pairs={{0,512},{256,768},{512,0},{768,256},{1,513},{257,769},{513,1},{769... | collective-permute-start | bytes 786440 | tf_op jit(solution)/shard_map/ppermute | solution.py:23
  28.6 14.6 %all_to_all.25 = bf16[8,16,384]{2,1,0:T(8,128)(2,1)S(1)} all-to-all(bf16[8,16,384]{2,1,0:T(8,128)(2,1)S(1)} %copy.25), channel_id=1, replica_groups=mesh['xl'=4,'core'=2,'ex'=8,'y'=8,'h'=2] {'ex'}, dimensions={0} | all-to-all | bytes 196608 | tf_op jit(solution)/shard_map/all_to_all | solution.py:19
  43.3 1.0 broadcast_in_dim.7
  44.2 7.4 %all-to-all-start.2 = ((bf16[8,128,384]{2,1,0:T(8,128)(2,1)}), bf16[8,128,384]{2,1,0:T(8,128)(2,1)S(1)}, u32[]{:S(2)}, u32[]{:S(2)}) async-start(bf16[8,128,384]{2,1,0:T(8,128)(2,1)} %broadcast_in_dim.7), calls=%async_computation.2 | async-start | bytes 1572864 | tf_op jit(solution)/shard_map/all_to_all | solution.py:19
  51.7 4.4 %collective-permute-start.3 = (bf16[384,1024]{1,0:T(8,128)(2,1)S(1)}, bf16[384,1024]{1,0:T(8,128)(2,1)S(1)}, u32[]{:S(2)}, u32[]{:S(2)}) collective-permute-start(bf16[384,1024]{1,0:T(8,128)(2,1)S(1)} %bitcast.29), channel_id=1, source_target_pairs={{0,128},{128,0},{1,129},{129,1},{2,130},{130,2},{3,131},{131,3},{4... | collective-permute-start | bytes 2359304 | tf_op jit(solution)/shard_map/ppermute | solution.py:168
  56.1 1.9 %collective-permute-start.2 = (bf16[128,1024]{1,0:T(8,128)(2,1)S(1)}, bf16[128,1024]{1,0:T(8,128)(2,1)S(1)}, u32[]{:S(2)}, u32[]{:S(2)}) collective-permute-start(bf16[128,1024]{1,0:T(8,128)(2,1)S(1)} %bitcast.27), channel_id=1, source_target_pairs={{0,768},{256,512},{512,256},{768,0},{1,769},{257,513},{513,257},{7... | collective-permute-start | bytes 786440 | tf_op jit(solution)/shard_map/ppermute | solution.py:23
  58.1 9.7 %collective-permute-done.2.refs_3_ = bf16[128,1024]{1,0:T(8,128)(2,1)S(1)} collective-permute-done((bf16[128,1024]{1,0:T(8,128)(2,1)S(1)}, bf16[128,1024]{1,0:T(8,128)(2,1)S(1)}, u32[]{:S(2)}, u32[]{:S(2)}) %collective-permute-start.2) | collective-permute-done | bytes 262176 | tf_op jit(solution)/shard_map/ppermute | solution.py:23
  67.8 0.7 copy-done.4
  68.5 0.9 copy-done.2
  69.4 1.1 copy-done.3
  70.5 0.9 copy-done.5
  71.4 2.7 %row_partials.1 = (bf16[8,4,16,768]{3,2,1,0:T(8,128)(2,1)}, bf16[4,128,1024]{2,1,0:T(8,128)(2,1)S(1)}) custom-call(s32[2]{0:T(128)S(1)} %pad_add_fusion.place, bf16[128,1024]{1,0:T(8,128)(2,1)S(1)} %bitcast.28, bf16[128,1024]{1,0:T(8,128)(2,1)S(1)} %collective-permute-done.refs_1_, bf16[128,1024]{1,0:T(8,128)(2,1)S(1)} %collective-permute-done.1.refs_2_, ...), custom_call_target="tpu_custom_call" | custom-call | flops 805306368 | bytes 6291456 | tf_op jit(solution)/shard_map/row_partials/pallas_call | solution.py:57
  74.2 13.8 %all-to-all-start.3 = ((bf16[64,8,768]{2,1,0:T(8,128)(2,1)}), bf16[64,8,768]{2,1,0:T(8,128)(2,1)S(1)}, u32[]{:S(2)}, u32[]{:S(2)}) async-start(bf16[64,8,768]{2,1,0:T(8,128)(2,1)} %bitcast.13), calls=%async_computation.3 | async-start | bytes 1572864 | tf_op jit(solution)/shard_map/all_to_all | solution.py:19
  88.0 3.0 %collective-permute-start.4 = (bf16[4,128,1024]{2,1,0:T(8,128)(2,1)S(1)}, bf16[4,128,1024]{2,1,0:T(8,128)(2,1)}, u32[]{:S(2)}, u32[]{:S(2)}) collective-permute-start(bf16[4,128,1024]{2,1,0:T(8,128)(2,1)S(1)} %get-tuple-element.19.own_ref), channel_id=1, source_target_pairs={{0,128},{128,0},{1,129},{129,1},{2,130},{130,2},{3,131},{131,3},{4... | collective-permute-start | bytes 3145736 | tf_op jit(solution)/shard_map/ppermute | solution.py:189
  91.0 21.7 %all-to-all-done.3 = bf16[64,8,768]{2,1,0:T(8,128)(2,1)S(1)} async-done(((bf16[64,8,768]{2,1,0:T(8,128)(2,1)}), bf16[64,8,768]{2,1,0:T(8,128)(2,1)S(1)}, u32[]{:S(2)}, u32[]{:S(2)}) %all-to-all-start.3) | async-done | bytes 786464 | tf_op jit(solution)/shard_map/all_to_all | solution.py:19
  112.7 0.8 reduce_rows.1
  113.5 3.3 %all-to-all-start.4 = ((bf16[8,4,768]{2,1,0:T(4,128)(2,1)}), bf16[8,4,768]{2,1,0:T(4,128)(2,1)S(1)}, u32[]{:S(2)}, u32[]{:S(2)}) async-start(bf16[8,4,768]{2,1,0:T(4,128)(2,1)} %reduce_rows.1), calls=%async_computation.4 | async-start | bytes 98304 | tf_op jit(solution)/shard_map/all_to_all | solution.py:19
  116.9 3.2 %weight_gradient.1 = bf16[384,1024]{1,0:T(8,128)(2,1)} custom-call(s32[1]{0:T(128)} %bitcast.2.place, bf16[8,128,384]{2,1,0:T(8,128)(2,1)S(1)} %all-to-all-done.2.token_ref, bf16[4,128,1024]{2,1,0:T(8,128)(2,1)S(1)} %get-tuple-element.19.own_ref, bf16[4,128,1024]{2,1,0:T(8,128)(2,1)} %collective-permute-done.4.other_ref), custom_call_target="tpu_custom_call" | custom-call | flops 805306368 | bytes 6291456 | tf_op jit(solution)/shard_map/weight_gradient/pallas_call | solution.py:126
  120.1 3.7 %all-to-all-done.4 = bf16[8,4,768]{2,1,0:T(4,128)(2,1)S(1)} async-done(((bf16[8,4,768]{2,1,0:T(4,128)(2,1)}), bf16[8,4,768]{2,1,0:T(4,128)(2,1)S(1)}, u32[]{:S(2)}, u32[]{:S(2)}) %all-to-all-start.4) | async-done | bytes 49184 | tf_op jit(solution)/shard_map/all_to_all | solution.py:19
  123.8 0.7 convolution_convert_fusion.1
  (24 shorter events, 1.3 us)
Async XLA Ops:
  0.6 0.8 copy-start
  0.6 19.1 %copy-start.6 = (bf16[1,128,1024]{2,1,0:T(8,128)(2,1)S(1)}, bf16[1,128,1024]{2,1,0:T(8,128)(2,1)}, u32[]{:S(2)}) copy-start(bf16[1,128,1024]{2,1,0:T(8,128)(2,1)} %param.9) | copy-start | bytes 786436
  2.3 26.2 %all-to-all-start = ((bf16[16,8,384]{2,1,0:T(8,128)(2,1)}), bf16[16,8,384]{2,1,0:T(8,128)(2,1)S(1)}, u32[]{:S(2)}, u32[]{:S(2)}) async-start(bf16[16,8,384]{2,1,0:T(8,128)(2,1)} %bitcast.7), calls=%async_computation | async-start | bytes 196608 | tf_op jit(solution)/shard_map/all_to_all | solution.py:19
  21.2 22.1 %collective-permute-start = (bf16[128,1024]{1,0:T(8,128)(2,1)S(1)}, bf16[128,1024]{1,0:T(8,128)(2,1)S(1)}, u32[]{:S(2)}, u32[]{:S(2)}) collective-permute-start(bf16[128,1024]{1,0:T(8,128)(2,1)S(1)} %bitcast.25), channel_id=1, source_target_pairs={{0,256},{256,0},{512,768},{768,512},{1,257},{257,1},{513,769},{769... | collective-permute-start | bytes 786440 | tf_op jit(solution)/shard_map/ppermute | solution.py:23
  24.5 18.8 %collective-permute-start.1 = (bf16[128,1024]{1,0:T(8,128)(2,1)S(1)}, bf16[128,1024]{1,0:T(8,128)(2,1)S(1)}, u32[]{:S(2)}, u32[]{:S(2)}) collective-permute-start(bf16[128,1024]{1,0:T(8,128)(2,1)S(1)} %bitcast.26), channel_id=1, source_target_pairs={{0,512},{256,768},{512,0},{768,256},{1,513},{257,769},{513,1},{769... | collective-permute-start | bytes 786440 | tf_op jit(solution)/shard_map/ppermute | solution.py:23
  44.2 7.4 %copy-start.1 = (bf16[1,384,1024]{2,1,0:T(8,128)(2,1)S(1)}, bf16[1,384,1024]{2,1,0:T(8,128)(2,1)}, u32[]{:S(2)}) copy-start(bf16[1,384,1024]{2,1,0:T(8,128)(2,1)} %param.7) | copy-start | bytes 2359300
  44.2 29.9 %all-to-all-start.2 = ((bf16[8,128,384]{2,1,0:T(8,128)(2,1)}), bf16[8,128,384]{2,1,0:T(8,128)(2,1)S(1)}, u32[]{:S(2)}, u32[]{:S(2)}) async-start(bf16[8,128,384]{2,1,0:T(8,128)(2,1)} %broadcast_in_dim.7), calls=%async_computation.2 | async-start | bytes 1572864 | tf_op jit(solution)/shard_map/all_to_all | solution.py:19
  51.7 16.8 %collective-permute-start.3 = (bf16[384,1024]{1,0:T(8,128)(2,1)S(1)}, bf16[384,1024]{1,0:T(8,128)(2,1)S(1)}, u32[]{:S(2)}, u32[]{:S(2)}) collective-permute-start(bf16[384,1024]{1,0:T(8,128)(2,1)S(1)} %bitcast.29), channel_id=1, source_target_pairs={{0,128},{128,0},{1,129},{129,1},{2,130},{130,2},{3,131},{131,3},{4... | collective-permute-start | bytes 2359304 | tf_op jit(solution)/shard_map/ppermute | solution.py:168
  56.1 11.7 %collective-permute-start.2 = (bf16[128,1024]{1,0:T(8,128)(2,1)S(1)}, bf16[128,1024]{1,0:T(8,128)(2,1)S(1)}, u32[]{:S(2)}, u32[]{:S(2)}) collective-permute-start(bf16[128,1024]{1,0:T(8,128)(2,1)S(1)} %bitcast.27), channel_id=1, source_target_pairs={{0,768},{256,512},{512,256},{768,0},{1,769},{257,513},{513,257},{7... | collective-permute-start | bytes 786440 | tf_op jit(solution)/shard_map/ppermute | solution.py:23
  67.8 0.7 copy-start.4
  68.5 0.9 copy-start.2
  69.4 1.1 copy-start.3
  70.5 0.9 copy-start.5
  74.2 38.5 %all-to-all-start.3 = ((bf16[64,8,768]{2,1,0:T(8,128)(2,1)}), bf16[64,8,768]{2,1,0:T(8,128)(2,1)S(1)}, u32[]{:S(2)}, u32[]{:S(2)}) async-start(bf16[64,8,768]{2,1,0:T(8,128)(2,1)} %bitcast.13), calls=%async_computation.3 | async-start | bytes 1572864 | tf_op jit(solution)/shard_map/all_to_all | solution.py:19
  88.0 28.9 %collective-permute-start.4 = (bf16[4,128,1024]{2,1,0:T(8,128)(2,1)S(1)}, bf16[4,128,1024]{2,1,0:T(8,128)(2,1)}, u32[]{:S(2)}, u32[]{:S(2)}) collective-permute-start(bf16[4,128,1024]{2,1,0:T(8,128)(2,1)S(1)} %get-tuple-element.19.own_ref), channel_id=1, source_target_pairs={{0,128},{128,0},{1,129},{129,1},{2,130},{130,2},{3,131},{131,3},{4... | collective-permute-start | bytes 3145736 | tf_op jit(solution)/shard_map/ppermute | solution.py:189
  113.5 10.3 %all-to-all-start.4 = ((bf16[8,4,768]{2,1,0:T(4,128)(2,1)}), bf16[8,4,768]{2,1,0:T(4,128)(2,1)S(1)}, u32[]{:S(2)}, u32[]{:S(2)}) async-start(bf16[8,4,768]{2,1,0:T(4,128)(2,1)} %reduce_rows.1), calls=%async_computation.4 | async-start | bytes 98304 | tf_op jit(solution)/shard_map/all_to_all | solution.py:19

commit v4 on v3

--- a/solution.py
+++ b/solution.py
@@ -23,6 +23,11 @@
     return lax.ppermute(value, axis, [(i, i ^ bits) for i in range(lax.axis_size(axis))])
 
 
+def shift(value, axis, by):
+    size = lax.axis_size(axis)
+    return lax.ppermute(value, axis, [(i, (i + by) % size) for i in range(size)])
+
+
 def place_of(*indices):
     return jnp.stack(indices).astype(jnp.int32)
 
@@ -35,7 +40,7 @@
     chips = len(chip_rows)
     rows, hidden = chip_rows[0].shape
     shard = weight.shape[0]
-    ys = lax.axis_size("y")
+    ys = lax.axis_size("yh") * lax.axis_size("yl")
     inner = rows // ys
 
     def kernel(place, *refs):
@@ -64,7 +69,7 @@
         out_specs=(VMEM,) * 2,
         compiler_params=pltpu.CompilerParams(vmem_limit_bytes=VMEM_BYTES),
         cost_estimate=pl.CostEstimate(
-            flops=4 * chips * rows * hidden * shard, bytes_accessed=6 << 20, transcendentals=0
+            flops=64 * chips * rows * hidden * shard, bytes_accessed=6 << 20, transcendentals=0
         ),
         name="row_partials",
     )(
@@ -99,18 +104,22 @@
     )(partials)
 
 
-def weight_gradient(token_rows, chip_rows, other_rows):
+def weight_gradient(pieces, chip_rows, other_rows):
     chips, rows, hidden = chip_rows.shape
-    ys, _, shard = token_rows.shape
+    twins, shard = pieces[0].shape[0] // rows, pieces[0].shape[1]
+    ys = len(pieces) * twins
     inner = rows // ys
 
-    def kernel(place, token_ref, own_ref, other_ref, out_ref, layer):
-        core = place[0]
-        for y in range(ys):
-            for chip in range(chips):
-                for c in range(2):
-                    start = (chip * 2 + c) * inner
-                    layer[core ^ c, chip, y] = token_ref[y, start : start + inner]
+    def kernel(place, *refs):
+        piece_refs, (own_ref, other_ref, out_ref, layer) = refs[: len(pieces)], refs[len(pieces) :]
+        core, pair = place[0], place[1]
+        for away, ref in enumerate(piece_refs):
+            for twin in range(twins):
+                y = ((pair + away) & (len(pieces) - 1)) * twins + twin
+                for chip in range(chips):
+                    for c in range(2):
+                        start = twin * rows + (chip * 2 + c) * inner
+                        layer[core ^ c, chip, y] = ref[start : start + inner]
         contract = (((0,), (0,)), ((), ()))
         for n in range(0, hidden, 256):
             total = jnp.zeros((shard, 256), jnp.float32)
@@ -126,7 +135,7 @@
     return pl.pallas_call(
         kernel,
         out_shape=jax.ShapeDtypeStruct((shard, hidden), jnp.bfloat16),
-        in_specs=[SMEM] + [VMEM] * 3,
+        in_specs=[SMEM] + [VMEM] * (len(pieces) + 2),
         out_specs=VMEM,
         scratch_shapes=[pltpu.VMEM((2, chips, ys, inner, shard), jnp.bfloat16)],
         compiler_params=pltpu.CompilerParams(vmem_limit_bytes=VMEM_BYTES),
@@ -134,12 +143,13 @@
             flops=4 * chips * rows * hidden * shard, bytes_accessed=6 << 20, transcendentals=0
         ),
         name="weight_gradient",
-    )(place_of(lax.axis_index("core")), token_rows, chip_rows, other_rows)
+    )(place_of(lax.axis_index("core"), lax.axis_index("yh")), *pieces, chip_rows, other_rows)
 
 
 def on_device(tokens, routes, up_weight, hidden_grad, gate_pre):
     chips, cores, experts = lax.axis_size("xl"), lax.axis_size("core"), lax.axis_size("ex")
-    ys, halves = lax.axis_size("y"), lax.axis_size("h")
+    pairs, twins = lax.axis_size("yh"), lax.axis_size("yl")
+    ys, halves = pairs * twins, lax.axis_size("h")
     owners = chips * cores
     token_count, width = tokens.shape
     _, shard, hidden = up_weight.shape
@@ -164,21 +174,22 @@
     arrived = exchange(
         outgoing.reshape(owners * halves, experts, shard), ("xl", "core", "h")
     )
-    arrived, weight = lax.optimization_barrier((arrived, up_weight[0]))
+    weight = up_weight[0]
     other_weight = lax.ppermute(weight, "core", CORE_SWAP)
-    arrived = exchange(arrived.transpose(1, 0, 2), "ex")
-    arrived = arrived.reshape(experts, owners, halves, shard).transpose(1, 2, 0, 3)
-    arrived = arrived.reshape(rows, shard)
-
-    arrived, near, far = lax.optimization_barrier((arrived, near, far))
-    token_rows = exchange(jnp.broadcast_to(arrived[None], (ys,) + arrived.shape), "y")
+    arrived = jnp.broadcast_to(
+        arrived.transpose(1, 0, 2)[:, None], (experts, twins, owners * halves, shard)
+    )
+    arrived = exchange(
+        arrived.reshape(experts * twins, owners * halves, shard), ("ex", "yl")
+    )
+    arrived = arrived.reshape(experts, twins, owners, halves, shard).transpose(1, 2, 3, 0, 4)
+    arrived = arrived.reshape(twins * rows, shard)
 
     partial, chip_rows = row_partials(
         (grad_up, near, far, farther), weight, other_weight
     )
-    partial, token_rows = lax.optimization_barrier((partial, token_rows))
     partial = exchange(
-        partial.reshape(ys * chips * halves, experts, cores * shard), ("y", "xl", "h")
+        partial.reshape(ys * chips * halves, experts, cores * shard), ("yh", "yl", "xl", "h")
     )
     row_grad = reduce_rows(partial.reshape(ys, chips, halves, experts, cores * shard))
     returned = exchange(row_grad, "ex")
@@ -186,16 +197,17 @@
         "te,eqc->tqc", picks, returned, preferred_element_type=jnp.float32
     ).astype(jnp.bfloat16)
 
+    pieces = [arrived] + [shift(arrived, "yh", -away) for away in range(1, pairs)]
     other_chip_rows = lax.ppermute(chip_rows, "core", CORE_SWAP)
-    weight_grad = weight_gradient(token_rows, chip_rows, other_chip_rows)
+    weight_grad = weight_gradient(pieces, chip_rows, other_chip_rows)
     return grad_tokens.reshape(token_count, width), weight_grad[None]
 
 
 def solution(mesh):
-    shape = (mesh.shape["dp"] // 2, 2, mesh.shape["expert"], mesh.shape["etensor"] // 2, 2)
-    fine = Mesh(mesh.devices.reshape(shape), ("xl", "core", "ex", "y", "h"))
-    tokens_spec = P(("xl", "core", "ex", "y", "h"), None)
-    expert_spec = P("ex", ("xl", "core"), ("y", "h"))
+    shape = (mesh.shape["dp"] // 2, 2, mesh.shape["expert"], mesh.shape["etensor"] // 4, 2, 2)
+    fine = Mesh(mesh.devices.reshape(shape), ("xl", "core", "ex", "yh", "yl", "h"))
+    tokens_spec = P(("xl", "core", "ex", "yh", "yl", "h"), None)
+    expert_spec = P("ex", ("xl", "core"), ("yh", "yl", "h"))
     return jax.shard_map(
         on_device,
         mesh=fine,

time: 127 us -> 123 us (0.969); the launches traced: 125 us -> 123 us
  blocking collectives: 14.6 us -> 0 us
  starting transfers between devices: 58.7 us -> 69.1 us
  waiting for transfers between devices: 35.2 us -> 39.5 us
  local copies, waits for them, and re-layouts: 5.62 us -> 4.35 us
    all_to_all x4, starting transfers between devices: 42 us -> 26.9 us  [exchange(): return lax.all_to_all(blocks, axes, split_axis=0, concat_axis=0, tiled=True)]
    all_to_all x1 -> x0, blocking collectives: 14.6 us -> none  [exchange(): return lax.all_to_all(blocks, axes, split_axis=0, concat_axis=0, tiled=True)]
    ppermute x0 -> x3, starting transfers between devices: none -> 13.4 us  [shift(): lax.ppermute(value, axis, [(i, (i + by) % size) for i in range(size)])]
    ppermute x0 -> x3, waiting for transfers between devices: none -> 11.8 us  [shift(): lax.ppermute(value, axis, [(i, (i + by) % size) for i in range(size)])]
    ppermute x1, starting transfers between devices: 4.44 us -> 16.1 us  [on_device(): other_weight = lax.ppermute(weight, 'core', CORE_SWAP)]
    ppermute x3, waiting for transfers between devices: 9.66 us -> 0.01 us  [flip(): lax.ppermute(value, axis, [(i, i ^ bits) for i in range(lax.axis_size(axi...]
    all_to_all x4, waiting for transfers between devices: 25.5 us -> 27.7 us  [exchange(): return lax.all_to_all(blocks, axes, split_axis=0, concat_axis=0, tiled=True)]
    unnamed x14 -> x10, local copies, waits for them, and re-layouts: 3.68 us -> 1.67 us
  transfers between devices with their start and end apart: 9 -> 12, of which waited for: 3 -> 6; matrix products, arithmetic and copies ran while one was open for 1% -> 4% of each run, Pallas kernels for 5% -> 5%
where the time goes in v4:
time: 123 us
  starting transfers between devices  69.1 us (56%)
  waiting for transfers between devices  39.5 us (32%)
  Pallas kernels  6.45 us (5%)
  local copies, waits for them, and re-layouts  4.35 us (4%)
  other arithmetic  1.42 us (1%)
    all_to_all x4, waiting for transfers between devices, exchange(): return lax.all_to_all(blocks, axes, split_axis=0, concat_axis=0, tiled=True)  27.7 us
    all_to_all x4, starting transfers between devices, exchange(): return lax.all_to_all(blocks, axes, split_axis=0, concat_axis=0, tiled=True)  26.9 us
    ppermute x1, starting transfers between devices, on_device(): other_weight = lax.ppermute(weight, 'core', CORE_SWAP)  16.1 us
    ppermute x3, starting transfers between devices, shift(): lax.ppermute(value, axis, [(i, (i + by) % size) for i in range(size)])  13.4 us
    ppermute x3, waiting for transfers between devices, shift(): lax.ppermute(value, axis, [(i, (i + by) % size) for i in range(size)])  11.8 us
    ppermute x3, starting transfers between devices, flip(): lax.ppermute(value, axis, [(i, i ^ bits) for i in range(lax.axis_size(axi...  9.4 us
    ppermute x1, starting transfers between devices, on_device(): other_chip_rows = lax.ppermute(chip_rows, 'core', CORE_SWAP)  3.41 us
    pallas_call x1, Pallas kernels, weight_gradient(): pl.pallas_call(kernel, out_shape=jax.ShapeDtypeStruct((shard, hidden), jn...  2.94 us
  transfers between devices with their start and end apart: 12, of which 6 were waited for; matrix products, arithmetic and copies ran while one was open for 4% of the time, Pallas kernels for 5%

profile of v4, /device:TPU:1, one launch (start us, length us, event | category | flops | bytes accessed | tf_op | source)
XLA Modules:
  0.0 122.6 jit_solution(8187881195369062265)
XLA Ops:
  0.6 16.1 %collective-permute-start.3 = (bf16[384,1024]{1,0:T(8,128)(2,1)}, bf16[384,1024]{1,0:T(8,128)(2,1)S(1)}, u32[]{:S(2)}, u32[]{:S(2)}) collective-permute-start(bf16[384,1024]{1,0:T(8,128)(2,1)} %bitcast.35), channel_id=1, source_target_pairs={{0,128},{128,0},{1,129},{129,1},{2,130},{130,2},{3,131},{131,3},{4... | collective-permute-start | bytes 2359304 | tf_op jit(solution)/shard_map/ppermute | solution.py:178
  16.7 1.2 fusion.2
  18.2 2.1 %collective-permute-start = (bf16[128,1024]{1,0:T(8,128)(2,1)S(1)}, bf16[128,1024]{1,0:T(8,128)(2,1)S(1)}, u32[]{:S(2)}, u32[]{:S(2)}) collective-permute-start(bf16[128,1024]{1,0:T(8,128)(2,1)S(1)} %bitcast.31), channel_id=1, source_target_pairs={{0,256},{256,0},{512,768},{768,512},{1,257},{257,1},{513,769},{769... | collective-permute-start | bytes 786440 | tf_op jit(solution)/shard_map/ppermute | solution.py:23
  20.3 1.9 %collective-permute-start.1 = (bf16[128,1024]{1,0:T(8,128)(2,1)S(1)}, bf16[128,1024]{1,0:T(8,128)(2,1)S(1)}, u32[]{:S(2)}, u32[]{:S(2)}) collective-permute-start(bf16[128,1024]{1,0:T(8,128)(2,1)S(1)} %bitcast.32), channel_id=1, source_target_pairs={{0,512},{256,768},{512,0},{768,256},{1,513},{257,769},{513,1},{769... | collective-permute-start | bytes 786440 | tf_op jit(solution)/shard_map/ppermute | solution.py:23
  22.2 5.4 %collective-permute-start.2 = (bf16[128,1024]{1,0:T(8,128)(2,1)S(1)}, bf16[128,1024]{1,0:T(8,128)(2,1)S(1)}, u32[]{:S(2)}, u32[]{:S(2)}) collective-permute-start(bf16[128,1024]{1,0:T(8,128)(2,1)S(1)} %bitcast.33), channel_id=1, source_target_pairs={{0,768},{256,512},{512,256},{768,0},{1,769},{257,513},{513,257},{7... | collective-permute-start | bytes 786440 | tf_op jit(solution)/shard_map/ppermute | solution.py:23
  28.6 4.2 %all-to-all-start.2 = ((bf16[16,8,384]{2,1,0:T(8,128)(2,1)}), bf16[16,8,384]{2,1,0:T(8,128)(2,1)S(1)}, u32[]{:S(2)}, u32[]{:S(2)}) async-start(bf16[16,8,384]{2,1,0:T(8,128)(2,1)} %bitcast.13), calls=%async_computation.2 | async-start | bytes 196608 | tf_op jit(solution)/shard_map/all_to_all | solution.py:19
  32.8 17.3 %all-to-all-done.2 = bf16[16,8,384]{2,1,0:T(8,128)(2,1)S(1)} async-done(((bf16[16,8,384]{2,1,0:T(8,128)(2,1)}), bf16[16,8,384]{2,1,0:T(8,128)(2,1)S(1)}, u32[]{:S(2)}, u32[]{:S(2)}) %all-to-all-start.2) | async-done | bytes 98336 | tf_op jit(solution)/shard_map/all_to_all | solution.py:19
  50.8 8.7 %all-to-all-start.3 = ((bf16[16,16,384]{2,1,0:T(8,128)(2,1)}), bf16[16,16,384]{2,1,0:T(8,128)(2,1)}, u32[]{:S(2)}, u32[]{:S(2)}) async-start(bf16[16,16,384]{2,1,0:T(8,128)(2,1)} %bitcast.15), calls=%async_computation.3 | async-start | bytes 393216 | tf_op jit(solution)/shard_map/all_to_all | solution.py:19
  60.3 0.9 copy-done.3
  61.2 2.7 %row_partials.1 = (bf16[8,4,16,768]{3,2,1,0:T(8,128)(2,1)}, bf16[4,128,1024]{2,1,0:T(8,128)(2,1)S(1)}) custom-call(s32[2]{0:T(128)S(1)} %pad_add_fusion.place, bf16[128,1024]{1,0:T(8,128)(2,1)S(1)} %bitcast.34, bf16[128,1024]{1,0:T(8,128)(2,1)S(1)} %collective-permute-done.refs_1_, bf16[128,1024]{1,0:T(8,128)(2,1)S(1)} %collective-permute-done.1.refs_2_, ...), custom_call_target="tpu_custom_call" | custom-call | flops 12884901888 | bytes 6291456 | tf_op jit(solution)/shard_map/row_partials/pallas_call | solution.py:62
  64.0 4.1 %all-to-all-done.3 = bf16[16,16,384]{2,1,0:T(8,128)(2,1)} async-done(((bf16[16,16,384]{2,1,0:T(8,128)(2,1)}), bf16[16,16,384]{2,1,0:T(8,128)(2,1)}, u32[]{:S(2)}, u32[]{:S(2)}) %all-to-all-start.3) | async-done | bytes 196640 | tf_op jit(solution)/shard_map/all_to_all | solution.py:19
  68.1 10.6 %all-to-all-start = ((bf16[64,8,768]{2,1,0:T(8,128)(2,1)}), bf16[64,8,768]{2,1,0:T(8,128)(2,1)S(1)}, u32[]{:S(2)}, u32[]{:S(2)}) async-start(bf16[64,8,768]{2,1,0:T(8,128)(2,1)} %bitcast.7), calls=%async_computation | async-start | bytes 1572864 | tf_op jit(solution)/shard_map/all_to_all | solution.py:19
  78.7 3.4 %collective-permute-start.7 = (bf16[4,128,1024]{2,1,0:T(8,128)(2,1)S(1)}, bf16[4,128,1024]{2,1,0:T(8,128)(2,1)S(1)}, u32[]{:S(2)}, u32[]{:S(2)}) collective-permute-start(bf16[4,128,1024]{2,1,0:T(8,128)(2,1)S(1)} %get-tuple-element.5.refs_4_), channel_id=1, source_target_pairs={{0,128},{128,0},{1,129},{129,1},{2,130},{130,2},{3,131},{131,3},{4... | collective-permute-start | bytes 3145736 | tf_op jit(solution)/shard_map/ppermute | solution.py:201
  82.1 1.0 reshape.51
  83.2 5.5 %collective-permute-start.4 = (bf16[256,384]{1,0:T(8,128)(2,1)S(1)}, bf16[256,384]{1,0:T(8,128)(2,1)S(1)}, u32[]{:S(2)}, u32[]{:S(2)}) collective-permute-start(bf16[256,384]{1,0:T(8,128)(2,1)S(1)} %bitcast.27), channel_id=1, source_target_pairs={{0,12},{4,0},{8,4},{12,8},{1,13},{5,1},{9,5},{13,9},{2,14},{6,2},{... | collective-permute-start | bytes 589832 | tf_op jit(solution)/shard_map/ppermute | solution.py:28
  88.7 3.8 %collective-permute-start.5 = (bf16[256,384]{1,0:T(8,128)(2,1)S(1)}, bf16[256,384]{1,0:T(8,128)(2,1)S(1)}, u32[]{:S(2)}, u32[]{:S(2)}) collective-permute-start(bf16[256,384]{1,0:T(8,128)(2,1)S(1)} %bitcast.28), channel_id=1, source_target_pairs={{0,8},{4,12},{8,0},{12,4},{1,9},{5,13},{9,1},{13,5},{2,10},{6,14},... | collective-permute-start | bytes 589832 | tf_op jit(solution)/shard_map/ppermute | solution.py:28
  92.5 4.1 %collective-permute-start.6 = (bf16[256,384]{1,0:T(8,128)(2,1)S(1)}, bf16[256,384]{1,0:T(8,128)(2,1)}, u32[]{:S(2)}, u32[]{:S(2)}) collective-permute-start(bf16[256,384]{1,0:T(8,128)(2,1)S(1)} %bitcast.29), channel_id=1, source_target_pairs={{0,4},{4,8},{8,12},{12,0},{1,5},{5,9},{9,13},{13,1},{2,6},{6,10},{... | collective-permute-start | bytes 589832 | tf_op jit(solution)/shard_map/ppermute | solution.py:28
  96.6 6.2 %all-to-all-done = bf16[64,8,768]{2,1,0:T(8,128)(2,1)S(1)} async-done(((bf16[64,8,768]{2,1,0:T(8,128)(2,1)}), bf16[64,8,768]{2,1,0:T(8,128)(2,1)S(1)}, u32[]{:S(2)}, u32[]{:S(2)}) %all-to-all-start) | async-done | bytes 786464 | tf_op jit(solution)/shard_map/all_to_all | solution.py:19
  102.9 0.8 reduce_rows.1
  103.7 3.3 %all-to-all-start.1 = ((bf16[8,4,768]{2,1,0:T(4,128)(2,1)}), bf16[8,4,768]{2,1,0:T(4,128)(2,1)S(1)}, u32[]{:S(2)}, u32[]{:S(2)}) async-start(bf16[8,4,768]{2,1,0:T(4,128)(2,1)} %reduce_rows.1), calls=%async_computation.1 | async-start | bytes 98304 | tf_op jit(solution)/shard_map/all_to_all | solution.py:19
  107.1 2.6 %collective-permute-done.4.refs_1_ = bf16[256,384]{1,0:T(8,128)(2,1)S(1)} collective-permute-done((bf16[256,384]{1,0:T(8,128)(2,1)S(1)}, bf16[256,384]{1,0:T(8,128)(2,1)S(1)}, u32[]{:S(2)}, u32[]{:S(2)}) %collective-permute-start.4) | collective-permute-done | bytes 196640 | tf_op jit(solution)/shard_map/ppermute | solution.py:28
  109.7 4.8 %collective-permute-done.5.refs_2_ = bf16[256,384]{1,0:T(8,128)(2,1)S(1)} collective-permute-done((bf16[256,384]{1,0:T(8,128)(2,1)S(1)}, bf16[256,384]{1,0:T(8,128)(2,1)S(1)}, u32[]{:S(2)}, u32[]{:S(2)}) %collective-permute-start.5) | collective-permute-done | bytes 196640 | tf_op jit(solution)/shard_map/ppermute | solution.py:28
  114.5 4.4 %collective-permute-done.6.refs_3_ = bf16[256,384]{1,0:T(8,128)(2,1)} collective-permute-done((bf16[256,384]{1,0:T(8,128)(2,1)S(1)}, bf16[256,384]{1,0:T(8,128)(2,1)}, u32[]{:S(2)}, u32[]{:S(2)}) %collective-permute-start.6) | collective-permute-done | bytes 196640 | tf_op jit(solution)/shard_map/ppermute | solution.py:28
  118.9 2.9 %weight_gradient.1 = bf16[384,1024]{1,0:T(8,128)(2,1)} custom-call(s32[2]{0:T(128)S(1)} %pad_add_fusion.1.place, bf16[256,384]{1,0:T(8,128)(2,1)S(1)} %bitcast.30, bf16[256,384]{1,0:T(8,128)(2,1)S(1)} %collective-permute-done.4.refs_1_, bf16[256,384]{1,0:T(8,128)(2,1)S(1)} %collective-permute-done.5.refs_2_, ...), custom_call_target="tpu_custom_call" | custom-call | flops 805306368 | bytes 6291456 | tf_op jit(solution)/shard_map/weight_gradient/pallas_call | solution.py:135
  (26 shorter events, 3.6 us)
Async XLA Ops:
  0.6 27.1 %copy-start = (bf16[4,3072]{1,0:T(4,128)(2,1)S(1)}, bf16[4,3072]{1,0:T(4,128)(2,1)}, u32[]{:S(2)}) copy-start(bf16[4,3072]{1,0:T(4,128)(2,1)} %param.5) | copy-start | bytes 73732
  0.6 59.6 %collective-permute-start.3 = (bf16[384,1024]{1,0:T(8,128)(2,1)}, bf16[384,1024]{1,0:T(8,128)(2,1)S(1)}, u32[]{:S(2)}, u32[]{:S(2)}) collective-permute-start(bf16[384,1024]{1,0:T(8,128)(2,1)} %bitcast.35), channel_id=1, source_target_pairs={{0,128},{128,0},{1,129},{129,1},{2,130},{130,2},{3,131},{131,3},{4... | collective-permute-start | bytes 2359304 | tf_op jit(solution)/shard_map/ppermute | solution.py:178
  18.0 9.6 %copy-start.4 = (s32[4,2]{0,1:T(2,128)S(1)}, s32[4,2]{0,1:T(2,128)}, u32[]{:S(2)}) copy-start(s32[4,2]{0,1:T(2,128)} %param.6) | copy-start | bytes 100
  18.2 42.1 %copy-start.1 = (bf16[1,384,1024]{2,1,0:T(8,128)(2,1)S(1)}, bf16[1,384,1024]{2,1,0:T(8,128)(2,1)}, u32[]{:S(2)}) copy-start(bf16[1,384,1024]{2,1,0:T(8,128)(2,1)} %param.7) | copy-start | bytes 2359300
  18.2 41.4 %collective-permute-start = (bf16[128,1024]{1,0:T(8,128)(2,1)S(1)}, bf16[128,1024]{1,0:T(8,128)(2,1)S(1)}, u32[]{:S(2)}, u32[]{:S(2)}) collective-permute-start(bf16[128,1024]{1,0:T(8,128)(2,1)S(1)} %bitcast.31), channel_id=1, source_target_pairs={{0,256},{256,0},{512,768},{768,512},{1,257},{257,1},{513,769},{769... | collective-permute-start | bytes 786440 | tf_op jit(solution)/shard_map/ppermute | solution.py:23
  20.3 39.3 %collective-permute-start.1 = (bf16[128,1024]{1,0:T(8,128)(2,1)S(1)}, bf16[128,1024]{1,0:T(8,128)(2,1)S(1)}, u32[]{:S(2)}, u32[]{:S(2)}) collective-permute-start(bf16[128,1024]{1,0:T(8,128)(2,1)S(1)} %bitcast.32), channel_id=1, source_target_pairs={{0,512},{256,768},{512,0},{768,256},{1,513},{257,769},{513,1},{769... | collective-permute-start | bytes 786440 | tf_op jit(solution)/shard_map/ppermute | solution.py:23
  22.2 37.4 %collective-permute-start.2 = (bf16[128,1024]{1,0:T(8,128)(2,1)S(1)}, bf16[128,1024]{1,0:T(8,128)(2,1)S(1)}, u32[]{:S(2)}, u32[]{:S(2)}) collective-permute-start(bf16[128,1024]{1,0:T(8,128)(2,1)S(1)} %bitcast.33), channel_id=1, source_target_pairs={{0,768},{256,512},{512,256},{768,0},{1,769},{257,513},{513,257},{7... | collective-permute-start | bytes 786440 | tf_op jit(solution)/shard_map/ppermute | solution.py:23
  28.6 21.5 %all-to-all-start.2 = ((bf16[16,8,384]{2,1,0:T(8,128)(2,1)}), bf16[16,8,384]{2,1,0:T(8,128)(2,1)S(1)}, u32[]{:S(2)}, u32[]{:S(2)}) async-start(bf16[16,8,384]{2,1,0:T(8,128)(2,1)} %bitcast.13), calls=%async_computation.2 | async-start | bytes 196608 | tf_op jit(solution)/shard_map/all_to_all | solution.py:19
  50.8 17.3 %all-to-all-start.3 = ((bf16[16,16,384]{2,1,0:T(8,128)(2,1)}), bf16[16,16,384]{2,1,0:T(8,128)(2,1)}, u32[]{:S(2)}, u32[]{:S(2)}) async-start(bf16[16,16,384]{2,1,0:T(8,128)(2,1)} %bitcast.15), calls=%async_computation.3 | async-start | bytes 393216 | tf_op jit(solution)/shard_map/all_to_all | solution.py:19
  59.6 0.7 copy-start.2
  60.3 1.0 copy-start.3
  68.1 34.8 %all-to-all-start = ((bf16[64,8,768]{2,1,0:T(8,128)(2,1)}), bf16[64,8,768]{2,1,0:T(8,128)(2,1)S(1)}, u32[]{:S(2)}, u32[]{:S(2)}) async-start(bf16[64,8,768]{2,1,0:T(8,128)(2,1)} %bitcast.7), calls=%async_computation | async-start | bytes 1572864 | tf_op jit(solution)/shard_map/all_to_all | solution.py:19
  78.7 40.2 %collective-permute-start.7 = (bf16[4,128,1024]{2,1,0:T(8,128)(2,1)S(1)}, bf16[4,128,1024]{2,1,0:T(8,128)(2,1)S(1)}, u32[]{:S(2)}, u32[]{:S(2)}) collective-permute-start(bf16[4,128,1024]{2,1,0:T(8,128)(2,1)S(1)} %get-tuple-element.5.refs_4_), channel_id=1, source_target_pairs={{0,128},{128,0},{1,129},{129,1},{2,130},{130,2},{3,131},{131,3},{4... | collective-permute-start | bytes 3145736 | tf_op jit(solution)/shard_map/ppermute | solution.py:201
  83.2 26.5 %collective-permute-start.4 = (bf16[256,384]{1,0:T(8,128)(2,1)S(1)}, bf16[256,384]{1,0:T(8,128)(2,1)S(1)}, u32[]{:S(2)}, u32[]{:S(2)}) collective-permute-start(bf16[256,384]{1,0:T(8,128)(2,1)S(1)} %bitcast.27), channel_id=1, source_target_pairs={{0,12},{4,0},{8,4},{12,8},{1,13},{5,1},{9,5},{13,9},{2,14},{6,2},{... | collective-permute-start | bytes 589832 | tf_op jit(solution)/shard_map/ppermute | solution.py:28
  88.7 25.8 %collective-permute-start.5 = (bf16[256,384]{1,0:T(8,128)(2,1)S(1)}, bf16[256,384]{1,0:T(8,128)(2,1)S(1)}, u32[]{:S(2)}, u32[]{:S(2)}) collective-permute-start(bf16[256,384]{1,0:T(8,128)(2,1)S(1)} %bitcast.28), channel_id=1, source_target_pairs={{0,8},{4,12},{8,0},{12,4},{1,9},{5,13},{9,1},{13,5},{2,10},{6,14},... | collective-permute-start | bytes 589832 | tf_op jit(solution)/shard_map/ppermute | solution.py:28
  92.5 26.4 %collective-permute-start.6 = (bf16[256,384]{1,0:T(8,128)(2,1)S(1)}, bf16[256,384]{1,0:T(8,128)(2,1)}, u32[]{:S(2)}, u32[]{:S(2)}) collective-permute-start(bf16[256,384]{1,0:T(8,128)(2,1)S(1)} %bitcast.29), channel_id=1, source_target_pairs={{0,4},{4,8},{8,12},{12,0},{1,5},{5,9},{9,13},{13,1},{2,6},{6,10},{... | collective-permute-start | bytes 589832 | tf_op jit(solution)/shard_map/ppermute | solution.py:28
  103.7 18.2 %all-to-all-start.1 = ((bf16[8,4,768]{2,1,0:T(4,128)(2,1)}), bf16[8,4,768]{2,1,0:T(4,128)(2,1)S(1)}, u32[]{:S(2)}, u32[]{:S(2)}) async-start(bf16[8,4,768]{2,1,0:T(4,128)(2,1)} %reduce_rows.1), calls=%async_computation.1 | async-start | bytes 98304 | tf_op jit(solution)/shard_map/all_to_all | solution.py:19

commit v5 on v4

--- a/solution.py
+++ b/solution.py
@@ -69,7 +69,7 @@
         out_specs=(VMEM,) * 2,
         compiler_params=pltpu.CompilerParams(vmem_limit_bytes=VMEM_BYTES),
         cost_estimate=pl.CostEstimate(
-            flops=64 * chips * rows * hidden * shard, bytes_accessed=6 << 20, transcendentals=0
+            flops=8 * chips * rows * hidden * shard, bytes_accessed=6 << 20, transcendentals=0
         ),
         name="row_partials",
     )(

time: 123 us -> 112 us (0.911)
  the two profiles are of different devices: /device:TPU:1 before, /device:TPU:2 now
where the time goes in v5:
time: 112 us; the launch traced here: 111 us
  starting transfers between devices  73.5 us (66%)
  waiting for transfers between devices  23.6 us (21%)
  Pallas kernels  6.45 us (6%)
  local copies, waits for them, and re-layouts  4.36 us (4%)
  other arithmetic  1.34 us (1%)
    all_to_all x4, starting transfers between devices, exchange(): return lax.all_to_all(blocks, axes, split_axis=0, concat_axis=0, tiled=True)  46.1 us
    ppermute x3, starting transfers between devices, shift(): lax.ppermute(value, axis, [(i, (i + by) % size) for i in range(size)])  14.1 us
    all_to_all x4, waiting for transfers between devices, exchange(): return lax.all_to_all(blocks, axes, split_axis=0, concat_axis=0, tiled=True)  12.3 us
    ppermute x3, waiting for transfers between devices, flip(): lax.ppermute(value, axis, [(i, i ^ bits) for i in range(lax.axis_size(axi...  11.3 us
    ppermute x3, starting transfers between devices, flip(): lax.ppermute(value, axis, [(i, i ^ bits) for i in range(lax.axis_size(axi...  9.35 us
    pallas_call x1, Pallas kernels, weight_gradient(): pl.pallas_call(kernel, out_shape=jax.ShapeDtypeStruct((shard, hidden), jn...  2.94 us
    pallas_call x1, Pallas kernels, row_partials(): pl.pallas_call(kernel, out_shape=(jax.ShapeDtypeStruct((ys, chips, inner,...  2.72 us
  transfers between devices with their start and end apart: 12, of which 4 were waited for; matrix products, arithmetic and copies ran while one was open for 4% of the time, Pallas kernels for 6%

profile of v5, /device:TPU:2, one launch (start us, length us, event | category | flops | bytes accessed | tf_op | source)
XLA Modules:
  0.0 111.1 jit_solution(3417804756989935985)
XLA Ops:
  0.7 2.1 %collective-permute-start.3 = (bf16[384,1024]{1,0:T(8,128)(2,1)}, bf16[384,1024]{1,0:T(8,128)(2,1)S(1)}, u32[]{:S(2)}, u32[]{:S(2)}) collective-permute-start(bf16[384,1024]{1,0:T(8,128)(2,1)} %bitcast.35), channel_id=1, source_target_pairs={{0,128},{128,0},{1,129},{129,1},{2,130},{130,2},{3,131},{131,3},{4... | collective-permute-start | bytes 2359304 | tf_op jit(solution)/shard_map/ppermute | solution.py:178
  3.7 16.5 %all-to-all-start.2 = ((bf16[16,8,384]{2,1,0:T(8,128)(2,1)}), bf16[16,8,384]{2,1,0:T(8,128)(2,1)S(1)}, u32[]{:S(2)}, u32[]{:S(2)}) async-start(bf16[16,8,384]{2,1,0:T(8,128)(2,1)} %bitcast.13), calls=%async_computation.2 | async-start | bytes 196608 | tf_op jit(solution)/shard_map/all_to_all | solution.py:19
  20.2 1.1 fusion.2
  21.6 2.2 %collective-permute-start = (bf16[128,1024]{1,0:T(8,128)(2,1)S(1)}, bf16[128,1024]{1,0:T(8,128)(2,1)S(1)}, u32[]{:S(2)}, u32[]{:S(2)}) collective-permute-start(bf16[128,1024]{1,0:T(8,128)(2,1)S(1)} %bitcast.31), channel_id=1, source_target_pairs={{0,256},{256,0},{512,768},{768,512},{1,257},{257,1},{513,769},{769... | collective-permute-start | bytes 786440 | tf_op jit(solution)/shard_map/ppermute | solution.py:23
  23.8 4.7 %collective-permute-start.1 = (bf16[128,1024]{1,0:T(8,128)(2,1)S(1)}, bf16[128,1024]{1,0:T(8,128)(2,1)S(1)}, u32[]{:S(2)}, u32[]{:S(2)}) collective-permute-start(bf16[128,1024]{1,0:T(8,128)(2,1)S(1)} %bitcast.32), channel_id=1, source_target_pairs={{0,512},{256,768},{512,0},{768,256},{1,513},{257,769},{513,1},{769... | collective-permute-start | bytes 786440 | tf_op jit(solution)/shard_map/ppermute | solution.py:23
  28.5 2.4 %collective-permute-start.2 = (bf16[128,1024]{1,0:T(8,128)(2,1)S(1)}, bf16[128,1024]{1,0:T(8,128)(2,1)S(1)}, u32[]{:S(2)}, u32[]{:S(2)}) collective-permute-start(bf16[128,1024]{1,0:T(8,128)(2,1)S(1)} %bitcast.33), channel_id=1, source_target_pairs={{0,768},{256,512},{512,256},{768,0},{1,769},{257,513},{513,257},{7... | collective-permute-start | bytes 786440 | tf_op jit(solution)/shard_map/ppermute | solution.py:23
  31.7 8.9 %all-to-all-start.3 = ((bf16[16,16,384]{2,1,0:T(8,128)(2,1)}), bf16[16,16,384]{2,1,0:T(8,128)(2,1)}, u32[]{:S(2)}, u32[]{:S(2)}) async-start(bf16[16,16,384]{2,1,0:T(8,128)(2,1)} %bitcast.15), calls=%async_computation.3 | async-start | bytes 393216 | tf_op jit(solution)/shard_map/all_to_all | solution.py:19
  40.6 5.8 %collective-permute-done.1.refs_2_ = bf16[128,1024]{1,0:T(8,128)(2,1)S(1)} collective-permute-done((bf16[128,1024]{1,0:T(8,128)(2,1)S(1)}, bf16[128,1024]{1,0:T(8,128)(2,1)S(1)}, u32[]{:S(2)}, u32[]{:S(2)}) %collective-permute-start.1) | collective-permute-done | bytes 262176 | tf_op jit(solution)/shard_map/ppermute | solution.py:23
  46.4 5.5 %collective-permute-done.2.refs_3_ = bf16[128,1024]{1,0:T(8,128)(2,1)S(1)} collective-permute-done((bf16[128,1024]{1,0:T(8,128)(2,1)S(1)}, bf16[128,1024]{1,0:T(8,128)(2,1)S(1)}, u32[]{:S(2)}, u32[]{:S(2)}) %collective-permute-start.2) | collective-permute-done | bytes 262176 | tf_op jit(solution)/shard_map/ppermute | solution.py:23
  52.0 0.7 copy-done.2
  52.7 0.9 copy-done.3
  53.6 2.7 %row_partials.1 = (bf16[8,4,16,768]{3,2,1,0:T(8,128)(2,1)}, bf16[4,128,1024]{2,1,0:T(8,128)(2,1)S(1)}) custom-call(s32[2]{0:T(128)S(1)} %pad_add_fusion.place, bf16[128,1024]{1,0:T(8,128)(2,1)S(1)} %bitcast.34, bf16[128,1024]{1,0:T(8,128)(2,1)S(1)} %collective-permute-done.refs_1_, bf16[128,1024]{1,0:T(8,128)(2,1)S(1)} %collective-permute-done.1.refs_2_, ...), custom_call_target="tpu_custom_call" | custom-call | flops 1610612736 | bytes 6291456 | tf_op jit(solution)/shard_map/row_partials/pallas_call | solution.py:62
  56.3 7.5 %all-to-all-start = ((bf16[64,8,768]{2,1,0:T(8,128)(2,1)}), bf16[64,8,768]{2,1,0:T(8,128)(2,1)S(1)}, u32[]{:S(2)}, u32[]{:S(2)}) async-start(bf16[64,8,768]{2,1,0:T(8,128)(2,1)} %bitcast.7), calls=%async_computation | async-start | bytes 1572864 | tf_op jit(solution)/shard_map/all_to_all | solution.py:19
  63.8 1.9 %collective-permute-start.7 = (bf16[4,128,1024]{2,1,0:T(8,128)(2,1)S(1)}, bf16[4,128,1024]{2,1,0:T(8,128)(2,1)S(1)}, u32[]{:S(2)}, u32[]{:S(2)}) collective-permute-start(bf16[4,128,1024]{2,1,0:T(8,128)(2,1)S(1)} %get-tuple-element.5.refs_4_), channel_id=1, source_target_pairs={{0,128},{128,0},{1,129},{129,1},{2,130},{130,2},{3,131},{131,3},{4... | collective-permute-start | bytes 3145736 | tf_op jit(solution)/shard_map/ppermute | solution.py:201
  65.7 1.0 reshape.51
  66.8 5.7 %collective-permute-start.4 = (bf16[256,384]{1,0:T(8,128)(2,1)S(1)}, bf16[256,384]{1,0:T(8,128)(2,1)S(1)}, u32[]{:S(2)}, u32[]{:S(2)}) collective-permute-start(bf16[256,384]{1,0:T(8,128)(2,1)S(1)} %bitcast.27), channel_id=1, source_target_pairs={{0,12},{4,0},{8,4},{12,8},{1,13},{5,1},{9,5},{13,9},{2,14},{6,2},{... | collective-permute-start | bytes 589832 | tf_op jit(solution)/shard_map/ppermute | solution.py:28
  72.5 4.1 %collective-permute-start.5 = (bf16[256,384]{1,0:T(8,128)(2,1)S(1)}, bf16[256,384]{1,0:T(8,128)(2,1)S(1)}, u32[]{:S(2)}, u32[]{:S(2)}) collective-permute-start(bf16[256,384]{1,0:T(8,128)(2,1)S(1)} %bitcast.28), channel_id=1, source_target_pairs={{0,8},{4,12},{8,0},{12,4},{1,9},{5,13},{9,1},{13,5},{2,10},{6,14},... | collective-permute-start | bytes 589832 | tf_op jit(solution)/shard_map/ppermute | solution.py:28
  76.6 4.4 %collective-permute-start.6 = (bf16[256,384]{1,0:T(8,128)(2,1)S(1)}, bf16[256,384]{1,0:T(8,128)(2,1)}, u32[]{:S(2)}, u32[]{:S(2)}) collective-permute-start(bf16[256,384]{1,0:T(8,128)(2,1)S(1)} %bitcast.29), channel_id=1, source_target_pairs={{0,4},{4,8},{8,12},{12,0},{1,5},{5,9},{9,13},{13,1},{2,6},{6,10},{... | collective-permute-start | bytes 589832 | tf_op jit(solution)/shard_map/ppermute | solution.py:28
  81.0 7.1 %all-to-all-done = bf16[64,8,768]{2,1,0:T(8,128)(2,1)S(1)} async-done(((bf16[64,8,768]{2,1,0:T(8,128)(2,1)}), bf16[64,8,768]{2,1,0:T(8,128)(2,1)S(1)}, u32[]{:S(2)}, u32[]{:S(2)}) %all-to-all-start) | async-done | bytes 786464 | tf_op jit(solution)/shard_map/all_to_all | solution.py:19
  88.1 0.8 reduce_rows.1
  88.9 13.2 %all-to-all-start.1 = ((bf16[8,4,768]{2,1,0:T(4,128)(2,1)}), bf16[8,4,768]{2,1,0:T(4,128)(2,1)S(1)}, u32[]{:S(2)}, u32[]{:S(2)}) async-start(bf16[8,4,768]{2,1,0:T(4,128)(2,1)} %reduce_rows.1), calls=%async_computation.1 | async-start | bytes 98304 | tf_op jit(solution)/shard_map/all_to_all | solution.py:19
  102.2 2.9 %weight_gradient.1 = bf16[384,1024]{1,0:T(8,128)(2,1)} custom-call(s32[2]{0:T(128)S(1)} %pad_add_fusion.1.place, bf16[256,384]{1,0:T(8,128)(2,1)S(1)} %bitcast.30, bf16[256,384]{1,0:T(8,128)(2,1)S(1)} %collective-permute-done.4.refs_1_, bf16[256,384]{1,0:T(8,128)(2,1)S(1)} %collective-permute-done.5.refs_2_, ...), custom_call_target="tpu_custom_call" | custom-call | flops 805306368 | bytes 6291456 | tf_op jit(solution)/shard_map/weight_gradient/pallas_call | solution.py:135
  105.2 5.2 %all-to-all-done.1 = bf16[8,4,768]{2,1,0:T(4,128)(2,1)S(1)} async-done(((bf16[8,4,768]{2,1,0:T(4,128)(2,1)}), bf16[8,4,768]{2,1,0:T(4,128)(2,1)S(1)}, u32[]{:S(2)}, u32[]{:S(2)}) %all-to-all-start.1) | async-done | bytes 49184 | tf_op jit(solution)/shard_map/all_to_all | solution.py:19
  110.3 0.7 convolution_convert_fusion.1
  (28 shorter events, 2.2 us)
Async XLA Ops:
  0.6 2.2 %copy-start = (bf16[4,3072]{1,0:T(4,128)(2,1)S(1)}, bf16[4,3072]{1,0:T(4,128)(2,1)}, u32[]{:S(2)}) copy-start(bf16[4,3072]{1,0:T(4,128)(2,1)} %param.5) | copy-start | bytes 73732
  0.6 2.1 %copy-start.5 = (s32[4,2]{0,1:T(2,128)S(1)}, s32[4,2]{0,1:T(2,128)}, u32[]{:S(2)}) copy-start(s32[4,2]{0,1:T(2,128)} %param.6) | copy-start | bytes 100
  0.7 19.5 %copy-start.4 = (bf16[1,128,1024]{2,1,0:T(8,128)(2,1)S(1)}, bf16[1,128,1024]{2,1,0:T(8,128)(2,1)}, u32[]{:S(2)}) copy-start(bf16[1,128,1024]{2,1,0:T(8,128)(2,1)} %param.9) | copy-start | bytes 786436
  0.7 52.0 %collective-permute-start.3 = (bf16[384,1024]{1,0:T(8,128)(2,1)}, bf16[384,1024]{1,0:T(8,128)(2,1)S(1)}, u32[]{:S(2)}, u32[]{:S(2)}) collective-permute-start(bf16[384,1024]{1,0:T(8,128)(2,1)} %bitcast.35), channel_id=1, source_target_pairs={{0,128},{128,0},{1,129},{129,1},{2,130},{130,2},{3,131},{131,3},{4... | collective-permute-start | bytes 2359304 | tf_op jit(solution)/shard_map/ppermute | solution.py:178
  3.7 27.3 %all-to-all-start.2 = ((bf16[16,8,384]{2,1,0:T(8,128)(2,1)}), bf16[16,8,384]{2,1,0:T(8,128)(2,1)S(1)}, u32[]{:S(2)}, u32[]{:S(2)}) async-start(bf16[16,8,384]{2,1,0:T(8,128)(2,1)} %bitcast.13), calls=%async_computation.2 | async-start | bytes 196608 | tf_op jit(solution)/shard_map/all_to_all | solution.py:19
  21.4 31.3 %copy-start.1 = (bf16[1,384,1024]{2,1,0:T(8,128)(2,1)S(1)}, bf16[1,384,1024]{2,1,0:T(8,128)(2,1)}, u32[]{:S(2)}) copy-start(bf16[1,384,1024]{2,1,0:T(8,128)(2,1)} %param.7) | copy-start | bytes 2359300
  21.6 19.1 %collective-permute-start = (bf16[128,1024]{1,0:T(8,128)(2,1)S(1)}, bf16[128,1024]{1,0:T(8,128)(2,1)S(1)}, u32[]{:S(2)}, u32[]{:S(2)}) collective-permute-start(bf16[128,1024]{1,0:T(8,128)(2,1)S(1)} %bitcast.31), channel_id=1, source_target_pairs={{0,256},{256,0},{512,768},{768,512},{1,257},{257,1},{513,769},{769... | collective-permute-start | bytes 786440 | tf_op jit(solution)/shard_map/ppermute | solution.py:23
  23.8 22.6 %collective-permute-start.1 = (bf16[128,1024]{1,0:T(8,128)(2,1)S(1)}, bf16[128,1024]{1,0:T(8,128)(2,1)S(1)}, u32[]{:S(2)}, u32[]{:S(2)}) collective-permute-start(bf16[128,1024]{1,0:T(8,128)(2,1)S(1)} %bitcast.32), channel_id=1, source_target_pairs={{0,512},{256,768},{512,0},{768,256},{1,513},{257,769},{513,1},{769... | collective-permute-start | bytes 786440 | tf_op jit(solution)/shard_map/ppermute | solution.py:23
  28.5 23.5 %collective-permute-start.2 = (bf16[128,1024]{1,0:T(8,128)(2,1)S(1)}, bf16[128,1024]{1,0:T(8,128)(2,1)S(1)}, u32[]{:S(2)}, u32[]{:S(2)}) collective-permute-start(bf16[128,1024]{1,0:T(8,128)(2,1)S(1)} %bitcast.33), channel_id=1, source_target_pairs={{0,768},{256,512},{512,256},{768,0},{1,769},{257,513},{513,257},{7... | collective-permute-start | bytes 786440 | tf_op jit(solution)/shard_map/ppermute | solution.py:23
  31.7 24.7 %all-to-all-start.3 = ((bf16[16,16,384]{2,1,0:T(8,128)(2,1)}), bf16[16,16,384]{2,1,0:T(8,128)(2,1)}, u32[]{:S(2)}, u32[]{:S(2)}) async-start(bf16[16,16,384]{2,1,0:T(8,128)(2,1)} %bitcast.15), calls=%async_computation.3 | async-start | bytes 393216 | tf_op jit(solution)/shard_map/all_to_all | solution.py:19
  52.0 0.7 copy-start.2
  52.7 1.0 copy-start.3
  56.3 31.8 %all-to-all-start = ((bf16[64,8,768]{2,1,0:T(8,128)(2,1)}), bf16[64,8,768]{2,1,0:T(8,128)(2,1)S(1)}, u32[]{:S(2)}, u32[]{:S(2)}) async-start(bf16[64,8,768]{2,1,0:T(8,128)(2,1)} %bitcast.7), calls=%async_computation | async-start | bytes 1572864 | tf_op jit(solution)/shard_map/all_to_all | solution.py:19
  63.8 38.4 %collective-permute-start.7 = (bf16[4,128,1024]{2,1,0:T(8,128)(2,1)S(1)}, bf16[4,128,1024]{2,1,0:T(8,128)(2,1)S(1)}, u32[]{:S(2)}, u32[]{:S(2)}) collective-permute-start(bf16[4,128,1024]{2,1,0:T(8,128)(2,1)S(1)} %get-tuple-element.5.refs_4_), channel_id=1, source_target_pairs={{0,128},{128,0},{1,129},{129,1},{2,130},{130,2},{3,131},{131,3},{4... | collective-permute-start | bytes 3145736 | tf_op jit(solution)/shard_map/ppermute | solution.py:201
  66.8 35.4 %collective-permute-start.4 = (bf16[256,384]{1,0:T(8,128)(2,1)S(1)}, bf16[256,384]{1,0:T(8,128)(2,1)S(1)}, u32[]{:S(2)}, u32[]{:S(2)}) collective-permute-start(bf16[256,384]{1,0:T(8,128)(2,1)S(1)} %bitcast.27), channel_id=1, source_target_pairs={{0,12},{4,0},{8,4},{12,8},{1,13},{5,1},{9,5},{13,9},{2,14},{6,2},{... | collective-permute-start | bytes 589832 | tf_op jit(solution)/shard_map/ppermute | solution.py:28
  72.5 29.7 %collective-permute-start.5 = (bf16[256,384]{1,0:T(8,128)(2,1)S(1)}, bf16[256,384]{1,0:T(8,128)(2,1)S(1)}, u32[]{:S(2)}, u32[]{:S(2)}) collective-permute-start(bf16[256,384]{1,0:T(8,128)(2,1)S(1)} %bitcast.28), channel_id=1, source_target_pairs={{0,8},{4,12},{8,0},{12,4},{1,9},{5,13},{9,1},{13,5},{2,10},{6,14},... | collective-permute-start | bytes 589832 | tf_op jit(solution)/shard_map/ppermute | solution.py:28
  76.6 25.6 %collective-permute-start.6 = (bf16[256,384]{1,0:T(8,128)(2,1)S(1)}, bf16[256,384]{1,0:T(8,128)(2,1)}, u32[]{:S(2)}, u32[]{:S(2)}) collective-permute-start(bf16[256,384]{1,0:T(8,128)(2,1)S(1)} %bitcast.29), channel_id=1, source_target_pairs={{0,4},{4,8},{8,12},{12,0},{1,5},{5,9},{9,13},{13,1},{2,6},{6,10},{... | collective-permute-start | bytes 589832 | tf_op jit(solution)/shard_map/ppermute | solution.py:28
  88.9 21.4 %all-to-all-start.1 = ((bf16[8,4,768]{2,1,0:T(4,128)(2,1)}), bf16[8,4,768]{2,1,0:T(4,128)(2,1)S(1)}, u32[]{:S(2)}, u32[]{:S(2)}) async-start(bf16[8,4,768]{2,1,0:T(4,128)(2,1)} %reduce_rows.1), calls=%async_computation.1 | async-start | bytes 98304 | tf_op jit(solution)/shard_map/all_to_all | solution.py:19

commit v6 on v5

--- a/solution.py
+++ b/solution.py
@@ -37,17 +37,29 @@
 
 
 def row_partials(chip_rows, weight, other_weight):
-    chips = len(chip_rows)
+    chips = lax.axis_size("xl")
     rows, hidden = chip_rows[0].shape
     shard = weight.shape[0]
     ys = lax.axis_size("yh") * lax.axis_size("yl")
     inner = rows // ys
 
     def kernel(place, *refs):
-        row_refs, (weight_ref, other_ref, out_ref, stack_ref) = refs[:chips], refs[chips:]
+        own, near, opposite, across, forwarded = refs[:5]
+        weight_ref, other_ref, out_ref, stack_ref = refs[5:]
         chip, core = place[0], place[1]
-        for k in range(chips):
-            stack_ref[chip ^ k] = row_refs[k][...]
+        middle = jnp.logical_and(chip > 0, chip < chips - 1)
+        stack_ref[chip] = own[...]
+        stack_ref[chip ^ 1] = near[...]
+        stack_ref[chip ^ 3] = opposite[...]
+
+        @pl.when(middle)
+        def _():
+            stack_ref[chip ^ 2] = across[...]
+
+        @pl.when(jnp.logical_not(middle))
+        def _():
+            stack_ref[chip ^ 2] = forwarded[...]
+
         blocks = stack_ref[...].reshape(chips * rows, hidden)
         for side, ref in ((core, weight_ref), (1 - core, other_ref)):
             part = lax.dot_general(
@@ -65,7 +77,7 @@
             jax.ShapeDtypeStruct((ys, chips, inner, 2 * shard), jnp.bfloat16),
             jax.ShapeDtypeStruct((chips, rows, hidden), jnp.bfloat16),
         ),
-        in_specs=[SMEM] + [VMEM] * (chips + 2),
+        in_specs=[SMEM] + [VMEM] * (len(chip_rows) + 2),
         out_specs=(VMEM,) * 2,
         compiler_params=pltpu.CompilerParams(vmem_limit_bytes=VMEM_BYTES),
         cost_estimate=pl.CostEstimate(
@@ -159,7 +171,10 @@
     grad_up = derive(hidden_grad[0], gate_pre[0])
     grad_up = grad_up.reshape(experts, ys, halves, hidden).transpose(1, 2, 0, 3)
     grad_up = grad_up.reshape(rows, hidden)
-    far, farther, near = (flip(grad_up, "xl", k) for k in (2, 3, 1))
+    opposite = flip(grad_up, "xl", 3)
+    across = lax.ppermute(grad_up, "xl", [(0, 2), (3, 1)])
+    near = flip(grad_up, "xl", 1)
+    forwarded = lax.ppermute(opposite, "xl", [(2, 3), (1, 0)])
 
     picks = jnp.any(
         routes[:, :, None] == jnp.arange(experts, dtype=jnp.int32)[None, None, :], axis=1
@@ -186,7 +201,7 @@
     arrived = arrived.reshape(twins * rows, shard)
 
     partial, chip_rows = row_partials(
-        (grad_up, near, far, farther), weight, other_weight
+        (grad_up, near, opposite, across, forwarded), weight, other_weight
     )
     partial = exchange(
         partial.reshape(ys * chips * halves, experts, cores * shard), ("yh", "yl", "xl", "h")
@@ -197,7 +212,8 @@
         "te,eqc->tqc", picks, returned, preferred_element_type=jnp.float32
     ).astype(jnp.bfloat16)
 
-    pieces = [arrived] + [shift(arrived, "yh", -away) for away in range(1, pairs)]
+    facing = shift(arrived, "yh", pairs // 2)
+    pieces = [arrived, shift(arrived, "yh", -1), facing, shift(arrived, "yh", 1)]
     other_chip_rows = lax.ppermute(chip_rows, "core", CORE_SWAP)
     weight_grad = weight_gradient(pieces, chip_rows, other_chip_rows)
     return grad_tokens.reshape(token_count, width), weight_grad[None]

time: 112 us -> 109 us (0.973)
  the two profiles are of different devices: /device:TPU:2 before, /device:TPU:1 now
where the time goes in v6:
time: 109 us; the launch traced here: 108 us
  starting transfers between devices  72 us (66%)
  waiting for transfers between devices  20.6 us (19%)
  Pallas kernels  6.47 us (6%)
  local copies, waits for them, and re-layouts  6.03 us (6%)
  other arithmetic  1.42 us (1%)
    all_to_all x4, starting transfers between devices, exchange(): return lax.all_to_all(blocks, axes, split_axis=0, concat_axis=0, tiled=True)  28.5 us
    ppermute x1, starting transfers between devices, on_device(): other_weight = lax.ppermute(weight, 'core', CORE_SWAP)  16.1 us
    ppermute x3, starting transfers between devices, shift(): lax.ppermute(value, axis, [(i, (i + by) % size) for i in range(size)])  13.4 us
    ppermute x3, waiting for transfers between devices, shift(): lax.ppermute(value, axis, [(i, (i + by) % size) for i in range(size)])  11.8 us
    all_to_all x4, waiting for transfers between devices, exchange(): return lax.all_to_all(blocks, axes, split_axis=0, concat_axis=0, tiled=True)  8.78 us
    ppermute x2, starting transfers between devices, flip(): lax.ppermute(value, axis, [(i, i ^ bits) for i in range(lax.axis_size(axi...  5.33 us
    ppermute x1, starting transfers between devices, on_device(): across = lax.ppermute(grad_up, 'xl', [(0, 2), (3, 1)])  4.01 us
    ppermute x1, starting transfers between devices, on_device(): other_chip_rows = lax.ppermute(chip_rows, 'core', CORE_SWAP)  3.41 us
  transfers between devices with their start and end apart: 13, of which 5 were waited for; matrix products, arithmetic and copies ran while one was open for 4% of the time, Pallas kernels for 6%

profile of v6, /device:TPU:1, one launch (start us, length us, event | category | flops | bytes accessed | tf_op | source)
XLA Modules:
  0.0 108.3 jit_solution(8396578085906280038)
XLA Ops:
  0.6 16.1 %collective-permute-start.4 = (bf16[384,1024]{1,0:T(8,128)(2,1)}, bf16[384,1024]{1,0:T(8,128)(2,1)S(1)}, u32[]{:S(2)}, u32[]{:S(2)}) collective-permute-start(bf16[384,1024]{1,0:T(8,128)(2,1)} %bitcast.35), channel_id=1, source_target_pairs={{0,128},{128,0},{1,129},{129,1},{2,130},{130,2},{3,131},{131,3},{4... | collective-permute-start | bytes 2359304 | tf_op jit(solution)/shard_map/ppermute | solution.py:193
  16.7 1.2 %fusion.2 = bf16[1,128,1024]{2,1,0:T(8,128)(2,1)S(1)} fusion(bf16[1,128,1024]{2,1,0:T(8,128)(2,1)} %param.9, bf16[1,128,1024]{2,1,0:T(8,128)(2,1)} %param.8), kind=kLoop, calls=%fused_computation.6 | loop fusion | flops 1048576 | bytes 786432 | tf_op jit(solution)/shard_map/convert_element_type | solution.py:15
  18.2 2.1 %collective-permute-start.1 = (bf16[128,1024]{1,0:T(8,128)(2,1)S(1)}, bf16[128,1024]{1,0:T(8,128)(2,1)S(1)}, u32[]{:S(2)}, u32[]{:S(2)}) collective-permute-start(bf16[128,1024]{1,0:T(8,128)(2,1)S(1)} %bitcast.31), channel_id=1, source_target_pairs={{0,768},{256,512},{512,256},{768,0},{1,769},{257,513},{513,257},{7... | collective-permute-start | bytes 786440 | tf_op jit(solution)/shard_map/ppermute | solution.py:23
  21.2 5.1 %all-to-all-start.2 = ((bf16[16,8,384]{2,1,0:T(8,128)(2,1)}), bf16[16,8,384]{2,1,0:T(8,128)(2,1)S(1)}, u32[]{:S(2)}, u32[]{:S(2)}) async-start(bf16[16,8,384]{2,1,0:T(8,128)(2,1)} %bitcast.13), calls=%async_computation.2 | async-start | bytes 196608 | tf_op jit(solution)/shard_map/all_to_all | solution.py:19
  26.3 3.3 %collective-permute-start = (bf16[128,1024]{1,0:T(8,128)(2,1)S(1)}, bf16[128,1024]{1,0:T(8,128)(2,1)S(1)}, u32[]{:S(2)}, u32[]{:S(2)}) collective-permute-start(bf16[128,1024]{1,0:T(8,128)(2,1)S(1)} %bitcast.32), channel_id=1, source_target_pairs={{0,256},{256,0},{512,768},{768,512},{1,257},{257,1},{513,769},{769... | collective-permute-start | bytes 786440 | tf_op jit(solution)/shard_map/ppermute | solution.py:23
  29.6 4.0 %collective-permute-start.2 = (bf16[128,1024]{1,0:T(8,128)(2,1)S(1)}, bf16[128,1024]{1,0:T(8,128)(2,1)S(1)}, u32[]{:S(2)}, u32[]{:S(2)}) collective-permute-start(bf16[128,1024]{1,0:T(8,128)(2,1)S(1)} %bitcast.33), channel_id=1, source_target_pairs={{0,512},{768,256},{1,513},{769,257},{2,514},{770,258},{3,515},{771... | collective-permute-start | bytes 786440 | tf_op jit(solution)/shard_map/ppermute | solution.py:175
  33.6 1.3 %collective-permute-start.3 = (bf16[128,1024]{1,0:T(8,128)(2,1)S(1)}, bf16[128,1024]{1,0:T(8,128)(2,1)S(1)}, u32[]{:S(2)}, u32[]{:S(2)}) collective-permute-start(bf16[128,1024]{1,0:T(8,128)(2,1)S(1)} %collective-permute-done.1.refs_2_), channel_id=1, source_target_pairs={{512,768},{256,0},{513,769},{257,1},{514,770},{258,2},{515,771},{2... | collective-permute-start | bytes 786440 | tf_op jit(solution)/shard_map/ppermute | solution.py:177
  35.7 9.5 %all-to-all-start.3 = ((bf16[16,16,384]{2,1,0:T(8,128)(2,1)}), bf16[16,16,384]{2,1,0:T(8,128)(2,1)}, u32[]{:S(2)}, u32[]{:S(2)}) async-start(bf16[16,16,384]{2,1,0:T(8,128)(2,1)} %bitcast.15), calls=%async_computation.3 | async-start | bytes 393216 | tf_op jit(solution)/shard_map/all_to_all | solution.py:19
  46.7 0.9 copy-done.3
  47.6 0.9 copy-done.5
  48.6 2.8 %row_partials.1 = (bf16[8,4,16,768]{3,2,1,0:T(8,128)(2,1)}, bf16[4,128,1024]{2,1,0:T(8,128)(2,1)S(1)}) custom-call(s32[2]{0:T(128)S(1)} %pad_add_fusion.place, bf16[128,1024]{1,0:T(8,128)(2,1)S(1)} %bitcast.34, bf16[128,1024]{1,0:T(8,128)(2,1)S(1)} %collective-permute-done.refs_1_, bf16[128,1024]{1,0:T(8,128)(2,1)S(1)} %collective-permute-done.1.refs_2_, ...), custom_call_target="tpu_custom_call" | custom-call | flops 1610612736 | bytes 6291456 | tf_op jit(solution)/shard_map/row_partials/pallas_call | solution.py:74
  51.3 2.5 %all-to-all-done.3 = bf16[16,16,384]{2,1,0:T(8,128)(2,1)} async-done(((bf16[16,16,384]{2,1,0:T(8,128)(2,1)}), bf16[16,16,384]{2,1,0:T(8,128)(2,1)}, u32[]{:S(2)}, u32[]{:S(2)}) %all-to-all-start.3) | async-done | bytes 196640 | tf_op jit(solution)/shard_map/all_to_all | solution.py:19
  53.9 10.6 %all-to-all-start = ((bf16[64,8,768]{2,1,0:T(8,128)(2,1)}), bf16[64,8,768]{2,1,0:T(8,128)(2,1)S(1)}, u32[]{:S(2)}, u32[]{:S(2)}) async-start(bf16[64,8,768]{2,1,0:T(8,128)(2,1)} %bitcast.7), calls=%async_computation | async-start | bytes 1572864 | tf_op jit(solution)/shard_map/all_to_all | solution.py:19
  64.4 3.4 %collective-permute-start.8 = (bf16[4,128,1024]{2,1,0:T(8,128)(2,1)S(1)}, bf16[4,128,1024]{2,1,0:T(8,128)(2,1)S(1)}, u32[]{:S(2)}, u32[]{:S(2)}) collective-permute-start(bf16[4,128,1024]{2,1,0:T(8,128)(2,1)S(1)} %get-tuple-element.5.refs_4_), channel_id=1, source_target_pairs={{0,128},{128,0},{1,129},{129,1},{2,130},{130,2},{3,131},{131,3},{4... | collective-permute-start | bytes 3145736 | tf_op jit(solution)/shard_map/ppermute | solution.py:217
  67.8 1.0 reshape.51
  68.9 5.5 %collective-permute-start.5 = (bf16[256,384]{1,0:T(8,128)(2,1)S(1)}, bf16[256,384]{1,0:T(8,128)(2,1)S(1)}, u32[]{:S(2)}, u32[]{:S(2)}) collective-permute-start(bf16[256,384]{1,0:T(8,128)(2,1)S(1)} %bitcast.27), channel_id=1, source_target_pairs={{0,12},{4,0},{8,4},{12,8},{1,13},{5,1},{9,5},{13,9},{2,14},{6,2},{... | collective-permute-start | bytes 589832 | tf_op jit(solution)/shard_map/ppermute | solution.py:28
  74.4 3.8 %collective-permute-start.6 = (bf16[256,384]{1,0:T(8,128)(2,1)S(1)}, bf16[256,384]{1,0:T(8,128)(2,1)S(1)}, u32[]{:S(2)}, u32[]{:S(2)}) collective-permute-start(bf16[256,384]{1,0:T(8,128)(2,1)S(1)} %bitcast.28), channel_id=1, source_target_pairs={{0,8},{4,12},{8,0},{12,4},{1,9},{5,13},{9,1},{13,5},{2,10},{6,14},... | collective-permute-start | bytes 589832 | tf_op jit(solution)/shard_map/ppermute | solution.py:28
  78.2 4.1 %collective-permute-start.7 = (bf16[256,384]{1,0:T(8,128)(2,1)S(1)}, bf16[256,384]{1,0:T(8,128)(2,1)}, u32[]{:S(2)}, u32[]{:S(2)}) collective-permute-start(bf16[256,384]{1,0:T(8,128)(2,1)S(1)} %bitcast.29), channel_id=1, source_target_pairs={{0,4},{4,8},{8,12},{12,0},{1,5},{5,9},{9,13},{13,1},{2,6},{6,10},{... | collective-permute-start | bytes 589832 | tf_op jit(solution)/shard_map/ppermute | solution.py:28
  82.3 6.2 %all-to-all-done = bf16[64,8,768]{2,1,0:T(8,128)(2,1)S(1)} async-done(((bf16[64,8,768]{2,1,0:T(8,128)(2,1)}), bf16[64,8,768]{2,1,0:T(8,128)(2,1)S(1)}, u32[]{:S(2)}, u32[]{:S(2)}) %all-to-all-start) | async-done | bytes 786464 | tf_op jit(solution)/shard_map/all_to_all | solution.py:19
  89.4 3.3 %all-to-all-start.1 = ((bf16[8,4,768]{2,1,0:T(4,128)(2,1)}), bf16[8,4,768]{2,1,0:T(4,128)(2,1)S(1)}, u32[]{:S(2)}, u32[]{:S(2)}) async-start(bf16[8,4,768]{2,1,0:T(4,128)(2,1)} %reduce_rows.1), calls=%async_computation.1 | async-start | bytes 98304 | tf_op jit(solution)/shard_map/all_to_all | solution.py:19
  92.8 2.6 %collective-permute-done.5.refs_1_ = bf16[256,384]{1,0:T(8,128)(2,1)S(1)} collective-permute-done((bf16[256,384]{1,0:T(8,128)(2,1)S(1)}, bf16[256,384]{1,0:T(8,128)(2,1)S(1)}, u32[]{:S(2)}, u32[]{:S(2)}) %collective-permute-start.5) | collective-permute-done | bytes 196640 | tf_op jit(solution)/shard_map/ppermute | solution.py:28
  95.4 4.8 %collective-permute-done.6.refs_2_ = bf16[256,384]{1,0:T(8,128)(2,1)S(1)} collective-permute-done((bf16[256,384]{1,0:T(8,128)(2,1)S(1)}, bf16[256,384]{1,0:T(8,128)(2,1)S(1)}, u32[]{:S(2)}, u32[]{:S(2)}) %collective-permute-start.6) | collective-permute-done | bytes 196640 | tf_op jit(solution)/shard_map/ppermute | solution.py:28
  100.2 4.4 %collective-permute-done.7.refs_3_ = bf16[256,384]{1,0:T(8,128)(2,1)} collective-permute-done((bf16[256,384]{1,0:T(8,128)(2,1)S(1)}, bf16[256,384]{1,0:T(8,128)(2,1)}, u32[]{:S(2)}, u32[]{:S(2)}) %collective-permute-start.7) | collective-permute-done | bytes 196640 | tf_op jit(solution)/shard_map/ppermute | solution.py:28
  104.6 2.9 %weight_gradient.1 = bf16[384,1024]{1,0:T(8,128)(2,1)} custom-call(s32[2]{0:T(128)S(1)} %pad_add_fusion.1.place, bf16[256,384]{1,0:T(8,128)(2,1)S(1)} %bitcast.30, bf16[256,384]{1,0:T(8,128)(2,1)S(1)} %collective-permute-done.5.refs_1_, bf16[256,384]{1,0:T(8,128)(2,1)S(1)} %collective-permute-done.6.refs_2_, ...), custom_call_target="tpu_custom_call" | custom-call | flops 805306368 | bytes 6291456 | tf_op jit(solution)/shard_map/weight_gradient/pallas_call | solution.py:147
  (32 shorter events, 5.1 us)
Async XLA Ops:
  0.6 19.7 %copy-start = (bf16[4,3072]{1,0:T(4,128)(2,1)S(1)}, bf16[4,3072]{1,0:T(4,128)(2,1)}, u32[]{:S(2)}) copy-start(bf16[4,3072]{1,0:T(4,128)(2,1)} %param.5) | copy-start | bytes 73732
  0.6 46.0 %collective-permute-start.4 = (bf16[384,1024]{1,0:T(8,128)(2,1)}, bf16[384,1024]{1,0:T(8,128)(2,1)S(1)}, u32[]{:S(2)}, u32[]{:S(2)}) collective-permute-start(bf16[384,1024]{1,0:T(8,128)(2,1)} %bitcast.35), channel_id=1, source_target_pairs={{0,128},{128,0},{1,129},{129,1},{2,130},{130,2},{3,131},{131,3},{4... | collective-permute-start | bytes 2359304 | tf_op jit(solution)/shard_map/ppermute | solution.py:193
  18.0 2.2 %copy-start.6 = (s32[4,2]{0,1:T(2,128)S(1)}, s32[4,2]{0,1:T(2,128)}, u32[]{:S(2)}) copy-start(s32[4,2]{0,1:T(2,128)} %param.6) | copy-start | bytes 100
  18.2 28.5 %copy-start.1 = (bf16[1,384,1024]{2,1,0:T(8,128)(2,1)S(1)}, bf16[1,384,1024]{2,1,0:T(8,128)(2,1)}, u32[]{:S(2)}) copy-start(bf16[1,384,1024]{2,1,0:T(8,128)(2,1)} %param.7) | copy-start | bytes 2359300
  18.2 15.4 %collective-permute-start.1 = (bf16[128,1024]{1,0:T(8,128)(2,1)S(1)}, bf16[128,1024]{1,0:T(8,128)(2,1)S(1)}, u32[]{:S(2)}, u32[]{:S(2)}) collective-permute-start(bf16[128,1024]{1,0:T(8,128)(2,1)S(1)} %bitcast.31), channel_id=1, source_target_pairs={{0,768},{256,512},{512,256},{768,0},{1,769},{257,513},{513,257},{7... | collective-permute-start | bytes 786440 | tf_op jit(solution)/shard_map/ppermute | solution.py:23
  21.2 13.7 %all-to-all-start.2 = ((bf16[16,8,384]{2,1,0:T(8,128)(2,1)}), bf16[16,8,384]{2,1,0:T(8,128)(2,1)S(1)}, u32[]{:S(2)}, u32[]{:S(2)}) async-start(bf16[16,8,384]{2,1,0:T(8,128)(2,1)} %bitcast.13), calls=%async_computation.2 | async-start | bytes 196608 | tf_op jit(solution)/shard_map/all_to_all | solution.py:19
  26.3 18.9 %collective-permute-start = (bf16[128,1024]{1,0:T(8,128)(2,1)S(1)}, bf16[128,1024]{1,0:T(8,128)(2,1)S(1)}, u32[]{:S(2)}, u32[]{:S(2)}) collective-permute-start(bf16[128,1024]{1,0:T(8,128)(2,1)S(1)} %bitcast.32), channel_id=1, source_target_pairs={{0,256},{256,0},{512,768},{768,512},{1,257},{257,1},{513,769},{769... | collective-permute-start | bytes 786440 | tf_op jit(solution)/shard_map/ppermute | solution.py:23
  29.6 15.6 %collective-permute-start.2 = (bf16[128,1024]{1,0:T(8,128)(2,1)S(1)}, bf16[128,1024]{1,0:T(8,128)(2,1)S(1)}, u32[]{:S(2)}, u32[]{:S(2)}) collective-permute-start(bf16[128,1024]{1,0:T(8,128)(2,1)S(1)} %bitcast.33), channel_id=1, source_target_pairs={{0,512},{768,256},{1,513},{769,257},{2,514},{770,258},{3,515},{771... | collective-permute-start | bytes 786440 | tf_op jit(solution)/shard_map/ppermute | solution.py:175
  33.6 12.3 %collective-permute-start.3 = (bf16[128,1024]{1,0:T(8,128)(2,1)S(1)}, bf16[128,1024]{1,0:T(8,128)(2,1)S(1)}, u32[]{:S(2)}, u32[]{:S(2)}) collective-permute-start(bf16[128,1024]{1,0:T(8,128)(2,1)S(1)} %collective-permute-done.1.refs_2_), channel_id=1, source_target_pairs={{512,768},{256,0},{513,769},{257,1},{514,770},{258,2},{515,771},{2... | collective-permute-start | bytes 786440 | tf_op jit(solution)/shard_map/ppermute | solution.py:177
  35.7 18.2 %all-to-all-start.3 = ((bf16[16,16,384]{2,1,0:T(8,128)(2,1)}), bf16[16,16,384]{2,1,0:T(8,128)(2,1)}, u32[]{:S(2)}, u32[]{:S(2)}) async-start(bf16[16,16,384]{2,1,0:T(8,128)(2,1)} %bitcast.15), calls=%async_computation.3 | async-start | bytes 393216 | tf_op jit(solution)/shard_map/all_to_all | solution.py:19
  45.2 0.7 copy-start.2
  46.0 0.7 copy-start.4
  46.7 1.0 copy-start.3
  47.6 0.9 copy-start.5
  53.9 34.7 %all-to-all-start = ((bf16[64,8,768]{2,1,0:T(8,128)(2,1)}), bf16[64,8,768]{2,1,0:T(8,128)(2,1)S(1)}, u32[]{:S(2)}, u32[]{:S(2)}) async-start(bf16[64,8,768]{2,1,0:T(8,128)(2,1)} %bitcast.7), calls=%async_computation | async-start | bytes 1572864 | tf_op jit(solution)/shard_map/all_to_all | solution.py:19
  64.4 40.2 %collective-permute-start.8 = (bf16[4,128,1024]{2,1,0:T(8,128)(2,1)S(1)}, bf16[4,128,1024]{2,1,0:T(8,128)(2,1)S(1)}, u32[]{:S(2)}, u32[]{:S(2)}) collective-permute-start(bf16[4,128,1024]{2,1,0:T(8,128)(2,1)S(1)} %get-tuple-element.5.refs_4_), channel_id=1, source_target_pairs={{0,128},{128,0},{1,129},{129,1},{2,130},{130,2},{3,131},{131,3},{4... | collective-permute-start | bytes 3145736 | tf_op jit(solution)/shard_map/ppermute | solution.py:217
  68.9 26.5 %collective-permute-start.5 = (bf16[256,384]{1,0:T(8,128)(2,1)S(1)}, bf16[256,384]{1,0:T(8,128)(2,1)S(1)}, u32[]{:S(2)}, u32[]{:S(2)}) collective-permute-start(bf16[256,384]{1,0:T(8,128)(2,1)S(1)} %bitcast.27), channel_id=1, source_target_pairs={{0,12},{4,0},{8,4},{12,8},{1,13},{5,1},{9,5},{13,9},{2,14},{6,2},{... | collective-permute-start | bytes 589832 | tf_op jit(solution)/shard_map/ppermute | solution.py:28
  74.4 25.8 %collective-permute-start.6 = (bf16[256,384]{1,0:T(8,128)(2,1)S(1)}, bf16[256,384]{1,0:T(8,128)(2,1)S(1)}, u32[]{:S(2)}, u32[]{:S(2)}) collective-permute-start(bf16[256,384]{1,0:T(8,128)(2,1)S(1)} %bitcast.28), channel_id=1, source_target_pairs={{0,8},{4,12},{8,0},{12,4},{1,9},{5,13},{9,1},{13,5},{2,10},{6,14},... | collective-permute-start | bytes 589832 | tf_op jit(solution)/shard_map/ppermute | solution.py:28
  78.2 26.4 %collective-permute-start.7 = (bf16[256,384]{1,0:T(8,128)(2,1)S(1)}, bf16[256,384]{1,0:T(8,128)(2,1)}, u32[]{:S(2)}, u32[]{:S(2)}) collective-permute-start(bf16[256,384]{1,0:T(8,128)(2,1)S(1)} %bitcast.29), channel_id=1, source_target_pairs={{0,4},{4,8},{8,12},{12,0},{1,5},{5,9},{9,13},{13,1},{2,6},{6,10},{... | collective-permute-start | bytes 589832 | tf_op jit(solution)/shard_map/ppermute | solution.py:28
  89.4 18.2 %all-to-all-start.1 = ((bf16[8,4,768]{2,1,0:T(4,128)(2,1)}), bf16[8,4,768]{2,1,0:T(4,128)(2,1)S(1)}, u32[]{:S(2)}, u32[]{:S(2)}) async-start(bf16[8,4,768]{2,1,0:T(4,128)(2,1)} %reduce_rows.1), calls=%async_computation.1 | async-start | bytes 98304 | tf_op jit(solution)/shard_map/all_to_all | solution.py:19

commit v7 on v6

--- a/solution.py
+++ b/solution.py
@@ -212,8 +212,10 @@
         "te,eqc->tqc", picks, returned, preferred_element_type=jnp.float32
     ).astype(jnp.bfloat16)
 
-    facing = shift(arrived, "yh", pairs // 2)
-    pieces = [arrived, shift(arrived, "yh", -1), facing, shift(arrived, "yh", 1)]
+    pieces = [arrived]
+    for _ in range(pairs // 2):
+        pieces.append(shift(pieces[-1], "yh", -1))
+    pieces.append(shift(arrived, "yh", 1))
     other_chip_rows = lax.ppermute(chip_rows, "core", CORE_SWAP)
     weight_grad = weight_gradient(pieces, chip_rows, other_chip_rows)
     return grad_tokens.reshape(token_count, width), weight_grad[None]

time: 109 us -> 112 us (1.028)
  waiting for transfers between devices: 20.6 us -> 26.4 us
  starting transfers between devices: 72 us -> 69.3 us
    ppermute x3, waiting for transfers between devices: 11.8 us -> 23.8 us  [shift(): lax.ppermute(value, axis, [(i, (i + by) % size) for i in range(size)])]
    all_to_all x4, waiting for transfers between devices: 8.78 us -> 2.54 us  [exchange(): return lax.all_to_all(blocks, axes, split_axis=0, concat_axis=0, tiled=True)]
    ppermute x3, starting transfers between devices: 13.4 us -> 10.7 us  [shift(): lax.ppermute(value, axis, [(i, (i + by) % size) for i in range(size)])]
  transfers between devices with their start and end apart: 13 -> 13, of which waited for: 5 -> 3; matrix products, arithmetic and copies ran while one was open for 4% -> 4% of each run, Pallas kernels for 6% -> 6%
where the time goes in v7:
time: 112 us; the launch traced here: 111 us
  starting transfers between devices  69.3 us (62%)
  waiting for transfers between devices  26.4 us (24%)
  Pallas kernels  6.48 us (6%)
  local copies, waits for them, and re-layouts  6.03 us (5%)
  other arithmetic  1.42 us (1%)
    all_to_all x4, starting transfers between devices, exchange(): return lax.all_to_all(blocks, axes, split_axis=0, concat_axis=0, tiled=True)  28.5 us
    ppermute x3, waiting for transfers between devices, shift(): lax.ppermute(value, axis, [(i, (i + by) % size) for i in range(size)])  23.8 us
    ppermute x1, starting transfers between devices, on_device(): other_weight = lax.ppermute(weight, 'core', CORE_SWAP)  16.1 us
    ppermute x3, starting transfers between devices, shift(): lax.ppermute(value, axis, [(i, (i + by) % size) for i in range(size)])  10.7 us
    ppermute x2, starting transfers between devices, flip(): lax.ppermute(value, axis, [(i, i ^ bits) for i in range(lax.axis_size(axi...  5.33 us
    ppermute x1, starting transfers between devices, on_device(): across = lax.ppermute(grad_up, 'xl', [(0, 2), (3, 1)])  4.01 us
    ppermute x1, starting transfers between devices, on_device(): other_chip_rows = lax.ppermute(chip_rows, 'core', CORE_SWAP)  3.41 us
    unnamed x14, local copies, waits for them, and re-layouts  3.32 us
  transfers between devices with their start and end apart: 13, of which 3 were waited for; matrix products, arithmetic and copies ran while one was open for 4% of the time, Pallas kernels for 6%

profile of v7, /device:TPU:1, one launch (start us, length us, event | category | flops | bytes accessed | tf_op | source)
XLA Modules:
  0.0 111.4 jit_solution(125128174315384043)
XLA Ops:
  0.6 16.1 %collective-permute-start.4 = (bf16[384,1024]{1,0:T(8,128)(2,1)}, bf16[384,1024]{1,0:T(8,128)(2,1)S(1)}, u32[]{:S(2)}, u32[]{:S(2)}) collective-permute-start(bf16[384,1024]{1,0:T(8,128)(2,1)} %bitcast.34), channel_id=1, source_target_pairs={{0,128},{128,0},{1,129},{129,1},{2,130},{130,2},{3,131},{131,3},{4... | collective-permute-start | bytes 2359304 | tf_op jit(solution)/shard_map/ppermute | solution.py:193
  16.7 1.2 %fusion.2 = bf16[1,128,1024]{2,1,0:T(8,128)(2,1)S(1)} fusion(bf16[1,128,1024]{2,1,0:T(8,128)(2,1)} %param.9, bf16[1,128,1024]{2,1,0:T(8,128)(2,1)} %param.8), kind=kLoop, calls=%fused_computation.6 | loop fusion | flops 1048576 | bytes 786432 | tf_op jit(solution)/shard_map/convert_element_type | solution.py:15
  18.2 2.1 %collective-permute-start.1 = (bf16[128,1024]{1,0:T(8,128)(2,1)S(1)}, bf16[128,1024]{1,0:T(8,128)(2,1)S(1)}, u32[]{:S(2)}, u32[]{:S(2)}) collective-permute-start(bf16[128,1024]{1,0:T(8,128)(2,1)S(1)} %bitcast.30), channel_id=1, source_target_pairs={{0,768},{256,512},{512,256},{768,0},{1,769},{257,513},{513,257},{7... | collective-permute-start | bytes 786440 | tf_op jit(solution)/shard_map/ppermute | solution.py:23
  21.2 5.1 %all-to-all-start.2 = ((bf16[16,8,384]{2,1,0:T(8,128)(2,1)}), bf16[16,8,384]{2,1,0:T(8,128)(2,1)S(1)}, u32[]{:S(2)}, u32[]{:S(2)}) async-start(bf16[16,8,384]{2,1,0:T(8,128)(2,1)} %bitcast.13), calls=%async_computation.2 | async-start | bytes 196608 | tf_op jit(solution)/shard_map/all_to_all | solution.py:19
  26.3 3.3 %collective-permute-start = (bf16[128,1024]{1,0:T(8,128)(2,1)S(1)}, bf16[128,1024]{1,0:T(8,128)(2,1)S(1)}, u32[]{:S(2)}, u32[]{:S(2)}) collective-permute-start(bf16[128,1024]{1,0:T(8,128)(2,1)S(1)} %bitcast.31), channel_id=1, source_target_pairs={{0,256},{256,0},{512,768},{768,512},{1,257},{257,1},{513,769},{769... | collective-permute-start | bytes 786440 | tf_op jit(solution)/shard_map/ppermute | solution.py:23
  29.6 4.0 %collective-permute-start.2 = (bf16[128,1024]{1,0:T(8,128)(2,1)S(1)}, bf16[128,1024]{1,0:T(8,128)(2,1)S(1)}, u32[]{:S(2)}, u32[]{:S(2)}) collective-permute-start(bf16[128,1024]{1,0:T(8,128)(2,1)S(1)} %bitcast.32), channel_id=1, source_target_pairs={{0,512},{768,256},{1,513},{769,257},{2,514},{770,258},{3,515},{771... | collective-permute-start | bytes 786440 | tf_op jit(solution)/shard_map/ppermute | solution.py:175
  33.6 1.3 %collective-permute-start.3 = (bf16[128,1024]{1,0:T(8,128)(2,1)S(1)}, bf16[128,1024]{1,0:T(8,128)(2,1)S(1)}, u32[]{:S(2)}, u32[]{:S(2)}) collective-permute-start(bf16[128,1024]{1,0:T(8,128)(2,1)S(1)} %collective-permute-done.1.refs_2_), channel_id=1, source_target_pairs={{512,768},{256,0},{513,769},{257,1},{514,770},{258,2},{515,771},{2... | collective-permute-start | bytes 786440 | tf_op jit(solution)/shard_map/ppermute | solution.py:177
  35.7 9.5 %all-to-all-start.3 = ((bf16[16,16,384]{2,1,0:T(8,128)(2,1)}), bf16[16,16,384]{2,1,0:T(8,128)(2,1)}, u32[]{:S(2)}, u32[]{:S(2)}) async-start(bf16[16,16,384]{2,1,0:T(8,128)(2,1)} %bitcast.15), calls=%async_computation.3 | async-start | bytes 393216 | tf_op jit(solution)/shard_map/all_to_all | solution.py:19
  46.7 0.9 copy-done.3
  47.6 0.9 copy-done.5
  48.6 2.8 %row_partials.1 = (bf16[8,4,16,768]{3,2,1,0:T(8,128)(2,1)}, bf16[4,128,1024]{2,1,0:T(8,128)(2,1)S(1)}) custom-call(s32[2]{0:T(128)S(1)} %pad_add_fusion.place, bf16[128,1024]{1,0:T(8,128)(2,1)S(1)} %bitcast.33, bf16[128,1024]{1,0:T(8,128)(2,1)S(1)} %collective-permute-done.refs_1_, bf16[128,1024]{1,0:T(8,128)(2,1)S(1)} %collective-permute-done.1.refs_2_, ...), custom_call_target="tpu_custom_call" | custom-call | flops 1610612736 | bytes 6291456 | tf_op jit(solution)/shard_map/row_partials/pallas_call | solution.py:74
  51.3 2.5 %all-to-all-done.3 = bf16[16,16,384]{2,1,0:T(8,128)(2,1)} async-done(((bf16[16,16,384]{2,1,0:T(8,128)(2,1)}), bf16[16,16,384]{2,1,0:T(8,128)(2,1)}, u32[]{:S(2)}, u32[]{:S(2)}) %all-to-all-start.3) | async-done | bytes 196640 | tf_op jit(solution)/shard_map/all_to_all | solution.py:19
  53.9 10.6 %all-to-all-start = ((bf16[64,8,768]{2,1,0:T(8,128)(2,1)}), bf16[64,8,768]{2,1,0:T(8,128)(2,1)S(1)}, u32[]{:S(2)}, u32[]{:S(2)}) async-start(bf16[64,8,768]{2,1,0:T(8,128)(2,1)} %bitcast.7), calls=%async_computation | async-start | bytes 1572864 | tf_op jit(solution)/shard_map/all_to_all | solution.py:19
  64.4 3.4 %collective-permute-start.8 = (bf16[4,128,1024]{2,1,0:T(8,128)(2,1)S(1)}, bf16[4,128,1024]{2,1,0:T(8,128)(2,1)S(1)}, u32[]{:S(2)}, u32[]{:S(2)}) collective-permute-start(bf16[4,128,1024]{2,1,0:T(8,128)(2,1)S(1)} %get-tuple-element.5.refs_4_), channel_id=1, source_target_pairs={{0,128},{128,0},{1,129},{129,1},{2,130},{130,2},{3,131},{131,3},{4... | collective-permute-start | bytes 3145736 | tf_op jit(solution)/shard_map/ppermute | solution.py:219
  67.8 1.0 reshape.51
  68.9 5.5 %collective-permute-start.5 = (bf16[256,384]{1,0:T(8,128)(2,1)S(1)}, bf16[256,384]{1,0:T(8,128)(2,1)S(1)}, u32[]{:S(2)}, u32[]{:S(2)}) collective-permute-start(bf16[256,384]{1,0:T(8,128)(2,1)S(1)} %bitcast.27), channel_id=1, source_target_pairs={{0,12},{4,0},{8,4},{12,8},{1,13},{5,1},{9,5},{13,9},{2,14},{6,2},{... | collective-permute-start | bytes 589832 | tf_op jit(solution)/shard_map/ppermute | solution.py:28
  74.4 1.9 %collective-permute-start.7 = (bf16[256,384]{1,0:T(8,128)(2,1)S(1)}, bf16[256,384]{1,0:T(8,128)(2,1)S(1)}, u32[]{:S(2)}, u32[]{:S(2)}) collective-permute-start(bf16[256,384]{1,0:T(8,128)(2,1)S(1)} %bitcast.28), channel_id=1, source_target_pairs={{0,4},{4,8},{8,12},{12,0},{1,5},{5,9},{9,13},{13,1},{2,6},{6,10},{... | collective-permute-start | bytes 589832 | tf_op jit(solution)/shard_map/ppermute | solution.py:28
  76.4 18.0 %collective-permute-done.5.refs_1_ = bf16[256,384]{1,0:T(8,128)(2,1)S(1)} collective-permute-done((bf16[256,384]{1,0:T(8,128)(2,1)S(1)}, bf16[256,384]{1,0:T(8,128)(2,1)S(1)}, u32[]{:S(2)}, u32[]{:S(2)}) %collective-permute-start.5) | collective-permute-done | bytes 196640 | tf_op jit(solution)/shard_map/ppermute | solution.py:28
  94.3 3.3 %collective-permute-start.6 = (bf16[256,384]{1,0:T(8,128)(2,1)S(1)}, bf16[256,384]{1,0:T(8,128)(2,1)}, u32[]{:S(2)}, u32[]{:S(2)}) collective-permute-start(bf16[256,384]{1,0:T(8,128)(2,1)S(1)} %collective-permute-done.5.refs_1_), channel_id=1, source_target_pairs={{0,12},{4,0},{8,4},{12,8},{1,13},{5,1},{9,5},{13,9},{2,14},{6,2},{... | collective-permute-start | bytes 589832 | tf_op jit(solution)/shard_map/ppermute | solution.py:28
  97.6 0.8 reduce_rows.1
  98.4 3.3 %all-to-all-start.1 = ((bf16[8,4,768]{2,1,0:T(4,128)(2,1)}), bf16[8,4,768]{2,1,0:T(4,128)(2,1)S(1)}, u32[]{:S(2)}, u32[]{:S(2)}) async-start(bf16[8,4,768]{2,1,0:T(4,128)(2,1)} %reduce_rows.1), calls=%async_computation.1 | async-start | bytes 98304 | tf_op jit(solution)/shard_map/all_to_all | solution.py:19
  101.8 5.8 %collective-permute-done.6.refs_2_ = bf16[256,384]{1,0:T(8,128)(2,1)} collective-permute-done((bf16[256,384]{1,0:T(8,128)(2,1)S(1)}, bf16[256,384]{1,0:T(8,128)(2,1)}, u32[]{:S(2)}, u32[]{:S(2)}) %collective-permute-start.6) | collective-permute-done | bytes 196640 | tf_op jit(solution)/shard_map/ppermute | solution.py:28
  107.7 2.9 %weight_gradient.1 = bf16[384,1024]{1,0:T(8,128)(2,1)} custom-call(s32[2]{0:T(128)S(1)} %pad_add_fusion.1.place, bf16[256,384]{1,0:T(8,128)(2,1)S(1)} %bitcast.29, bf16[256,384]{1,0:T(8,128)(2,1)S(1)} %collective-permute-done.5.refs_1_, bf16[256,384]{1,0:T(8,128)(2,1)} %collective-permute-done.6.refs_2_, ...), custom_call_target="tpu_custom_call" | custom-call | flops 805306368 | bytes 6291456 | tf_op jit(solution)/shard_map/weight_gradient/pallas_call | solution.py:147
  110.6 0.7 convolution_convert_fusion.1
  (32 shorter events, 3.6 us)
Async XLA Ops:
  0.6 19.7 %copy-start = (bf16[4,3072]{1,0:T(4,128)(2,1)S(1)}, bf16[4,3072]{1,0:T(4,128)(2,1)}, u32[]{:S(2)}) copy-start(bf16[4,3072]{1,0:T(4,128)(2,1)} %param.5) | copy-start | bytes 73732
  0.6 46.0 %collective-permute-start.4 = (bf16[384,1024]{1,0:T(8,128)(2,1)}, bf16[384,1024]{1,0:T(8,128)(2,1)S(1)}, u32[]{:S(2)}, u32[]{:S(2)}) collective-permute-start(bf16[384,1024]{1,0:T(8,128)(2,1)} %bitcast.34), channel_id=1, source_target_pairs={{0,128},{128,0},{1,129},{129,1},{2,130},{130,2},{3,131},{131,3},{4... | collective-permute-start | bytes 2359304 | tf_op jit(solution)/shard_map/ppermute | solution.py:193
  18.0 2.2 %copy-start.6 = (s32[4,2]{0,1:T(2,128)S(1)}, s32[4,2]{0,1:T(2,128)}, u32[]{:S(2)}) copy-start(s32[4,2]{0,1:T(2,128)} %param.6) | copy-start | bytes 100
  18.2 28.5 %copy-start.1 = (bf16[1,384,1024]{2,1,0:T(8,128)(2,1)S(1)}, bf16[1,384,1024]{2,1,0:T(8,128)(2,1)}, u32[]{:S(2)}) copy-start(bf16[1,384,1024]{2,1,0:T(8,128)(2,1)} %param.7) | copy-start | bytes 2359300
  18.2 15.4 %collective-permute-start.1 = (bf16[128,1024]{1,0:T(8,128)(2,1)S(1)}, bf16[128,1024]{1,0:T(8,128)(2,1)S(1)}, u32[]{:S(2)}, u32[]{:S(2)}) collective-permute-start(bf16[128,1024]{1,0:T(8,128)(2,1)S(1)} %bitcast.30), channel_id=1, source_target_pairs={{0,768},{256,512},{512,256},{768,0},{1,769},{257,513},{513,257},{7... | collective-permute-start | bytes 786440 | tf_op jit(solution)/shard_map/ppermute | solution.py:23
  21.2 13.7 %all-to-all-start.2 = ((bf16[16,8,384]{2,1,0:T(8,128)(2,1)}), bf16[16,8,384]{2,1,0:T(8,128)(2,1)S(1)}, u32[]{:S(2)}, u32[]{:S(2)}) async-start(bf16[16,8,384]{2,1,0:T(8,128)(2,1)} %bitcast.13), calls=%async_computation.2 | async-start | bytes 196608 | tf_op jit(solution)/shard_map/all_to_all | solution.py:19
  26.3 18.9 %collective-permute-start = (bf16[128,1024]{1,0:T(8,128)(2,1)S(1)}, bf16[128,1024]{1,0:T(8,128)(2,1)S(1)}, u32[]{:S(2)}, u32[]{:S(2)}) collective-permute-start(bf16[128,1024]{1,0:T(8,128)(2,1)S(1)} %bitcast.31), channel_id=1, source_target_pairs={{0,256},{256,0},{512,768},{768,512},{1,257},{257,1},{513,769},{769... | collective-permute-start | bytes 786440 | tf_op jit(solution)/shard_map/ppermute | solution.py:23
  29.6 15.6 %collective-permute-start.2 = (bf16[128,1024]{1,0:T(8,128)(2,1)S(1)}, bf16[128,1024]{1,0:T(8,128)(2,1)S(1)}, u32[]{:S(2)}, u32[]{:S(2)}) collective-permute-start(bf16[128,1024]{1,0:T(8,128)(2,1)S(1)} %bitcast.32), channel_id=1, source_target_pairs={{0,512},{768,256},{1,513},{769,257},{2,514},{770,258},{3,515},{771... | collective-permute-start | bytes 786440 | tf_op jit(solution)/shard_map/ppermute | solution.py:175
  33.6 12.3 %collective-permute-start.3 = (bf16[128,1024]{1,0:T(8,128)(2,1)S(1)}, bf16[128,1024]{1,0:T(8,128)(2,1)S(1)}, u32[]{:S(2)}, u32[]{:S(2)}) collective-permute-start(bf16[128,1024]{1,0:T(8,128)(2,1)S(1)} %collective-permute-done.1.refs_2_), channel_id=1, source_target_pairs={{512,768},{256,0},{513,769},{257,1},{514,770},{258,2},{515,771},{2... | collective-permute-start | bytes 786440 | tf_op jit(solution)/shard_map/ppermute | solution.py:177
  35.7 18.2 %all-to-all-start.3 = ((bf16[16,16,384]{2,1,0:T(8,128)(2,1)}), bf16[16,16,384]{2,1,0:T(8,128)(2,1)}, u32[]{:S(2)}, u32[]{:S(2)}) async-start(bf16[16,16,384]{2,1,0:T(8,128)(2,1)} %bitcast.15), calls=%async_computation.3 | async-start | bytes 393216 | tf_op jit(solution)/shard_map/all_to_all | solution.py:19
  45.2 0.7 copy-start.2
  46.0 0.7 copy-start.4
  46.7 1.0 copy-start.3
  47.6 0.9 copy-start.5
  53.9 43.8 %all-to-all-start = ((bf16[64,8,768]{2,1,0:T(8,128)(2,1)}), bf16[64,8,768]{2,1,0:T(8,128)(2,1)S(1)}, u32[]{:S(2)}, u32[]{:S(2)}) async-start(bf16[64,8,768]{2,1,0:T(8,128)(2,1)} %bitcast.7), calls=%async_computation | async-start | bytes 1572864 | tf_op jit(solution)/shard_map/all_to_all | solution.py:19
  64.4 43.3 %collective-permute-start.8 = (bf16[4,128,1024]{2,1,0:T(8,128)(2,1)S(1)}, bf16[4,128,1024]{2,1,0:T(8,128)(2,1)S(1)}, u32[]{:S(2)}, u32[]{:S(2)}) collective-permute-start(bf16[4,128,1024]{2,1,0:T(8,128)(2,1)S(1)} %get-tuple-element.5.refs_4_), channel_id=1, source_target_pairs={{0,128},{128,0},{1,129},{129,1},{2,130},{130,2},{3,131},{131,3},{4... | collective-permute-start | bytes 3145736 | tf_op jit(solution)/shard_map/ppermute | solution.py:219
  68.9 25.4 %collective-permute-start.5 = (bf16[256,384]{1,0:T(8,128)(2,1)S(1)}, bf16[256,384]{1,0:T(8,128)(2,1)S(1)}, u32[]{:S(2)}, u32[]{:S(2)}) collective-permute-start(bf16[256,384]{1,0:T(8,128)(2,1)S(1)} %bitcast.27), channel_id=1, source_target_pairs={{0,12},{4,0},{8,4},{12,8},{1,13},{5,1},{9,5},{13,9},{2,14},{6,2},{... | collective-permute-start | bytes 589832 | tf_op jit(solution)/shard_map/ppermute | solution.py:28
  74.4 27.4 %collective-permute-start.7 = (bf16[256,384]{1,0:T(8,128)(2,1)S(1)}, bf16[256,384]{1,0:T(8,128)(2,1)S(1)}, u32[]{:S(2)}, u32[]{:S(2)}) collective-permute-start(bf16[256,384]{1,0:T(8,128)(2,1)S(1)} %bitcast.28), channel_id=1, source_target_pairs={{0,4},{4,8},{8,12},{12,0},{1,5},{5,9},{9,13},{13,1},{2,6},{6,10},{... | collective-permute-start | bytes 589832 | tf_op jit(solution)/shard_map/ppermute | solution.py:28
  94.3 13.3 %collective-permute-start.6 = (bf16[256,384]{1,0:T(8,128)(2,1)S(1)}, bf16[256,384]{1,0:T(8,128)(2,1)}, u32[]{:S(2)}, u32[]{:S(2)}) collective-permute-start(bf16[256,384]{1,0:T(8,128)(2,1)S(1)} %collective-permute-done.5.refs_1_), channel_id=1, source_target_pairs={{0,12},{4,0},{8,4},{12,8},{1,13},{5,1},{9,5},{13,9},{2,14},{6,2},{... | collective-permute-start | bytes 589832 | tf_op jit(solution)/shard_map/ppermute | solution.py:28
  98.4 12.2 %all-to-all-start.1 = ((bf16[8,4,768]{2,1,0:T(4,128)(2,1)}), bf16[8,4,768]{2,1,0:T(4,128)(2,1)S(1)}, u32[]{:S(2)}, u32[]{:S(2)}) async-start(bf16[8,4,768]{2,1,0:T(4,128)(2,1)} %reduce_rows.1), calls=%async_computation.1 | async-start | bytes 98304 | tf_op jit(solution)/shard_map/all_to_all | solution.py:19

commit v8 on v6

--- a/solution.py
+++ b/solution.py
@@ -116,7 +116,7 @@
     )(partials)
 
 
-def weight_gradient(pieces, chip_rows, other_rows):
+def weight_gradient(pieces, aways, chip_rows, other_rows):
     chips, rows, hidden = chip_rows.shape
     twins, shard = pieces[0].shape[0] // rows, pieces[0].shape[1]
     ys = len(pieces) * twins
@@ -125,7 +125,7 @@
     def kernel(place, *refs):
         piece_refs, (own_ref, other_ref, out_ref, layer) = refs[: len(pieces)], refs[len(pieces) :]
         core, pair = place[0], place[1]
-        for away, ref in enumerate(piece_refs):
+        for away, ref in zip(aways, piece_refs):
             for twin in range(twins):
                 y = ((pair + away) & (len(pieces) - 1)) * twins + twin
                 for chip in range(chips):
@@ -212,10 +212,10 @@
         "te,eqc->tqc", picks, returned, preferred_element_type=jnp.float32
     ).astype(jnp.bfloat16)
 
-    facing = shift(arrived, "yh", pairs // 2)
-    pieces = [arrived, shift(arrived, "yh", -1), facing, shift(arrived, "yh", 1)]
+    aways = (0, pairs // 2, pairs - 1, 1)
+    pieces = [arrived] + [shift(arrived, "yh", -away) for away in aways[1:]]
     other_chip_rows = lax.ppermute(chip_rows, "core", CORE_SWAP)
-    weight_grad = weight_gradient(pieces, chip_rows, other_chip_rows)
+    weight_grad = weight_gradient(pieces, aways, chip_rows, other_chip_rows)
     return grad_tokens.reshape(token_count, width), weight_grad[None]
 
 

time: 109 us -> 108 us (level)
  waiting for transfers between devices: 20.6 us -> 18.3 us
  starting transfers between devices: 72 us -> 73.2 us
    ppermute x3, waiting for transfers between devices: 11.8 us -> 10.5 us  [shift(): lax.ppermute(value, axis, [(i, (i + by) % size) for i in range(size)])]
    ppermute x3, starting transfers between devices: 13.4 us -> 14.6 us  [shift(): lax.ppermute(value, axis, [(i, (i + by) % size) for i in range(size)])]
  transfers between devices with their start and end apart: 13 -> 13, of which waited for: 5 -> 4; matrix products, arithmetic and copies ran while one was open for 4% -> 4% of each run, Pallas kernels for 6% -> 6%
where the time goes in v8:
time: 108 us; the launch traced here: 107 us
  starting transfers between devices  73.2 us (68%)
  waiting for transfers between devices  18.3 us (17%)
  Pallas kernels  6.48 us (6%)
  local copies, waits for them, and re-layouts  6.03 us (6%)
  other arithmetic  1.42 us (1%)
    all_to_all x4, starting transfers between devices, exchange(): return lax.all_to_all(blocks, axes, split_axis=0, concat_axis=0, tiled=True)  28.5 us
    ppermute x1, starting transfers between devices, on_device(): other_weight = lax.ppermute(weight, 'core', CORE_SWAP)  16.1 us
    ppermute x3, starting transfers between devices, shift(): lax.ppermute(value, axis, [(i, (i + by) % size) for i in range(size)])  14.6 us
    ppermute x3, waiting for transfers between devices, shift(): lax.ppermute(value, axis, [(i, (i + by) % size) for i in range(size)])  10.5 us
    all_to_all x4, waiting for transfers between devices, exchange(): return lax.all_to_all(blocks, axes, split_axis=0, concat_axis=0, tiled=True)  7.81 us
    ppermute x2, starting transfers between devices, flip(): lax.ppermute(value, axis, [(i, i ^ bits) for i in range(lax.axis_size(axi...  5.33 us
    ppermute x1, starting transfers between devices, on_device(): across = lax.ppermute(grad_up, 'xl', [(0, 2), (3, 1)])  4.01 us
    ppermute x1, starting transfers between devices, on_device(): other_chip_rows = lax.ppermute(chip_rows, 'core', CORE_SWAP)  3.41 us
  transfers between devices with their start and end apart: 13, of which 4 were waited for; matrix products, arithmetic and copies ran while one was open for 4% of the time, Pallas kernels for 6%

profile of v8, /device:TPU:1, one launch (start us, length us, event | category | flops | bytes accessed | tf_op | source)
XLA Modules:
  0.0 107.2 jit_solution(5973551350237786527)
XLA Ops:
  0.6 16.1 %collective-permute-start.4 = (bf16[384,1024]{1,0:T(8,128)(2,1)}, bf16[384,1024]{1,0:T(8,128)(2,1)S(1)}, u32[]{:S(2)}, u32[]{:S(2)}) collective-permute-start(bf16[384,1024]{1,0:T(8,128)(2,1)} %bitcast.35), channel_id=1, source_target_pairs={{0,128},{128,0},{1,129},{129,1},{2,130},{130,2},{3,131},{131,3},{4... | collective-permute-start | bytes 2359304 | tf_op jit(solution)/shard_map/ppermute | solution.py:193
  16.7 1.2 %fusion.2 = bf16[1,128,1024]{2,1,0:T(8,128)(2,1)S(1)} fusion(bf16[1,128,1024]{2,1,0:T(8,128)(2,1)} %param.9, bf16[1,128,1024]{2,1,0:T(8,128)(2,1)} %param.8), kind=kLoop, calls=%fused_computation.6 | loop fusion | flops 1048576 | bytes 786432 | tf_op jit(solution)/shard_map/convert_element_type | solution.py:15
  18.2 2.1 %collective-permute-start.1 = (bf16[128,1024]{1,0:T(8,128)(2,1)S(1)}, bf16[128,1024]{1,0:T(8,128)(2,1)S(1)}, u32[]{:S(2)}, u32[]{:S(2)}) collective-permute-start(bf16[128,1024]{1,0:T(8,128)(2,1)S(1)} %bitcast.31), channel_id=1, source_target_pairs={{0,768},{256,512},{512,256},{768,0},{1,769},{257,513},{513,257},{7... | collective-permute-start | bytes 786440 | tf_op jit(solution)/shard_map/ppermute | solution.py:23
  21.2 5.1 %all-to-all-start.2 = ((bf16[16,8,384]{2,1,0:T(8,128)(2,1)}), bf16[16,8,384]{2,1,0:T(8,128)(2,1)S(1)}, u32[]{:S(2)}, u32[]{:S(2)}) async-start(bf16[16,8,384]{2,1,0:T(8,128)(2,1)} %bitcast.13), calls=%async_computation.2 | async-start | bytes 196608 | tf_op jit(solution)/shard_map/all_to_all | solution.py:19
  26.3 3.3 %collective-permute-start = (bf16[128,1024]{1,0:T(8,128)(2,1)S(1)}, bf16[128,1024]{1,0:T(8,128)(2,1)S(1)}, u32[]{:S(2)}, u32[]{:S(2)}) collective-permute-start(bf16[128,1024]{1,0:T(8,128)(2,1)S(1)} %bitcast.32), channel_id=1, source_target_pairs={{0,256},{256,0},{512,768},{768,512},{1,257},{257,1},{513,769},{769... | collective-permute-start | bytes 786440 | tf_op jit(solution)/shard_map/ppermute | solution.py:23
  29.6 4.0 %collective-permute-start.2 = (bf16[128,1024]{1,0:T(8,128)(2,1)S(1)}, bf16[128,1024]{1,0:T(8,128)(2,1)S(1)}, u32[]{:S(2)}, u32[]{:S(2)}) collective-permute-start(bf16[128,1024]{1,0:T(8,128)(2,1)S(1)} %bitcast.33), channel_id=1, source_target_pairs={{0,512},{768,256},{1,513},{769,257},{2,514},{770,258},{3,515},{771... | collective-permute-start | bytes 786440 | tf_op jit(solution)/shard_map/ppermute | solution.py:175
  33.6 1.3 %collective-permute-start.3 = (bf16[128,1024]{1,0:T(8,128)(2,1)S(1)}, bf16[128,1024]{1,0:T(8,128)(2,1)S(1)}, u32[]{:S(2)}, u32[]{:S(2)}) collective-permute-start(bf16[128,1024]{1,0:T(8,128)(2,1)S(1)} %collective-permute-done.1.refs_2_), channel_id=1, source_target_pairs={{512,768},{256,0},{513,769},{257,1},{514,770},{258,2},{515,771},{2... | collective-permute-start | bytes 786440 | tf_op jit(solution)/shard_map/ppermute | solution.py:177
  35.7 9.5 %all-to-all-start.3 = ((bf16[16,16,384]{2,1,0:T(8,128)(2,1)}), bf16[16,16,384]{2,1,0:T(8,128)(2,1)}, u32[]{:S(2)}, u32[]{:S(2)}) async-start(bf16[16,16,384]{2,1,0:T(8,128)(2,1)} %bitcast.15), calls=%async_computation.3 | async-start | bytes 393216 | tf_op jit(solution)/shard_map/all_to_all | solution.py:19
  46.7 0.9 copy-done.3
  47.6 0.9 copy-done.5
  48.6 2.8 %row_partials.1 = (bf16[8,4,16,768]{3,2,1,0:T(8,128)(2,1)}, bf16[4,128,1024]{2,1,0:T(8,128)(2,1)S(1)}) custom-call(s32[2]{0:T(128)S(1)} %pad_add_fusion.place, bf16[128,1024]{1,0:T(8,128)(2,1)S(1)} %bitcast.34, bf16[128,1024]{1,0:T(8,128)(2,1)S(1)} %collective-permute-done.refs_1_, bf16[128,1024]{1,0:T(8,128)(2,1)S(1)} %collective-permute-done.1.refs_2_, ...), custom_call_target="tpu_custom_call" | custom-call | flops 1610612736 | bytes 6291456 | tf_op jit(solution)/shard_map/row_partials/pallas_call | solution.py:74
  51.3 2.5 %all-to-all-done.3 = bf16[16,16,384]{2,1,0:T(8,128)(2,1)} async-done(((bf16[16,16,384]{2,1,0:T(8,128)(2,1)}), bf16[16,16,384]{2,1,0:T(8,128)(2,1)}, u32[]{:S(2)}, u32[]{:S(2)}) %all-to-all-start.3) | async-done | bytes 196640 | tf_op jit(solution)/shard_map/all_to_all | solution.py:19
  53.9 10.6 %all-to-all-start = ((bf16[64,8,768]{2,1,0:T(8,128)(2,1)}), bf16[64,8,768]{2,1,0:T(8,128)(2,1)S(1)}, u32[]{:S(2)}, u32[]{:S(2)}) async-start(bf16[64,8,768]{2,1,0:T(8,128)(2,1)} %bitcast.7), calls=%async_computation | async-start | bytes 1572864 | tf_op jit(solution)/shard_map/all_to_all | solution.py:19
  64.4 3.4 %collective-permute-start.8 = (bf16[4,128,1024]{2,1,0:T(8,128)(2,1)S(1)}, bf16[4,128,1024]{2,1,0:T(8,128)(2,1)S(1)}, u32[]{:S(2)}, u32[]{:S(2)}) collective-permute-start(bf16[4,128,1024]{2,1,0:T(8,128)(2,1)S(1)} %get-tuple-element.5.refs_4_), channel_id=1, source_target_pairs={{0,128},{128,0},{1,129},{129,1},{2,130},{130,2},{3,131},{131,3},{4... | collective-permute-start | bytes 3145736 | tf_op jit(solution)/shard_map/ppermute | solution.py:217
  67.8 1.0 reshape.51
  68.9 7.2 %collective-permute-start.5 = (bf16[256,384]{1,0:T(8,128)(2,1)S(1)}, bf16[256,384]{1,0:T(8,128)(2,1)S(1)}, u32[]{:S(2)}, u32[]{:S(2)}) collective-permute-start(bf16[256,384]{1,0:T(8,128)(2,1)S(1)} %bitcast.27), channel_id=1, source_target_pairs={{0,8},{4,12},{8,0},{12,4},{1,9},{5,13},{9,1},{13,5},{2,10},{6,14},... | collective-permute-start | bytes 589832 | tf_op jit(solution)/shard_map/ppermute | solution.py:28
  76.1 2.3 %collective-permute-start.6 = (bf16[256,384]{1,0:T(8,128)(2,1)S(1)}, bf16[256,384]{1,0:T(8,128)(2,1)S(1)}, u32[]{:S(2)}, u32[]{:S(2)}) collective-permute-start(bf16[256,384]{1,0:T(8,128)(2,1)S(1)} %bitcast.28), channel_id=1, source_target_pairs={{0,4},{4,8},{8,12},{12,0},{1,5},{5,9},{9,13},{13,1},{2,6},{6,10},{... | collective-permute-start | bytes 589832 | tf_op jit(solution)/shard_map/ppermute | solution.py:28
  78.4 5.1 %collective-permute-start.7 = (bf16[256,384]{1,0:T(8,128)(2,1)S(1)}, bf16[256,384]{1,0:T(8,128)(2,1)}, u32[]{:S(2)}, u32[]{:S(2)}) collective-permute-start(bf16[256,384]{1,0:T(8,128)(2,1)S(1)} %bitcast.29), channel_id=1, source_target_pairs={{0,12},{4,0},{8,4},{12,8},{1,13},{5,1},{9,5},{13,9},{2,14},{6,2},{... | collective-permute-start | bytes 589832 | tf_op jit(solution)/shard_map/ppermute | solution.py:28
  83.5 5.3 %all-to-all-done = bf16[64,8,768]{2,1,0:T(8,128)(2,1)S(1)} async-done(((bf16[64,8,768]{2,1,0:T(8,128)(2,1)}), bf16[64,8,768]{2,1,0:T(8,128)(2,1)S(1)}, u32[]{:S(2)}, u32[]{:S(2)}) %all-to-all-start) | async-done | bytes 786464 | tf_op jit(solution)/shard_map/all_to_all | solution.py:19
  88.8 0.8 reduce_rows.1
  89.6 3.3 %all-to-all-start.1 = ((bf16[8,4,768]{2,1,0:T(4,128)(2,1)}), bf16[8,4,768]{2,1,0:T(4,128)(2,1)S(1)}, u32[]{:S(2)}, u32[]{:S(2)}) async-start(bf16[8,4,768]{2,1,0:T(4,128)(2,1)} %reduce_rows.1), calls=%async_computation.1 | async-start | bytes 98304 | tf_op jit(solution)/shard_map/all_to_all | solution.py:19
  93.0 4.5 %collective-permute-done.5.refs_1_ = bf16[256,384]{1,0:T(8,128)(2,1)S(1)} collective-permute-done((bf16[256,384]{1,0:T(8,128)(2,1)S(1)}, bf16[256,384]{1,0:T(8,128)(2,1)S(1)}, u32[]{:S(2)}, u32[]{:S(2)}) %collective-permute-start.5) | collective-permute-done | bytes 196640 | tf_op jit(solution)/shard_map/ppermute | solution.py:28
  97.5 6.0 %collective-permute-done.6.refs_2_ = bf16[256,384]{1,0:T(8,128)(2,1)S(1)} collective-permute-done((bf16[256,384]{1,0:T(8,128)(2,1)S(1)}, bf16[256,384]{1,0:T(8,128)(2,1)S(1)}, u32[]{:S(2)}, u32[]{:S(2)}) %collective-permute-start.6) | collective-permute-done | bytes 196640 | tf_op jit(solution)/shard_map/ppermute | solution.py:28
  103.5 2.9 %weight_gradient.1 = bf16[384,1024]{1,0:T(8,128)(2,1)} custom-call(s32[2]{0:T(128)S(1)} %pad_add_fusion.1.place, bf16[256,384]{1,0:T(8,128)(2,1)S(1)} %bitcast.30, bf16[256,384]{1,0:T(8,128)(2,1)S(1)} %collective-permute-done.5.refs_1_, bf16[256,384]{1,0:T(8,128)(2,1)S(1)} %collective-permute-done.6.refs_2_, ...), custom_call_target="tpu_custom_call" | custom-call | flops 805306368 | bytes 6291456 | tf_op jit(solution)/shard_map/weight_gradient/pallas_call | solution.py:147
  (32 shorter events, 4.3 us)
Async XLA Ops:
  0.6 19.7 %copy-start = (bf16[4,3072]{1,0:T(4,128)(2,1)S(1)}, bf16[4,3072]{1,0:T(4,128)(2,1)}, u32[]{:S(2)}) copy-start(bf16[4,3072]{1,0:T(4,128)(2,1)} %param.5) | copy-start | bytes 73732
  0.6 46.0 %collective-permute-start.4 = (bf16[384,1024]{1,0:T(8,128)(2,1)}, bf16[384,1024]{1,0:T(8,128)(2,1)S(1)}, u32[]{:S(2)}, u32[]{:S(2)}) collective-permute-start(bf16[384,1024]{1,0:T(8,128)(2,1)} %bitcast.35), channel_id=1, source_target_pairs={{0,128},{128,0},{1,129},{129,1},{2,130},{130,2},{3,131},{131,3},{4... | collective-permute-start | bytes 2359304 | tf_op jit(solution)/shard_map/ppermute | solution.py:193
  18.0 2.2 %copy-start.6 = (s32[4,2]{0,1:T(2,128)S(1)}, s32[4,2]{0,1:T(2,128)}, u32[]{:S(2)}) copy-start(s32[4,2]{0,1:T(2,128)} %param.6) | copy-start | bytes 100
  18.2 28.5 %copy-start.1 = (bf16[1,384,1024]{2,1,0:T(8,128)(2,1)S(1)}, bf16[1,384,1024]{2,1,0:T(8,128)(2,1)}, u32[]{:S(2)}) copy-start(bf16[1,384,1024]{2,1,0:T(8,128)(2,1)} %param.7) | copy-start | bytes 2359300
  18.2 15.4 %collective-permute-start.1 = (bf16[128,1024]{1,0:T(8,128)(2,1)S(1)}, bf16[128,1024]{1,0:T(8,128)(2,1)S(1)}, u32[]{:S(2)}, u32[]{:S(2)}) collective-permute-start(bf16[128,1024]{1,0:T(8,128)(2,1)S(1)} %bitcast.31), channel_id=1, source_target_pairs={{0,768},{256,512},{512,256},{768,0},{1,769},{257,513},{513,257},{7... | collective-permute-start | bytes 786440 | tf_op jit(solution)/shard_map/ppermute | solution.py:23
  21.2 13.7 %all-to-all-start.2 = ((bf16[16,8,384]{2,1,0:T(8,128)(2,1)}), bf16[16,8,384]{2,1,0:T(8,128)(2,1)S(1)}, u32[]{:S(2)}, u32[]{:S(2)}) async-start(bf16[16,8,384]{2,1,0:T(8,128)(2,1)} %bitcast.13), calls=%async_computation.2 | async-start | bytes 196608 | tf_op jit(solution)/shard_map/all_to_all | solution.py:19
  26.3 18.9 %collective-permute-start = (bf16[128,1024]{1,0:T(8,128)(2,1)S(1)}, bf16[128,1024]{1,0:T(8,128)(2,1)S(1)}, u32[]{:S(2)}, u32[]{:S(2)}) collective-permute-start(bf16[128,1024]{1,0:T(8,128)(2,1)S(1)} %bitcast.32), channel_id=1, source_target_pairs={{0,256},{256,0},{512,768},{768,512},{1,257},{257,1},{513,769},{769... | collective-permute-start | bytes 786440 | tf_op jit(solution)/shard_map/ppermute | solution.py:23
  29.6 15.6 %collective-permute-start.2 = (bf16[128,1024]{1,0:T(8,128)(2,1)S(1)}, bf16[128,1024]{1,0:T(8,128)(2,1)S(1)}, u32[]{:S(2)}, u32[]{:S(2)}) collective-permute-start(bf16[128,1024]{1,0:T(8,128)(2,1)S(1)} %bitcast.33), channel_id=1, source_target_pairs={{0,512},{768,256},{1,513},{769,257},{2,514},{770,258},{3,515},{771... | collective-permute-start | bytes 786440 | tf_op jit(solution)/shard_map/ppermute | solution.py:175
  33.6 12.3 %collective-permute-start.3 = (bf16[128,1024]{1,0:T(8,128)(2,1)S(1)}, bf16[128,1024]{1,0:T(8,128)(2,1)S(1)}, u32[]{:S(2)}, u32[]{:S(2)}) collective-permute-start(bf16[128,1024]{1,0:T(8,128)(2,1)S(1)} %collective-permute-done.1.refs_2_), channel_id=1, source_target_pairs={{512,768},{256,0},{513,769},{257,1},{514,770},{258,2},{515,771},{2... | collective-permute-start | bytes 786440 | tf_op jit(solution)/shard_map/ppermute | solution.py:177
  35.7 18.2 %all-to-all-start.3 = ((bf16[16,16,384]{2,1,0:T(8,128)(2,1)}), bf16[16,16,384]{2,1,0:T(8,128)(2,1)}, u32[]{:S(2)}, u32[]{:S(2)}) async-start(bf16[16,16,384]{2,1,0:T(8,128)(2,1)} %bitcast.15), calls=%async_computation.3 | async-start | bytes 393216 | tf_op jit(solution)/shard_map/all_to_all | solution.py:19
  45.2 0.7 copy-start.2
  46.0 0.7 copy-start.4
  46.7 1.0 copy-start.3
  47.6 0.9 copy-start.5
  53.9 35.0 %all-to-all-start = ((bf16[64,8,768]{2,1,0:T(8,128)(2,1)}), bf16[64,8,768]{2,1,0:T(8,128)(2,1)S(1)}, u32[]{:S(2)}, u32[]{:S(2)}) async-start(bf16[64,8,768]{2,1,0:T(8,128)(2,1)} %bitcast.7), calls=%async_computation | async-start | bytes 1572864 | tf_op jit(solution)/shard_map/all_to_all | solution.py:19
  64.4 39.1 %collective-permute-start.8 = (bf16[4,128,1024]{2,1,0:T(8,128)(2,1)S(1)}, bf16[4,128,1024]{2,1,0:T(8,128)(2,1)S(1)}, u32[]{:S(2)}, u32[]{:S(2)}) collective-permute-start(bf16[4,128,1024]{2,1,0:T(8,128)(2,1)S(1)} %get-tuple-element.5.refs_4_), channel_id=1, source_target_pairs={{0,128},{128,0},{1,129},{129,1},{2,130},{130,2},{3,131},{131,3},{4... | collective-permute-start | bytes 3145736 | tf_op jit(solution)/shard_map/ppermute | solution.py:217
  68.9 28.6 %collective-permute-start.5 = (bf16[256,384]{1,0:T(8,128)(2,1)S(1)}, bf16[256,384]{1,0:T(8,128)(2,1)S(1)}, u32[]{:S(2)}, u32[]{:S(2)}) collective-permute-start(bf16[256,384]{1,0:T(8,128)(2,1)S(1)} %bitcast.27), channel_id=1, source_target_pairs={{0,8},{4,12},{8,0},{12,4},{1,9},{5,13},{9,1},{13,5},{2,10},{6,14},... | collective-permute-start | bytes 589832 | tf_op jit(solution)/shard_map/ppermute | solution.py:28
  76.1 27.4 %collective-permute-start.6 = (bf16[256,384]{1,0:T(8,128)(2,1)S(1)}, bf16[256,384]{1,0:T(8,128)(2,1)S(1)}, u32[]{:S(2)}, u32[]{:S(2)}) collective-permute-start(bf16[256,384]{1,0:T(8,128)(2,1)S(1)} %bitcast.28), channel_id=1, source_target_pairs={{0,4},{4,8},{8,12},{12,0},{1,5},{5,9},{9,13},{13,1},{2,6},{6,10},{... | collective-permute-start | bytes 589832 | tf_op jit(solution)/shard_map/ppermute | solution.py:28
  78.4 25.1 %collective-permute-start.7 = (bf16[256,384]{1,0:T(8,128)(2,1)S(1)}, bf16[256,384]{1,0:T(8,128)(2,1)}, u32[]{:S(2)}, u32[]{:S(2)}) collective-permute-start(bf16[256,384]{1,0:T(8,128)(2,1)S(1)} %bitcast.29), channel_id=1, source_target_pairs={{0,12},{4,0},{8,4},{12,8},{1,13},{5,1},{9,5},{13,9},{2,14},{6,2},{... | collective-permute-start | bytes 589832 | tf_op jit(solution)/shard_map/ppermute | solution.py:28
  89.6 16.9 %all-to-all-start.1 = ((bf16[8,4,768]{2,1,0:T(4,128)(2,1)}), bf16[8,4,768]{2,1,0:T(4,128)(2,1)S(1)}, u32[]{:S(2)}, u32[]{:S(2)}) async-start(bf16[8,4,768]{2,1,0:T(4,128)(2,1)} %reduce_rows.1), calls=%async_computation.1 | async-start | bytes 98304 | tf_op jit(solution)/shard_map/all_to_all | solution.py:19

commit v9 on v8

--- a/solution.py
+++ b/solution.py
@@ -215,6 +215,7 @@
     aways = (0, pairs // 2, pairs - 1, 1)
     pieces = [arrived] + [shift(arrived, "yh", -away) for away in aways[1:]]
     other_chip_rows = lax.ppermute(chip_rows, "core", CORE_SWAP)
+    grad_tokens, other_chip_rows = lax.optimization_barrier((grad_tokens, other_chip_rows))
     weight_grad = weight_gradient(pieces, aways, chip_rows, other_chip_rows)
     return grad_tokens.reshape(token_count, width), weight_grad[None]
 

time: 108 us -> 132 us (1.22)
  waiting for transfers between devices: 18.3 us -> 47.8 us
  starting transfers between devices: 73.2 us -> 68.9 us
    all_to_all x4, waiting for transfers between devices: 7.81 us -> 28.8 us  [exchange(): return lax.all_to_all(blocks, axes, split_axis=0, concat_axis=0, tiled=True)]
    ppermute x3, starting transfers between devices: 14.6 us -> 10.3 us  [shift(): lax.ppermute(value, axis, [(i, (i + by) % size) for i in range(size)])]
    ppermute x1, waiting for transfers between devices: 0.01 us -> 3.22 us  [on_device(): forwarded = lax.ppermute(opposite, 'xl', [(2, 3), (1, 0)])]
    ppermute x3, waiting for transfers between devices: 10.5 us -> 13.4 us  [shift(): lax.ppermute(value, axis, [(i, (i + by) % size) for i in range(size)])]
    ppermute x2, waiting for transfers between devices: 0.01 us -> 2.22 us  [flip(): lax.ppermute(value, axis, [(i, i ^ bits) for i in range(lax.axis_size(axi...]
    ppermute x2, starting transfers between devices: 5.33 us -> 3.84 us  [flip(): lax.ppermute(value, axis, [(i, i ^ bits) for i in range(lax.axis_size(axi...]
    ppermute x1, starting transfers between devices: 4.01 us -> 5.44 us  [on_device(): across = lax.ppermute(grad_up, 'xl', [(0, 2), (3, 1)])]
  transfers between devices with their start and end apart: 13 -> 13, of which waited for: 4 -> 7; matrix products, arithmetic and copies ran while one was open for 4% -> 3% of each run, Pallas kernels for 6% -> 3%
where the time goes in v9:
time: 132 us; the launch traced here: 131 us
  starting transfers between devices  68.9 us (52%)
  waiting for transfers between devices  47.8 us (36%)
  Pallas kernels  6.06 us (5%)
  local copies, waits for them, and re-layouts  5.06 us (4%)
  other arithmetic  1.42 us (1%)
    all_to_all x4, waiting for transfers between devices, exchange(): return lax.all_to_all(blocks, axes, split_axis=0, concat_axis=0, tiled=True)  28.8 us
    all_to_all x4, starting transfers between devices, exchange(): return lax.all_to_all(blocks, axes, split_axis=0, concat_axis=0, tiled=True)  28.7 us
    ppermute x1, starting transfers between devices, on_device(): other_weight = lax.ppermute(weight, 'core', CORE_SWAP)  16.1 us
    ppermute x3, waiting for transfers between devices, shift(): lax.ppermute(value, axis, [(i, (i + by) % size) for i in range(size)])  13.4 us
    ppermute x3, starting transfers between devices, shift(): lax.ppermute(value, axis, [(i, (i + by) % size) for i in range(size)])  10.3 us
    ppermute x1, starting transfers between devices, on_device(): across = lax.ppermute(grad_up, 'xl', [(0, 2), (3, 1)])  5.44 us
    ppermute x2, starting transfers between devices, flip(): lax.ppermute(value, axis, [(i, i ^ bits) for i in range(lax.axis_size(axi...  3.84 us
    unnamed x14, local copies, waits for them, and re-layouts  3.32 us
  transfers between devices with their start and end apart: 13, of which 7 were waited for; matrix products, arithmetic and copies ran while one was open for 3% of the time, Pallas kernels for 3%

profile of v9, /device:TPU:1, one launch (start us, length us, event | category | flops | bytes accessed | tf_op | source)
XLA Modules:
  0.0 131.0 jit_solution(8924415886778878246)
XLA Ops:
  0.6 16.1 %collective-permute-start.4 = (bf16[384,1024]{1,0:T(8,128)(2,1)}, bf16[384,1024]{1,0:T(8,128)(2,1)S(1)}, u32[]{:S(2)}, u32[]{:S(2)}) collective-permute-start(bf16[384,1024]{1,0:T(8,128)(2,1)} %bitcast.35), channel_id=1, source_target_pairs={{0,128},{128,0},{1,129},{129,1},{2,130},{130,2},{3,131},{131,3},{4... | collective-permute-start | bytes 2359304 | tf_op jit(solution)/shard_map/ppermute | solution.py:193
  16.7 1.2 fusion.2
  18.2 1.9 %collective-permute-start.1 = (bf16[128,1024]{1,0:T(8,128)(2,1)S(1)}, bf16[128,1024]{1,0:T(8,128)(2,1)S(1)}, u32[]{:S(2)}, u32[]{:S(2)}) collective-permute-start(bf16[128,1024]{1,0:T(8,128)(2,1)S(1)} %bitcast.31), channel_id=1, source_target_pairs={{0,768},{256,512},{512,256},{768,0},{1,769},{257,513},{513,257},{7... | collective-permute-start | bytes 786440 | tf_op jit(solution)/shard_map/ppermute | solution.py:23
  20.1 1.9 %collective-permute-start = (bf16[128,1024]{1,0:T(8,128)(2,1)S(1)}, bf16[128,1024]{1,0:T(8,128)(2,1)S(1)}, u32[]{:S(2)}, u32[]{:S(2)}) collective-permute-start(bf16[128,1024]{1,0:T(8,128)(2,1)S(1)} %bitcast.32), channel_id=1, source_target_pairs={{0,256},{256,0},{512,768},{768,512},{1,257},{257,1},{513,769},{769... | collective-permute-start | bytes 786440 | tf_op jit(solution)/shard_map/ppermute | solution.py:23
  22.1 5.4 %collective-permute-start.2 = (bf16[128,1024]{1,0:T(8,128)(2,1)S(1)}, bf16[128,1024]{1,0:T(8,128)(2,1)S(1)}, u32[]{:S(2)}, u32[]{:S(2)}) collective-permute-start(bf16[128,1024]{1,0:T(8,128)(2,1)S(1)} %bitcast.33), channel_id=1, source_target_pairs={{0,512},{768,256},{1,513},{769,257},{2,514},{770,258},{3,515},{771... | collective-permute-start | bytes 786440 | tf_op jit(solution)/shard_map/ppermute | solution.py:175
  27.6 2.2 %collective-permute-done.1.refs_2_ = bf16[128,1024]{1,0:T(8,128)(2,1)S(1)} collective-permute-done((bf16[128,1024]{1,0:T(8,128)(2,1)S(1)}, bf16[128,1024]{1,0:T(8,128)(2,1)S(1)}, u32[]{:S(2)}, u32[]{:S(2)}) %collective-permute-start.1) | collective-permute-done | bytes 262176 | tf_op jit(solution)/shard_map/ppermute | solution.py:23
  29.8 1.3 collective-permute-start.3
  32.0 5.1 %all-to-all-start.2 = ((bf16[16,8,384]{2,1,0:T(8,128)(2,1)}), bf16[16,8,384]{2,1,0:T(8,128)(2,1)S(1)}, u32[]{:S(2)}, u32[]{:S(2)}) async-start(bf16[16,8,384]{2,1,0:T(8,128)(2,1)} %bitcast.13), calls=%async_computation.2 | async-start | bytes 196608 | tf_op jit(solution)/shard_map/all_to_all | solution.py:19
  38.0 3.2 %collective-permute-done.3.refs_4_ = bf16[128,1024]{1,0:T(8,128)(2,1)S(1)} collective-permute-done((bf16[128,1024]{1,0:T(8,128)(2,1)S(1)}, bf16[128,1024]{1,0:T(8,128)(2,1)S(1)}, u32[]{:S(2)}, u32[]{:S(2)}) %collective-permute-start.3) | collective-permute-done | bytes 262176 | tf_op jit(solution)/shard_map/ppermute | solution.py:177
  41.9 0.9 copy-done.3
  42.8 0.9 copy-done.5
  43.8 2.8 %row_partials.1 = (bf16[8,4,16,768]{3,2,1,0:T(8,128)(2,1)}, bf16[4,128,1024]{2,1,0:T(8,128)(2,1)S(1)}) custom-call(s32[2]{0:T(128)S(1)} %pad_add_fusion.place, bf16[128,1024]{1,0:T(8,128)(2,1)S(1)} %bitcast.34, bf16[128,1024]{1,0:T(8,128)(2,1)S(1)} %collective-permute-done.refs_1_, bf16[128,1024]{1,0:T(8,128)(2,1)S(1)} %collective-permute-done.1.refs_2_, ...), custom_call_target="tpu_custom_call" | custom-call | flops 1610612736 | bytes 6291456 | tf_op jit(solution)/shard_map/row_partials/pallas_call | solution.py:74
  46.6 4.6 %all-to-all-start = ((bf16[64,8,768]{2,1,0:T(8,128)(2,1)}), bf16[64,8,768]{2,1,0:T(8,128)(2,1)S(1)}, u32[]{:S(2)}, u32[]{:S(2)}) async-start(bf16[64,8,768]{2,1,0:T(8,128)(2,1)} %bitcast.7), calls=%async_computation | async-start | bytes 1572864 | tf_op jit(solution)/shard_map/all_to_all | solution.py:19
  51.2 3.3 %collective-permute-start.5 = (bf16[4,128,1024]{2,1,0:T(8,128)(2,1)S(1)}, bf16[4,128,1024]{2,1,0:T(8,128)(2,1)S(1)}, u32[]{:S(2)}, u32[]{:S(2)}) collective-permute-start(bf16[4,128,1024]{2,1,0:T(8,128)(2,1)S(1)} %get-tuple-element.7.refs_4_), channel_id=1, source_target_pairs={{0,128},{128,0},{1,129},{129,1},{2,130},{130,2},{3,131},{131,3},{4... | collective-permute-start | bytes 3145736 | tf_op jit(solution)/shard_map/ppermute | solution.py:217
  54.5 21.1 %all-to-all-done = bf16[64,8,768]{2,1,0:T(8,128)(2,1)S(1)} async-done(((bf16[64,8,768]{2,1,0:T(8,128)(2,1)}), bf16[64,8,768]{2,1,0:T(8,128)(2,1)S(1)}, u32[]{:S(2)}, u32[]{:S(2)}) %all-to-all-start) | async-done | bytes 786464 | tf_op jit(solution)/shard_map/all_to_all | solution.py:19
  76.3 15.5 %all-to-all-start.3 = ((bf16[16,16,384]{2,1,0:T(8,128)(2,1)}), bf16[16,16,384]{2,1,0:T(8,128)(2,1)S(1)}, u32[]{:S(2)}, u32[]{:S(2)}) async-start(bf16[16,16,384]{2,1,0:T(8,128)(2,1)} %bitcast.15), calls=%async_computation.3 | async-start | bytes 393216 | tf_op jit(solution)/shard_map/all_to_all | solution.py:19
  92.7 7.6 %all-to-all-done.3 = bf16[16,16,384]{2,1,0:T(8,128)(2,1)S(1)} async-done(((bf16[16,16,384]{2,1,0:T(8,128)(2,1)}), bf16[16,16,384]{2,1,0:T(8,128)(2,1)S(1)}, u32[]{:S(2)}, u32[]{:S(2)}) %all-to-all-start.3) | async-done | bytes 196640 | tf_op jit(solution)/shard_map/all_to_all | solution.py:19
  100.3 3.3 %all-to-all-start.1 = ((bf16[8,4,768]{2,1,0:T(4,128)(2,1)}), bf16[8,4,768]{2,1,0:T(4,128)(2,1)S(1)}, u32[]{:S(2)}, u32[]{:S(2)}) async-start(bf16[8,4,768]{2,1,0:T(4,128)(2,1)} %reduce_rows.1), calls=%async_computation.1 | async-start | bytes 98304 | tf_op jit(solution)/shard_map/all_to_all | solution.py:19
  103.9 2.9 %collective-permute-start.6 = (bf16[256,384]{1,0:T(8,128)(2,1)S(1)}, bf16[256,384]{1,0:T(8,128)(2,1)S(1)}, u32[]{:S(2)}, u32[]{:S(2)}) collective-permute-start(bf16[256,384]{1,0:T(8,128)(2,1)S(1)} %bitcast.27), channel_id=1, source_target_pairs={{0,8},{4,12},{8,0},{12,4},{1,9},{5,13},{9,1},{13,5},{2,10},{6,14},... | collective-permute-start | bytes 589832 | tf_op jit(solution)/shard_map/ppermute | solution.py:28
  106.8 4.0 %collective-permute-start.7 = (bf16[256,384]{1,0:T(8,128)(2,1)S(1)}, bf16[256,384]{1,0:T(8,128)(2,1)S(1)}, u32[]{:S(2)}, u32[]{:S(2)}) collective-permute-start(bf16[256,384]{1,0:T(8,128)(2,1)S(1)} %bitcast.28), channel_id=1, source_target_pairs={{0,4},{4,8},{8,12},{12,0},{1,5},{5,9},{9,13},{13,1},{2,6},{6,10},{... | collective-permute-start | bytes 589832 | tf_op jit(solution)/shard_map/ppermute | solution.py:28
  110.9 3.4 %collective-permute-start.8 = (bf16[256,384]{1,0:T(8,128)(2,1)S(1)}, bf16[256,384]{1,0:T(8,128)(2,1)S(1)}, u32[]{:S(2)}, u32[]{:S(2)}) collective-permute-start(bf16[256,384]{1,0:T(8,128)(2,1)S(1)} %bitcast.29), channel_id=1, source_target_pairs={{0,12},{4,0},{8,4},{12,8},{1,13},{5,1},{9,5},{13,9},{2,14},{6,2},{... | collective-permute-start | bytes 589832 | tf_op jit(solution)/shard_map/ppermute | solution.py:28
  115.0 5.3 %collective-permute-done.7.refs_2_ = bf16[256,384]{1,0:T(8,128)(2,1)S(1)} collective-permute-done((bf16[256,384]{1,0:T(8,128)(2,1)S(1)}, bf16[256,384]{1,0:T(8,128)(2,1)S(1)}, u32[]{:S(2)}, u32[]{:S(2)}) %collective-permute-start.7) | collective-permute-done | bytes 196640 | tf_op jit(solution)/shard_map/ppermute | solution.py:28
  120.3 8.2 %collective-permute-done.8.refs_3_ = bf16[256,384]{1,0:T(8,128)(2,1)S(1)} collective-permute-done((bf16[256,384]{1,0:T(8,128)(2,1)S(1)}, bf16[256,384]{1,0:T(8,128)(2,1)S(1)}, u32[]{:S(2)}, u32[]{:S(2)}) %collective-permute-start.8) | collective-permute-done | bytes 196640 | tf_op jit(solution)/shard_map/ppermute | solution.py:28
  128.5 2.5 %weight_gradient.1 = bf16[384,1024]{1,0:T(8,128)(2,1)} custom-call(s32[2]{0:T(128)S(1)} %pad_add_fusion.1.place, bf16[256,384]{1,0:T(8,128)(2,1)S(1)} %bitcast.30, bf16[256,384]{1,0:T(8,128)(2,1)S(1)} %collective-permute-done.6.refs_1_, bf16[256,384]{1,0:T(8,128)(2,1)S(1)} %collective-permute-done.7.refs_2_, ...), custom_call_target="tpu_custom_call" | custom-call | flops 805306368 | bytes 6291456 | tf_op jit(solution)/shard_map/weight_gradient/pallas_call | solution.py:147
  (32 shorter events, 5.2 us)
Async XLA Ops:
  0.6 30.5 %copy-start = (bf16[4,3072]{1,0:T(4,128)(2,1)S(1)}, bf16[4,3072]{1,0:T(4,128)(2,1)}, u32[]{:S(2)}) copy-start(bf16[4,3072]{1,0:T(4,128)(2,1)} %param.5) | copy-start | bytes 73732
  0.6 41.2 %collective-permute-start.4 = (bf16[384,1024]{1,0:T(8,128)(2,1)}, bf16[384,1024]{1,0:T(8,128)(2,1)S(1)}, u32[]{:S(2)}, u32[]{:S(2)}) collective-permute-start(bf16[384,1024]{1,0:T(8,128)(2,1)} %bitcast.35), channel_id=1, source_target_pairs={{0,128},{128,0},{1,129},{129,1},{2,130},{130,2},{3,131},{131,3},{4... | collective-permute-start | bytes 2359304 | tf_op jit(solution)/shard_map/ppermute | solution.py:193
  17.9 24.0 %copy-start.1 = (bf16[1,384,1024]{2,1,0:T(8,128)(2,1)S(1)}, bf16[1,384,1024]{2,1,0:T(8,128)(2,1)}, u32[]{:S(2)}) copy-start(bf16[1,384,1024]{2,1,0:T(8,128)(2,1)} %param.7) | copy-start | bytes 2359300
  18.2 9.3 %copy-start.6 = (s32[4,2]{0,1:T(2,128)S(1)}, s32[4,2]{0,1:T(2,128)}, u32[]{:S(2)}) copy-start(s32[4,2]{0,1:T(2,128)} %param.6) | copy-start | bytes 100
  18.2 11.6 %collective-permute-start.1 = (bf16[128,1024]{1,0:T(8,128)(2,1)S(1)}, bf16[128,1024]{1,0:T(8,128)(2,1)S(1)}, u32[]{:S(2)}, u32[]{:S(2)}) collective-permute-start(bf16[128,1024]{1,0:T(8,128)(2,1)S(1)} %bitcast.31), channel_id=1, source_target_pairs={{0,768},{256,512},{512,256},{768,0},{1,769},{257,513},{513,257},{7... | collective-permute-start | bytes 786440 | tf_op jit(solution)/shard_map/ppermute | solution.py:23
  20.1 17.0 %collective-permute-start = (bf16[128,1024]{1,0:T(8,128)(2,1)S(1)}, bf16[128,1024]{1,0:T(8,128)(2,1)S(1)}, u32[]{:S(2)}, u32[]{:S(2)}) collective-permute-start(bf16[128,1024]{1,0:T(8,128)(2,1)S(1)} %bitcast.32), channel_id=1, source_target_pairs={{0,256},{256,0},{512,768},{768,512},{1,257},{257,1},{513,769},{769... | collective-permute-start | bytes 786440 | tf_op jit(solution)/shard_map/ppermute | solution.py:23
  22.1 15.2 %collective-permute-start.2 = (bf16[128,1024]{1,0:T(8,128)(2,1)S(1)}, bf16[128,1024]{1,0:T(8,128)(2,1)S(1)}, u32[]{:S(2)}, u32[]{:S(2)}) collective-permute-start(bf16[128,1024]{1,0:T(8,128)(2,1)S(1)} %bitcast.33), channel_id=1, source_target_pairs={{0,512},{768,256},{1,513},{769,257},{2,514},{770,258},{3,515},{771... | collective-permute-start | bytes 786440 | tf_op jit(solution)/shard_map/ppermute | solution.py:175
  29.8 11.4 %collective-permute-start.3 = (bf16[128,1024]{1,0:T(8,128)(2,1)S(1)}, bf16[128,1024]{1,0:T(8,128)(2,1)S(1)}, u32[]{:S(2)}, u32[]{:S(2)}) collective-permute-start(bf16[128,1024]{1,0:T(8,128)(2,1)S(1)} %collective-permute-done.1.refs_2_), channel_id=1, source_target_pairs={{512,768},{256,0},{513,769},{257,1},{514,770},{258,2},{515,771},{2... | collective-permute-start | bytes 786440 | tf_op jit(solution)/shard_map/ppermute | solution.py:177
  32.0 14.6 %all-to-all-start.2 = ((bf16[16,8,384]{2,1,0:T(8,128)(2,1)}), bf16[16,8,384]{2,1,0:T(8,128)(2,1)S(1)}, u32[]{:S(2)}, u32[]{:S(2)}) async-start(bf16[16,8,384]{2,1,0:T(8,128)(2,1)} %bitcast.13), calls=%async_computation.2 | async-start | bytes 196608 | tf_op jit(solution)/shard_map/all_to_all | solution.py:19
  37.3 0.7 copy-start.2
  41.2 0.7 copy-start.4
  41.9 1.0 copy-start.3
  42.8 0.9 copy-start.5
  46.6 29.1 %all-to-all-start = ((bf16[64,8,768]{2,1,0:T(8,128)(2,1)}), bf16[64,8,768]{2,1,0:T(8,128)(2,1)S(1)}, u32[]{:S(2)}, u32[]{:S(2)}) async-start(bf16[64,8,768]{2,1,0:T(8,128)(2,1)} %bitcast.7), calls=%async_computation | async-start | bytes 1572864 | tf_op jit(solution)/shard_map/all_to_all | solution.py:19
  51.2 63.8 %collective-permute-start.5 = (bf16[4,128,1024]{2,1,0:T(8,128)(2,1)S(1)}, bf16[4,128,1024]{2,1,0:T(8,128)(2,1)S(1)}, u32[]{:S(2)}, u32[]{:S(2)}) collective-permute-start(bf16[4,128,1024]{2,1,0:T(8,128)(2,1)S(1)} %get-tuple-element.7.refs_4_), channel_id=1, source_target_pairs={{0,128},{128,0},{1,129},{129,1},{2,130},{130,2},{3,131},{131,3},{4... | collective-permute-start | bytes 3145736 | tf_op jit(solution)/shard_map/ppermute | solution.py:217
  76.3 24.0 %all-to-all-start.3 = ((bf16[16,16,384]{2,1,0:T(8,128)(2,1)}), bf16[16,16,384]{2,1,0:T(8,128)(2,1)S(1)}, u32[]{:S(2)}, u32[]{:S(2)}) async-start(bf16[16,16,384]{2,1,0:T(8,128)(2,1)} %bitcast.15), calls=%async_computation.3 | async-start | bytes 393216 | tf_op jit(solution)/shard_map/all_to_all | solution.py:19
  100.3 13.9 %all-to-all-start.1 = ((bf16[8,4,768]{2,1,0:T(4,128)(2,1)}), bf16[8,4,768]{2,1,0:T(4,128)(2,1)S(1)}, u32[]{:S(2)}, u32[]{:S(2)}) async-start(bf16[8,4,768]{2,1,0:T(4,128)(2,1)} %reduce_rows.1), calls=%async_computation.1 | async-start | bytes 98304 | tf_op jit(solution)/shard_map/all_to_all | solution.py:19
  103.9 11.1 %collective-permute-start.6 = (bf16[256,384]{1,0:T(8,128)(2,1)S(1)}, bf16[256,384]{1,0:T(8,128)(2,1)S(1)}, u32[]{:S(2)}, u32[]{:S(2)}) collective-permute-start(bf16[256,384]{1,0:T(8,128)(2,1)S(1)} %bitcast.27), channel_id=1, source_target_pairs={{0,8},{4,12},{8,0},{12,4},{1,9},{5,13},{9,1},{13,5},{2,10},{6,14},... | collective-permute-start | bytes 589832 | tf_op jit(solution)/shard_map/ppermute | solution.py:28
  106.8 13.5 %collective-permute-start.7 = (bf16[256,384]{1,0:T(8,128)(2,1)S(1)}, bf16[256,384]{1,0:T(8,128)(2,1)S(1)}, u32[]{:S(2)}, u32[]{:S(2)}) collective-permute-start(bf16[256,384]{1,0:T(8,128)(2,1)S(1)} %bitcast.28), channel_id=1, source_target_pairs={{0,4},{4,8},{8,12},{12,0},{1,5},{5,9},{9,13},{13,1},{2,6},{6,10},{... | collective-permute-start | bytes 589832 | tf_op jit(solution)/shard_map/ppermute | solution.py:28
  110.9 17.6 %collective-permute-start.8 = (bf16[256,384]{1,0:T(8,128)(2,1)S(1)}, bf16[256,384]{1,0:T(8,128)(2,1)S(1)}, u32[]{:S(2)}, u32[]{:S(2)}) collective-permute-start(bf16[256,384]{1,0:T(8,128)(2,1)S(1)} %bitcast.29), channel_id=1, source_target_pairs={{0,12},{4,0},{8,4},{12,8},{1,13},{5,1},{9,5},{13,9},{2,14},{6,2},{... | collective-permute-start | bytes 589832 | tf_op jit(solution)/shard_map/ppermute | solution.py:28
